TPU v7x, 32 devices: a whole 2x2x4 slice. The times are simulated.
32 devices in a mesh: dp: 2 (over core), mp: 16 (over z, y, x).
Axes of the slice: x: 2, y: 2, z: 4, core: 2. Of those that a mesh axis runs over, the one named last changes fastest.
Arguments:
- inputs: bfloat16 [2, 8192, 8192], P('dp', 'mp'), may hold values from -6 to 6
- cotangent: bfloat16 [2, 8192, 8192], P('dp', 'mp'), may hold values from -6 to 6
- mixer_right: bfloat16 [64, 128, 128], replicated, may hold values from -0.5 to 0.5
- mixer_left: bfloat16 [64, 128, 128], replicated, may hold values from -0.5 to 0.5
- dense_right: bfloat16 [64, 128, 128], P('mp'), may hold values from -0.5 to 0.5
- dense_left: bfloat16 [64, 128, 128], P('mp'), may hold values from -0.5 to 0.5
Outputs:
- block_out: bfloat16 [2, 8192, 8192], P('dp', 'mp')
- grad_inputs: bfloat16 [2, 8192, 8192], P('dp', 'mp')
- grad_mixer_right: float32 [64, 128, 128], P('mp', 'dp')
- grad_mixer_left: float32 [64, 128, 128], P('mp', 'dp')
- grad_dense_right: float32 [64, 128, 128], P('mp', 'dp')
- grad_dense_left: float32 [64, 128, 128], P('mp', 'dp')
All inputs are finite; a program needn't handle non-finite values.
Results may differ from a plain program's by a relative error of at most 0.015.
Values may be sent and summed in bfloat16 or wider, within the bound.
No kernel may reach another device: no remote copies, remote signals or barrier semaphores. Data moves between devices by JAX's collectives and lax.ppermute only.
A program may use at most 256 MiB of HBM per device.

v0:
```python
import jax
import jax.numpy as jnp
from jax import lax
from jax.sharding import PartitionSpec as P

NB = 64
BS = 128
LB = 64
LS = 128


def mix_positions(values, weight, blocks):
    batch, chans, length = values.shape
    size = length // blocks
    fold = size // blocks
    shaped = values.reshape(batch, chans, blocks, size)
    table = weight.reshape(blocks, size, blocks, fold)
    mixed = jnp.einsum("scbi,bief->scebf", shaped, table, preferred_element_type=jnp.float32)
    return mixed.reshape(batch, chans, length)


def back_positions(grads, weight, blocks):
    batch, chans, length = grads.shape
    size = length // blocks
    fold = size // blocks
    shaped = grads.reshape(batch, chans, blocks, blocks, fold)
    table = weight.reshape(blocks, size, blocks, fold)
    result = jnp.einsum("ekbf,scbef->scek", table, shaped, preferred_element_type=jnp.float32)
    return result.reshape(batch, chans, length)


def grad_positions(values, grads, blocks):
    batch, chans, length = values.shape
    size = length // blocks
    fold = size // blocks
    left_side = values.reshape(batch, chans, blocks, size)
    right_side = grads.reshape(batch, chans, blocks, blocks, fold)
    result = jnp.einsum(
        "scek,scbef->ekbf", left_side, right_side, preferred_element_type=jnp.float32
    )
    return result.reshape(blocks, size, size)


def on_device(inputs, cotangent, mixer_right, mixer_left, dense_right, dense_left):
    batch, chans, length = inputs.shape
    local_blocks = dense_right.shape[0]
    fold = BS // NB
    values = inputs.astype(jnp.float32)
    first_mix = mix_positions(inputs, mixer_right, LB).astype(jnp.bfloat16)
    time_mixed = mix_positions(first_mix, mixer_left, LB).astype(jnp.bfloat16)
    sigma_in = jax.nn.sigmoid(values)
    silu_in = values * sigma_in
    slope_in = sigma_in * (1.0 + values * (1.0 - sigma_in))
    hidden = (values + silu_in * time_mixed.astype(jnp.float32)).astype(jnp.bfloat16)
    above = cotangent.astype(jnp.float32)
    hidden_f = hidden.astype(jnp.float32)
    hidden_blocks = hidden.reshape(batch, local_blocks, BS, length)
    right_table = dense_right.reshape(local_blocks, BS, NB, fold)
    left_table = dense_left.reshape(local_blocks, BS, NB, fold)
    pieces = jnp.einsum(
        "sail,aief->seafl", hidden_blocks, right_table, preferred_element_type=jnp.float32
    ).astype(jnp.bfloat16)
    panel = lax.all_to_all(pieces, "mp", split_axis=1, concat_axis=2, tiled=True).reshape(
        batch, local_blocks, BS, length
    )
    pre_gate = jnp.einsum(
        "sekl,ekaf->saefl", panel, left_table, preferred_element_type=jnp.float32
    ).astype(jnp.bfloat16)
    gate = lax.all_to_all(pre_gate, "mp", split_axis=1, concat_axis=2, tiled=True).reshape(
        batch, chans, length
    )
    gate_f = gate.astype(jnp.float32)
    sigma_gate = jax.nn.sigmoid(gate_f)
    silu_gate = gate_f * sigma_gate
    slope_gate = sigma_gate * (1.0 + gate_f * (1.0 - sigma_gate))
    block_out = (hidden_f * (1.0 + silu_gate)).astype(jnp.bfloat16)
    grad_gate = (above * hidden_f * slope_gate).astype(jnp.bfloat16)
    gate_perm = lax.all_to_all(
        grad_gate.reshape(batch, local_blocks, NB, fold, length),
        "mp",
        split_axis=2,
        concat_axis=1,
        tiled=True,
    )
    grad_panel = jnp.einsum(
        "ekaf,saefl->sekl", left_table, gate_perm, preferred_element_type=jnp.float32
    ).astype(jnp.bfloat16)
    term_dense_left = jnp.einsum(
        "sekl,saefl->ekaf", panel, gate_perm, preferred_element_type=jnp.float32
    ).reshape(local_blocks, BS, BS)
    panel_back = lax.all_to_all(
        grad_panel.reshape(batch, local_blocks, NB, fold, length),
        "mp",
        split_axis=2,
        concat_axis=1,
        tiled=True,
    )
    hidden_term = jnp.einsum(
        "aief,seafl->sail", right_table, panel_back, preferred_element_type=jnp.float32
    ).reshape(batch, chans, length)
    term_dense_right = jnp.einsum(
        "sail,seafl->aief", hidden_blocks, panel_back, preferred_element_type=jnp.float32
    ).reshape(local_blocks, BS, BS)
    grad_hidden = (above * (1.0 + silu_gate) + hidden_term).astype(jnp.bfloat16)
    grad_hidden_f = grad_hidden.astype(jnp.float32)
    grad_time = (grad_hidden_f * silu_in).astype(jnp.bfloat16)
    grad_first_mix = back_positions(grad_time, mixer_left, LB).astype(jnp.bfloat16)
    term_mixer_left = grad_positions(first_mix, grad_time, LB)
    input_term = back_positions(grad_first_mix, mixer_right, LB)
    grad_inputs = (
        grad_hidden_f * (1.0 + slope_in * time_mixed.astype(jnp.float32)) + input_term
    ).astype(jnp.bfloat16)
    term_mixer_right = grad_positions(inputs, grad_first_mix, LB)
    total_right, total_left = lax.psum((term_mixer_right, term_mixer_left), ("dp", "mp"))
    share = LB // lax.axis_size("mp")
    rows = LS // lax.axis_size("dp")
    anchor = (lax.axis_index("mp") * share, lax.axis_index("dp") * rows, jnp.zeros((), jnp.int32))
    mixer_rsum = lax.dynamic_slice(total_right, anchor, (share, rows, LS))
    mixer_lsum = lax.dynamic_slice(total_left, anchor, (share, rows, LS))
    dense_rsum, dense_lsum = (
        lax.psum_scatter(term_dense_right, "dp", scatter_dimension=1, tiled=True),
        lax.psum_scatter(term_dense_left, "dp", scatter_dimension=1, tiled=True),
    )
    sequences = batch * lax.axis_size("dp")
    dense_scale = float(sequences * length) ** (-0.5)
    mixer_scale = float(sequences * chans * lax.axis_size("mp")) ** (-0.5)
    return (
        block_out,
        grad_inputs,
        mixer_rsum * mixer_scale,
        mixer_lsum * mixer_scale,
        dense_rsum * dense_scale,
        dense_lsum * dense_scale,
    )


def solution(mesh):
    return jax.shard_map(
        on_device,
        mesh=mesh,
        in_specs=(
            P("dp", "mp", None),
            P("dp", "mp", None),
            P(),
            P(),
            P("mp", None, None),
            P("mp", None, None),
        ),
        out_specs=(
            P("dp", "mp", None),
            P("dp", "mp", None),
            P("mp", "dp", None),
            P("mp", "dp", None),
            P("mp", "dp", None),
            P("mp", "dp", None),
        ),
        check_vma=False,
    )
```

profile of v0, /device:TPU:4, one launch (start us, length us, event | category | flops | bytes accessed | tf_op | source)
XLA Modules:
  0.0 1485.6 jit_solution(9132821624796796895)
XLA Ops:
  25.9 27.0 %fusion.29 = bf16[64,64,2,512]{3,1,2,0:T(8,128)(2,1)} fusion(bf16[512,64,128,1]{2,1,0,3:T(8,128)(2,1)} %bitcast.128, bf16[64,128,64,2]{1,0,3,2:T(8,128)(2,1)} %bitcast.142), kind=kOutput, calls=%fused_computation.47 | convolution fusion | flops 1077936128 | bytes 18874368 | tf_op jit(solution)/shard_map/scbi,bief->scebf/dot_general | solution.py:18
  66.1 13.5 convert_bitcast_fusion
  79.6 20.1 %copy.181 = f32[1,512,64,64,2]{1,0,4,3,2:T(1,128)} copy(f32[1,512,64,64,2]{1,2,4,3,0:T(8,128)} %convert_bitcast_fusion) | data formatting | bytes 33554432 | tf_op jit(solution)/shard_map/convert_element_type | solution.py:54
  99.7 34.8 %copy.182 = f32[1,512,8192]{2,1,0:T(8,128)} copy(f32[1,512,8192]{1,0,2:T(1,128)} %bitcast.132) | data formatting | bytes 33554432 | tf_op jit(solution)/shard_map/convert_element_type | solution.py:54
  156.6 16.4 %copy.185 = bf16[1,64,4,2,8192]{4,3,2,0,1:T(2,128)(2,1)} copy(bf16[1,64,4,2,8192]{4,1,3,2,0:T(8,128)(2,1)} %fusion.16) | data formatting | bytes 16777216 | tf_op jit(solution)/shard_map/convert_element_type | solution.py:62
  181.2 168.0 %all-to-all-done = bf16[1,64,4,2,8192]{4,3,2,0,1:T(2,128)(2,1)} async-done(((bf16[1,64,4,2,8192]{4,3,2,0,1:T(2,128)(2,1)}), bf16[1,64,4,2,8192]{4,3,2,0,1:T(2,128)(2,1)}, u32[]{:S(2)}, u32[]{:S(2)}) %all-to-all-start) | async-done | bytes 8388640 | tf_op jit(solution)/shard_map/all_to_all | solution.py:63
  379.9 15.6 %copy.189 = bf16[1,64,4,2,8192]{4,3,2,0,1:T(2,128)(2,1)S(1)} copy(bf16[1,64,4,2,8192]{4,1,3,2,0:T(8,128)(2,1)} %fusion.17) | data formatting | bytes 16777216 | tf_op jit(solution)/shard_map/convert_element_type | solution.py:68
  395.5 209.4 %all_to_all.54 = bf16[1,64,4,2,8192]{4,3,2,0,1:T(2,128)(2,1)} all-to-all(bf16[1,64,4,2,8192]{4,3,2,0,1:T(2,128)(2,1)S(1)} %copy.189), channel_id=1, replica_groups=mesh['dp'=2,'mp'=16] {'mp'}, dimensions={1} | all-to-all | bytes 16777216 | tf_op jit(solution)/shard_map/all_to_all | solution.py:69
  604.9 19.1 %copy.190 = f32[1,16,4,4,2,8192]{5,0,4,3,1,2:T(1,128)S(1)} copy(bf16[1,16,4,4,2,8192]{5,4,3,2,1,0:T(2,128)(2,1)} %bitcast.135) | data formatting | bytes 25165824 | tf_op jit(solution)/shard_map/convert_element_type | solution.py:72
  624.1 25.0 %fusion.4 = (bf16[1,512,8192]{2,1,0:T(8,128)(2,1)}, bf16[1,512,8192]{2,1,0:T(8,128)(2,1)}) fusion(bf16[1,512,8192]{2,1,0:T(8,128)(2,1)S(1)} %bitcast.126, bf16[1,512,8192]{2,1,0:T(8,128)(2,1)} %param.7, f32[1,512,8192]{2,0,1:T(1,128)S(1)} %bitcast.121), kind=kLoop, calls=%fused_computation.13 | loop fusion | flops 67108864 | bytes 50331648 | tf_op jit(solution)/shard_map/convert_element_type | solution.py:77
  649.1 14.2 reshape.222
  670.9 186.7 %all_to_all.55 = bf16[1,4,64,2,8192]{4,3,1,0,2:T(2,128)(2,1)S(1)} all-to-all(bf16[1,4,64,2,8192]{4,3,1,0,2:T(2,128)(2,1)S(1)} %copy.194), channel_id=1, replica_groups=mesh['dp'=2,'mp'=16] {'mp'}, dimensions={2} | all-to-all | bytes 16777216 | tf_op jit(solution)/shard_map/all_to_all | solution.py:78
  865.6 13.4 copy.196
  900.6 14.2 reshape.224
  939.4 152.9 %all-to-all-done.3 = bf16[1,4,64,2,8192]{4,3,1,0,2:T(2,128)(2,1)} async-done(((bf16[1,4,64,2,8192]{4,3,1,0,2:T(2,128)(2,1)}), bf16[1,4,64,2,8192]{4,3,1,0,2:T(2,128)(2,1)}, u32[]{:S(2)}, u32[]{:S(2)}) %all-to-all-start.3) | async-done | bytes 8388640 | tf_op jit(solution)/shard_map/all_to_all | solution.py:91
  1136.7 27.9 %fusion.7 = (bf16[1,512,8192]{2,1,0:T(8,128)(2,1)}, bf16[1,512,8192]{2,1,0:T(8,128)(2,1)}) fusion(bf16[1,512,8192]{2,1,0:T(8,128)(2,1)} %param.6, f32[1,512,8192]{2,1,0:T(8,128)} %bitcast.134, f32[1,512,8192]{2,0,1:T(1,128)} %bitcast.122, bf16[1,512,8192]{2,1,0:T(8,128)(2,1)} %param.7), kind=kLoop, calls=%fused_computation.16 | loop fusion | flops 71303168 | bytes 67108864 | tf_op jit(solution)/shard_map/convert_element_type | solution.py:106
  1176.6 13.3 reshape.227
  1189.9 19.1 %fusion.32 = bf16[1,512,64,128]{1,3,2,0:T(8,128)(2,1)} fusion(bf16[512,64,64,2]{0,3,2,1:T(2,128)(2,1)} %reshape.227, bf16[64,128,64,2]{1,0,3,2:T(8,128)(2,1)S(1)} %bitcast.141), kind=kOutput, calls=%fused_computation.48 | convolution fusion | flops 1077936128 | bytes 18874368 | tf_op jit(solution)/shard_map/ekbf,scbef->scek/dot_general | solution.py:28
  1220.3 23.3 %fusion.35 = f32[64,128,64,2]{1,2,3,0:T(8,128)S(1)} fusion(bf16[512,64,64,2]{0,1,3,2:T(8,128)(2,1)} %bitcast.130, bf16[512,64,128,1]{2,1,0,3:T(8,128)(2,1)} %bitcast.129), kind=kOutput, calls=%fused_computation.49 | convolution fusion | flops 1073741824 | bytes 20971520 | tf_op jit(solution)/shard_map/scek,scbef->ekbf/dot_general | solution.py:38
  1248.3 17.4 %fusion.26 = f32[64,128,64,2]{1,2,3,0:T(8,128)} fusion(bf16[512,64,128,1]{2,0,3,1:T(8,128)(2,1)} %copy.225, bf16[512,64,64,2]{0,3,2,1:T(2,128)(2,1)} %reshape.227), kind=kOutput, calls=%fused_computation.44 | convolution fusion | flops 1073741824 | bytes 20971520 | tf_op jit(solution)/shard_map/scek,scbef->ekbf/dot_general | solution.py:38
  1272.7 14.4 fusion.40
  1287.1 17.6 %copy.238 = f32[1,512,8192]{2,1,0:T(8,128)} copy(f32[1,512,8192]{1,2,0:T(8,128)} %bitcast.133) | data formatting | bytes 33554432 | tf_op jit(solution)/shard_map/reshape | solution.py:29
  1304.7 22.1 %fusion.6 = bf16[1,512,8192]{2,1,0:T(8,128)(2,1)} fusion(f32[1,512,8192]{2,1,0:T(8,128)} %copy.238, bf16[1,512,8192]{2,1,0:T(8,128)(2,1)} %get-tuple-element.35, f32[1,512,8192]{2,1,0:T(8,128)} %copy.182, bf16[1,512,8192]{2,1,0:T(8,128)(2,1)} %param.6), kind=kLoop, calls=%fused_computation.15 | loop fusion | flops 58720256 | bytes 58720256 | tf_op jit(solution)/shard_map/convert_element_type | solution.py:112
  1329.7 145.7 %all-reduce.7.cloned.1.call-done = (f32[64,128,128]{1,0,2:T(8,128)}, f32[64,128,128]{1,0,2:T(8,128)}) async-done(((f32[64,128,128]{1,0,2:T(8,128)}, f32[64,128,128]{1,0,2:T(8,128)}), (f32[64,128,128]{1,0,2:T(8,128)}, f32[64,128,128]{1,0,2:T(8,128)})) %all-reduce.7.cloned.1.call-update) | async-done | bytes 8388624 | tf_op jit(solution)/shard_map/psum | solution.py:114
  (64 shorter events, 239.5 us)
Async XLA Ops:
  15.7 50.4 %copy-start.1 = (bf16[64,128,128]{1,0,2:T(8,128)(2,1)}, bf16[64,128,128]{1,0,2:T(8,128)(2,1)S(1)}, u32[]{:S(2)}) copy-start(bf16[64,128,128]{1,0,2:T(8,128)(2,1)S(1)} %copy.178) | copy-start | bytes 6291460
  173.0 8.0 copy-start.4
  173.0 176.1 %all-to-all-start = ((bf16[1,64,4,2,8192]{4,3,2,0,1:T(2,128)(2,1)}), bf16[1,64,4,2,8192]{4,3,2,0,1:T(2,128)(2,1)}, u32[]{:S(2)}, u32[]{:S(2)}) async-start(bf16[1,64,4,2,8192]{4,3,2,0,1:T(2,128)(2,1)} %copy.185), calls=%async_computation | async-start | bytes 16777216 | tf_op jit(solution)/shard_map/all_to_all | solution.py:63
  395.5 228.6 %slice-start = ((s8[8388608]{0:T(1024)(128)(4,1)}), s8[4194304]{0:T(1024)(128)(4,1)S(1)}, s32[]{:S(2)}) async-start(s8[8388608]{0:T(1024)(128)(4,1)} %bitcast.125), calls=%async_computation.6 | async-start | bytes 8388608
  604.9 19.1 %slice-start.1 = ((s8[8388608]{0:T(1024)(128)(4,1)}), s8[4194304]{0:T(1024)(128)(4,1)S(1)}, s32[]{:S(2)}) async-start(s8[8388608]{0:T(1024)(128)(4,1)} %bitcast.125), calls=%async_computation.7 | async-start | bytes 8388608
  624.0 25.1 %copy-start = (f32[1,16,4,4,2,8192]{5,0,4,3,1,2:T(1,128)}, f32[1,16,4,4,2,8192]{5,0,4,3,1,2:T(1,128)S(1)}, u32[]{:S(2)}) copy-start(f32[1,16,4,4,2,8192]{5,0,4,3,1,2:T(1,128)S(1)} %copy.190) | copy-start | bytes 50331652
  923.2 5.8 copy-start.5
  923.2 169.0 %all-to-all-start.3 = ((bf16[1,4,64,2,8192]{4,3,1,0,2:T(2,128)(2,1)}), bf16[1,4,64,2,8192]{4,3,1,0,2:T(2,128)(2,1)}, u32[]{:S(2)}, u32[]{:S(2)}) async-start(bf16[1,4,64,2,8192]{4,3,1,0,2:T(2,128)(2,1)} %copy.198), calls=%async_computation.3 | async-start | bytes 16777216 | tf_op jit(solution)/shard_map/all_to_all | solution.py:91
  929.0 397.8 %all-reduce.9.cloned.1.call-start = ((), (), s32[]{:S(2)}) async-start(), calls=%async_computation.5 | async-start | bytes 1048576
  1176.6 13.3 copy-start.2
  1248.2 227.2 %all-reduce.7.cloned.1.call-start = ((), (), s32[]{:S(2)}) async-start(), calls=%async_computation.4 | async-start | bytes 16777216 | tf_op jit(solution)/shard_map/psum | solution.py:114
  1265.7 7.0 copy-start.3
Sparse Core Ops, SparseCore 0:
  1248.3 40.1 all-reduce.8
  1295.5 179.9 all-reduce.6
where the time goes:
time: 1500 us; the launch traced here: 1490 us
  waiting for transfers between devices  467 us (31%)
  blocking collectives  396 us (26%)
  local copies, waits for them, and re-layouts  335 us (22%)
  matrix products  170 us (11%)
  other arithmetic  89.6 us (6%)
  between operations  15.2 us (1%)
    all_to_all x1, blocking collectives, on_device(): lax.all_to_all(pre_gate, 'mp', split_axis=1, concat_axis=2, tiled=True)  209 us
    all_to_all x1, blocking collectives, on_device(): lax.all_to_all(grad_gate.reshape(batch, local_blocks, NB, fold, length),...  187 us
    all_to_all x1, waiting for transfers between devices, on_device(): lax.all_to_all(pieces, 'mp', split_axis=1, concat_axis=2, tiled=True)  168 us
    all_to_all x1, waiting for transfers between devices, on_device(): lax.all_to_all(grad_panel.reshape(batch, local_blocks, NB, fold, length),...  153 us
    psum x1, waiting for transfers between devices, on_device(): lax.psum((term_mixer_right, term_mixer_left), ('dp', 'mp'))  146 us
    convert_element_type x2, local copies, waits for them, and re-layouts, on_device(): time_mixed.astype(jnp.float32)  54.9 us
    another operation x4, local copies, waits for them, and re-layouts  51.3 us
    dot_general x2, matrix products, grad_positions(): jnp.einsum('scek,scbef->ekbf', left_side, right_side, preferred_element_t...  40.7 us
  transfers between devices with their start and end apart: 4, of which 3 were waited for; matrix products, arithmetic and copies ran while one was open for 6% of the time, Pallas kernels for 0%

commit v1 on v0

v1 whole, which is shorter than its diff:
```python
import functools

import jax
import jax.numpy as jnp
from jax import lax
from jax.experimental import pallas as pl
from jax.experimental.pallas import tpu as pltpu
from jax.sharding import PartitionSpec as P

NB = 64
BS = 128
LB = 64
LS = 128
LANES = 128
CHUNKS = 2
UNROLL = 4
VMEM = 60 * 1024 * 1024
F32 = jnp.float32
BF16 = jnp.bfloat16

NN = (((1,), (0,)), ((), ()))
NT = (((1,), (1,)), ((), ()))
TN = (((0,), (0,)), ((), ()))


def dot(left, right, dims=NN):
    return lax.dot_general(left, right, dims, preferred_element_type=F32)


def each(count, step, unroll=UNROLL):
    def group(index, carry):
        for inner in range(unroll):
            step(index * unroll + inner, inner)
        return carry

    lax.fori_loop(0, count // unroll, group, 0)


def block_of(index, size):
    return pl.ds(pl.multiple_of(index * size, size), size)


def gathered(ref, index, blocks, size):
    fold = size // blocks
    parts = [ref[pl.ds(f * blocks + index, blocks, stride=size), :] for f in range(fold)]
    return jnp.concatenate(parts, 0).astype(BF16)


def gathered_natural(ref, index, blocks, size):
    fold = size // blocks
    parts = [ref[pl.ds(index * fold + f, blocks, stride=size), :] for f in range(fold)]
    return jnp.concatenate(parts, 0).astype(BF16)


def mix_kernel(x_ref, right_ref, left_ref, order_ref, *refs):
    hidden_refs, (time_ref, first_ref, one, two) = refs[:CHUNKS], refs[CHUNKS:]

    def first(b, _):
        one[block_of(b, LS), :] = dot(right_ref[b], x_ref[:, block_of(b, LS)], NT)

    def second(e, _):
        rows = gathered(one, e, LB, LS)
        first_ref[e] = rows
        two[block_of(e, LS), :] = dot(left_ref[e], rows)

    devices, _, piece = hidden_refs[0].shape
    per_device = LB // devices
    per_chunk = piece // LS

    def third(e, inner):
        mixed = dot(gathered(two, e, LB, LS), order_ref[...], TN)
        time_ref[:, block_of(e, LS)] = mixed.astype(BF16)
        x = x_ref[:, block_of(e, LS)].astype(F32)
        hidden = x + x * jax.nn.sigmoid(x) * mixed.astype(BF16).astype(F32)
        place = pl.ds(inner % per_chunk * LS, LS)
        hidden_refs[inner // per_chunk][e // per_device, :, place] = hidden.astype(BF16)

    each(LB, first)
    each(LB, second)
    each(LB, third, per_device)


def feature_kernel(
    hidden_ref, above_ref, right_ref, right_back_ref, left_ref, left_back_ref, order_ref,
    out_ref, grad_ref, term_right_ref, term_left_ref, one, two, direct, panel,
):
    @pl.when(pl.program_id(0) == 0)
    def _():
        term_right_ref[...] = jnp.zeros_like(term_right_ref)
        term_left_ref[...] = jnp.zeros_like(term_left_ref)

    def first(b, _):
        one[block_of(b, BS), :] = dot(right_ref[b], hidden_ref[block_of(b, BS), :])

    def second(e, _):
        rows = gathered(one, e, NB, BS)
        panel[e] = rows
        two[block_of(e, BS), :] = dot(left_ref[e], rows)

    def third(e, _):
        rows = block_of(e, BS)
        gate = dot(order_ref[...], gathered(two, e, NB, BS))
        hidden = hidden_ref[rows, :].astype(F32)
        above = above_ref[rows, :].astype(F32)
        sigma = jax.nn.sigmoid(gate)
        through = 1.0 + gate * sigma
        slope = sigma * (1.0 + gate * (1.0 - sigma))
        out_ref[rows, :] = (hidden * through).astype(BF16)
        direct[rows, :] = above * through
        one[rows, :] = above * hidden * slope

    def fourth(e, _):
        rows = gathered_natural(one, e, NB, BS)
        two[block_of(e, BS), :] = dot(left_back_ref[e], rows)
        term_left_ref[e] += dot(panel[e], rows, NT)

    def fifth(b, _):
        rows = gathered(two, b, NB, BS)
        place = block_of(b, BS)
        grad_ref[place, :] = (direct[place, :] + dot(right_back_ref[b], rows)).astype(BF16)
        term_right_ref[b] += dot(hidden_ref[place, :], rows, NT)

    each(NB, first)
    each(NB, second)
    each(NB, third)
    each(NB, fourth)
    each(NB, fifth)


def back_kernel(x_ref, time_ref, first_ref, right_ref, left_back_ref, eye_ref, *refs):
    grad_refs = refs[:CHUNKS]
    out_ref, term_right_ref, term_left_ref, one, two = refs[CHUNKS:]
    devices, _, piece = grad_refs[0].shape
    per_device = LB // devices
    per_chunk = piece // LS

    @pl.when(pl.program_id(0) == 0)
    def _():
        term_right_ref[...] = jnp.zeros_like(term_right_ref)
        term_left_ref[...] = jnp.zeros_like(term_left_ref)

    def grad_of(e, inner):
        place = pl.ds(inner % per_chunk * LS, LS)
        return grad_refs[inner // per_chunk][e // per_device, :, place].astype(F32)

    def first(e, inner):
        x = x_ref[:, block_of(e, LS)].astype(F32)
        grad_time = (grad_of(e, inner) * (x * jax.nn.sigmoid(x))).astype(BF16)
        one[block_of(e, LS), :] = dot(eye_ref[...], grad_time, NT)

    def second(e, _):
        rows = gathered_natural(one, e, LB, LS)
        two[block_of(e, LS), :] = dot(left_back_ref[e], rows)
        term_left_ref[e] += dot(first_ref[e], rows, NT)

    def third(b, inner):
        place = block_of(b, LS)
        rows = gathered(two, b, LB, LS)
        x = x_ref[:, place]
        term = dot(rows, right_ref[b], TN)
        values = x.astype(F32)
        sigma = jax.nn.sigmoid(values)
        slope = sigma * (1.0 + values * (1.0 - sigma))
        grad = grad_of(b, inner)
        result = grad * (1.0 + slope * time_ref[:, place].astype(F32)) + term
        out_ref[:, place] = result.astype(BF16)
        term_right_ref[b] += lax.dot_general(
            x, rows, (((0,), (1,)), ((), ())), preferred_element_type=F32
        )

    each(LB, first, per_device)
    each(LB, second)
    each(LB, third, per_device)


def split_kernel(whole_ref, *part_refs):
    piece = part_refs[0].shape[-1]
    for part, ref in enumerate(part_refs):
        ref[0] = whole_ref[:, part * piece : (part + 1) * piece]


def join_kernel(*refs):
    whole_ref = refs[-1]
    piece = refs[0].shape[-1]
    for part, ref in enumerate(refs[:-1]):
        whole_ref[:, part * piece : (part + 1) * piece] = ref[0]


def call(kernel, *args, **more):
    return pl.pallas_call(
        kernel, *args, compiler_params=pltpu.CompilerParams(vmem_limit_bytes=VMEM), **more
    )


def fixed(shape):
    return pl.BlockSpec(shape, lambda i: (0,) * len(shape), pipeline_mode=pl.Buffered(1))


def split(whole, devices):
    chans, length = whole.shape
    piece = length // (devices * CHUNKS)
    return call(
        split_kernel,
        grid=(devices,),
        in_specs=[pl.BlockSpec((chans, piece * CHUNKS), lambda i: (0, i))],
        out_specs=[pl.BlockSpec((1, chans, piece), lambda i: (i, 0, 0))] * CHUNKS,
        out_shape=[jax.ShapeDtypeStruct((devices, chans, piece), whole.dtype)] * CHUNKS,
        name="split",
    )(whole)


def join(parts):
    devices, chans, piece = parts[0].shape
    return call(
        join_kernel,
        grid=(devices,),
        in_specs=[pl.BlockSpec((1, chans, piece), lambda i: (i, 0, 0))] * CHUNKS,
        out_specs=pl.BlockSpec((chans, piece * CHUNKS), lambda i: (0, i)),
        out_shape=jax.ShapeDtypeStruct((chans, devices * CHUNKS * piece), parts[0].dtype),
        name="join",
    )(*parts)


def mix(inputs, right, left, order, devices):
    chans, length = inputs.shape
    piece = length // (devices * CHUNKS)
    table = fixed((LB, LS, LS))
    strip = pl.BlockSpec((LANES, length), lambda i: (i, 0))
    results = call(
        mix_kernel,
        grid=(chans // LANES,),
        in_specs=[strip, table, table, fixed((LS, LS))],
        out_specs=[pl.BlockSpec((devices, LANES, piece), lambda i: (0, i, 0))] * CHUNKS
        + [strip, pl.BlockSpec((LB, LS, LANES), lambda i: (0, 0, i))],
        out_shape=[jax.ShapeDtypeStruct((devices, chans, piece), BF16)] * CHUNKS
        + [
            jax.ShapeDtypeStruct((chans, length), BF16),
            jax.ShapeDtypeStruct((LB, LS, chans), BF16),
        ],
        scratch_shapes=[pltpu.VMEM((length, LANES), F32)] * 2,
        name="mix",
    )(inputs, right, left, order)
    return results[:CHUNKS], results[CHUNKS], results[CHUNKS + 1]


def feature(hidden, above, right, right_back, left, left_back, order):
    total, piece = hidden.shape
    table = fixed((NB, BS, BS))
    strip = pl.BlockSpec((total, LANES), lambda i: (0, i))
    terms = pl.BlockSpec((NB, BS, BS), lambda i: (0, 0, 0))
    return call(
        feature_kernel,
        grid=(piece // LANES,),
        in_specs=[strip, strip, table, table, table, table, fixed((BS, BS))],
        out_specs=[strip, strip, terms, terms],
        out_shape=[jax.ShapeDtypeStruct((total, piece), BF16)] * 2
        + [jax.ShapeDtypeStruct((NB, BS, BS), F32)] * 2,
        scratch_shapes=[pltpu.VMEM((total, LANES), F32)] * 3
        + [pltpu.VMEM((NB, BS, LANES), BF16)],
        name="feature",
    )(hidden, above, right, right_back, left, left_back, order)


def back(inputs, time_mixed, first_mix, right, left_back, eye, grads):
    chans, length = inputs.shape
    devices, _, piece = grads[0].shape
    table = fixed((LB, LS, LS))
    strip = pl.BlockSpec((LANES, length), lambda i: (i, 0))
    terms = pl.BlockSpec((LB, LS, LS), lambda i: (0, 0, 0))
    return call(
        back_kernel,
        grid=(chans // LANES,),
        in_specs=[
            strip, strip, pl.BlockSpec((LB, LS, LANES), lambda i: (0, 0, i)),
            table, table, fixed((LS, LS)),
        ]
        + [pl.BlockSpec((devices, LANES, piece), lambda i: (0, i, 0))] * CHUNKS,
        out_specs=[strip, terms, terms],
        out_shape=[jax.ShapeDtypeStruct((chans, length), BF16)]
        + [jax.ShapeDtypeStruct((LB, LS, LS), F32)] * 2,
        scratch_shapes=[pltpu.VMEM((length, LANES), F32)] * 2,
        name="back",
    )(inputs, time_mixed, first_mix, right, left_back, eye, *grads)


def unfolded(table, axis, blocks):
    shape = table.shape
    fold = shape[axis] // blocks
    cut = table.reshape(shape[:axis] + (blocks, fold) + shape[axis + 1 :])
    return jnp.swapaxes(cut, axis, axis + 1).reshape(shape)


def folded(table, axis, fold):
    shape = table.shape
    cut = table.reshape(shape[:axis] + (fold, shape[axis] // fold) + shape[axis + 1 :])
    return jnp.swapaxes(cut, axis, axis + 1).reshape(shape)


def log2(size):
    return size.bit_length() - 1


def scatter_sum(terms, groups):
    blocks, size, width = terms[0].shape
    dp, mp = lax.axis_size("dp"), lax.axis_size("mp")

    def halve(parts, name, bit, outer, kind):
        count = lax.axis_size(name)
        mine = (lax.axis_index(name) >> bit) & 1
        parts = [part.reshape(outer, 2, -1, width) for part in parts]
        keep = sum(lax.dynamic_index_in_dim(part, mine, 1, keepdims=False) for part in parts)
        give = sum(lax.dynamic_index_in_dim(part, 1 - mine, 1, keepdims=False) for part in parts)
        got = lax.ppermute(give.astype(kind), name, [(i, i ^ (1 << bit)) for i in range(count)])
        return [keep + got.astype(F32)]

    for bit in range(log2(dp)):
        terms = halve(terms, "dp", bit, blocks * groups * (dp >> (bit + 1)), F32 if bit == 0 else BF16)
    for bit in range(log2(mp)):
        terms = halve(terms, "mp", bit, mp >> (bit + 1), BF16)
    return terms[0].reshape(blocks // mp, size // dp, width)


def gathered_tables(*tables):
    kinds = len(tables)
    share, size, width = tables[0].shape
    dp, mp = lax.axis_size("dp"), lax.axis_size("mp")
    cut = jnp.stack(tables).reshape(kinds, share, dp, size // dp, width)
    cut = lax.dynamic_index_in_dim(cut, lax.axis_index("dp"), 2, keepdims=False)
    full = lax.all_gather(cut, ("dp", "mp"), axis=0, tiled=False)
    full = full.reshape(dp, mp, kinds, share, size // dp, width).transpose(2, 1, 3, 0, 4, 5)
    return full.reshape(kinds, mp * share, size, width)


def on_device(inputs, cotangent, mixer_right, mixer_left, dense_right, dense_left):
    batch, chans, length = inputs.shape
    devices = lax.axis_size("mp")
    fold = LS // LB
    inputs = inputs.reshape(batch * chans, length)
    cotangent = cotangent.reshape(batch * chans, length)

    def exchange(part):
        shape = part.shape
        part = part.reshape(devices, chans, length // (devices * CHUNKS))
        return lax.all_to_all(part, "mp", 0, 0, tiled=True).reshape(shape)

    def rows(part):
        return part.reshape(devices * chans, -1)

    sent = split(cotangent, devices)
    sent, inputs, mixer_right, mixer_left = lax.optimization_barrier(
        (sent, inputs, mixer_right, mixer_left)
    )
    above = []
    for part in sent:
        if above:
            part, above[-1] = lax.optimization_barrier((part, above[-1]))
        above.append(exchange(part))

    eye = jnp.eye(LS, dtype=BF16)
    order = unfolded(eye, 0, LB)
    mix_right = unfolded(mixer_right, 2, LB).swapaxes(1, 2)
    mix_left_back = unfolded(unfolded(mixer_left, 1, LB), 2, LB)
    mix_left = mix_left_back.swapaxes(1, 2)
    right_back, left_back = gathered_tables(
        unfolded(dense_right, 2, NB), unfolded(unfolded(dense_left, 1, NB), 2, NB)
    )
    right, left = right_back.swapaxes(1, 2), left_back.swapaxes(1, 2)

    hidden, time_mixed, first_mix = mix(inputs, mix_right, mix_left, order, devices)
    tables = (right, right_back, left, left_back)
    hidden, above, tables = lax.optimization_barrier((hidden, above, tables))
    arrived = []
    for part in hidden:
        if arrived:
            part, arrived[-1] = lax.optimization_barrier((part, arrived[-1]))
        arrived.append(exchange(part))
    outs, grads, rights, lefts = [], [], [], []
    for part in range(CHUNKS):
        out, grad, term_right, term_left = feature(
            rows(arrived[part]), rows(above[part]), *tables, order.T
        )
        outs.append(out.reshape(devices, chans, -1))
        grad = grad.reshape(devices, chans, -1)
        if part:
            grad, grads[-1] = lax.optimization_barrier((grad, grads[-1]))
        grads.append(exchange(grad))
        rights.append(term_right)
        lefts.append(term_left)
    dense_rsum = scatter_sum(rights, 1)
    dense_lsum = scatter_sum(lefts, fold)
    grads, outs, dense_rsum, dense_lsum = lax.optimization_barrier(
        (grads, outs, dense_rsum, dense_lsum)
    )
    returned = [exchange(outs[0])]
    grad_inputs, term_right, term_left = back(
        inputs, time_mixed, first_mix, mix_right, mix_left_back, eye, grads
    )
    grad_inputs, term_right, term_left, outs, returned = lax.optimization_barrier(
        (grad_inputs, term_right, term_left, outs, returned)
    )
    for part in outs[1:]:
        part, returned[-1] = lax.optimization_barrier((part, returned[-1]))
        returned.append(exchange(part))
    mixer_rsum = scatter_sum([term_right], 1)
    mixer_lsum = scatter_sum([term_left], fold)
    block_out = join(returned)

    sequences = batch * lax.axis_size("dp")
    dense_scale = float(sequences * length) ** (-0.5)
    mixer_scale = float(sequences * chans * devices) ** (-0.5)
    return (
        block_out.reshape(batch, chans, length),
        grad_inputs.reshape(batch, chans, length),
        folded(mixer_rsum, 2, fold) * mixer_scale,
        folded(folded(mixer_lsum, 1, fold), 2, fold) * mixer_scale,
        folded(dense_rsum, 2, fold) * dense_scale,
        folded(folded(dense_lsum, 1, fold), 2, fold) * dense_scale,
    )


def solution(mesh):
    whole = P("dp", "mp", None)
    table = P("mp", None, None)
    return jax.shard_map(
        on_device,
        mesh=mesh,
        in_specs=(whole, whole, P(), P(), table, table),
        out_specs=(whole, whole) + (P("mp", "dp", None),) * 4,
        check_vma=False,
    )
```

time: 1500 us -> 857 us (0.57)
  blocking collectives: 396 us -> 100 us
  local copies, waits for them, and re-layouts: 335 us -> 50.1 us
  Pallas kernels: 0 us -> 277 us
  matrix products: 170 us -> 0 us
  waiting for transfers between devices: 467 us -> 300 us
  starting transfers between devices: 13.8 us -> 92.9 us
  other arithmetic: 89.6 us -> 20.4 us
    all_to_all x2 -> x1, blocking collectives: 396 us -> 100 us  [exchange(): return lax.all_to_all(part, 'mp', 0, 0, tiled=True).reshape(shape)]
    pallas_call x0 -> x6, Pallas kernels: none -> 277 us  [the longest x2 117 us: feature(): call(feature_kernel, grid=(piece // LANES,), in_specs=[strip, strip, tabl...]
    all_to_all x2 -> x7, waiting for transfers between devices: 321 us -> 139 us  [exchange(): return lax.all_to_all(part, 'mp', 0, 0, tiled=True).reshape(shape)]
    dot_general x12 -> x0, matrix products: 170 us -> none  [the longest x2 40.7 us: grad_positions(): jnp.einsum('scek,scbef->ekbf', left_side, right_side, preferred_element_t...]
    ppermute x0 -> x20, waiting for transfers between devices: none -> 162 us  [halve(): lax.ppermute(give.astype(kind), name, [(i, i ^ 1 << bit) for i in range(c...]
    psum x1 -> x0, waiting for transfers between devices: 146 us -> none  [on_device(): lax.psum((term_mixer_right, term_mixer_left), ('dp', 'mp'))]
    convert_element_type x8 -> x16, local copies, waits for them, and re-layouts: 143 us -> 1.5 us  [halve(): give.astype(kind)]
    convert_element_type x4 -> x2, other arithmetic: 88 us -> 1.33 us  [on_device(): eye = jnp.eye(LS, dtype=BF16)]
  transfers between devices with their start and end apart: 4 -> 28, of which waited for: 3 -> 20; matrix products, arithmetic and copies ran while one was open for 6% -> 8% of each run, Pallas kernels for 0% -> 30%
where the time goes in v1:
time: 857 us; the launch traced here: 855 us
  waiting for transfers between devices  300 us (35%)
  Pallas kernels  277 us (32%)
  blocking collectives  100 us (12%)
  starting transfers between devices  92.9 us (11%)
  local copies, waits for them, and re-layouts  50.1 us (6%)
  other arithmetic  20.4 us (2%)
  between operations  14.7 us (2%)
    ppermute x20, waiting for transfers between devices, halve(): lax.ppermute(give.astype(kind), name, [(i, i ^ 1 << bit) for i in range(c...  162 us
    all_to_all x7, waiting for transfers between devices, exchange(): return lax.all_to_all(part, 'mp', 0, 0, tiled=True).reshape(shape)  139 us
    pallas_call x2, Pallas kernels, feature(): call(feature_kernel, grid=(piece // LANES,), in_specs=[strip, strip, tabl...  117 us
    all_to_all x1, blocking collectives, exchange(): return lax.all_to_all(part, 'mp', 0, 0, tiled=True).reshape(shape)  100 us
    all_to_all x7, starting transfers between devices, exchange(): return lax.all_to_all(part, 'mp', 0, 0, tiled=True).reshape(shape)  84.2 us
    pallas_call x1, Pallas kernels, back(): call(back_kernel, grid=(chans // LANES,), in_specs=[strip, strip, pl.Bloc...  75.6 us
    pallas_call x1, Pallas kernels, mix(): call(mix_kernel, grid=(chans // LANES,), in_specs=[strip, table, table, f...  60.4 us
  transfers between devices with their start and end apart: 28, of which 20 were waited for; matrix products, arithmetic and copies ran while one was open for 8% of the time, Pallas kernels for 30%

profile of v1, /device:TPU:4, one launch (start us, length us, event | category | flops | bytes accessed | tf_op | source)
XLA Modules:
  0.0 855.5 jit_solution(12887984373690844981)
XLA Ops:
  7.2 11.8 %split.1 = (bf16[16,512,256]{2,1,0:T(8,128)(2,1)}, bf16[16,512,256]{2,1,0:T(8,128)(2,1)}) custom-call(bf16[512,8192]{1,0:T(8,128)(2,1)} %bitcast.193), custom_call_target="tpu_custom_call" | custom-call | tf_op jit(solution)/shard_map/split/pallas_call | solution.py:202
  19.0 7.4 all-to-all-start
  28.3 94.4 %all-to-all-done = bf16[16,512,256]{2,1,0:T(8,128)(2,1)} async-done(((bf16[16,512,256]{2,1,0:T(8,128)(2,1)}), bf16[16,512,256]{2,1,0:T(8,128)(2,1)}, u32[]{:S(2)}, u32[]{:S(2)}) %all-to-all-start) | async-done | bytes 4194336 | tf_op jit(solution)/shard_map/all_to_all | solution.py:344
  122.7 23.0 %all-to-all-start.1 = ((bf16[16,512,256]{2,1,0:T(8,128)(2,1)}), bf16[16,512,256]{2,1,0:T(8,128)(2,1)}, u32[]{:S(2)}, u32[]{:S(2)}) async-start(bf16[16,512,256]{2,1,0:T(8,128)(2,1)} %get-tuple-element.67), calls=%async_computation.1 | async-start | bytes 8388608 | tf_op jit(solution)/shard_map/all_to_all | solution.py:344
  169.4 60.4 %mix.1 = (bf16[16,512,256]{2,1,0:T(8,128)(2,1)}, bf16[16,512,256]{2,1,0:T(8,128)(2,1)}, bf16[512,8192]{1,0:T(8,128)(2,1)}, bf16[64,128,512]{2,1,0:T(8,128)(2,1)}) custom-call(bf16[512,8192]{1,0:T(8,128)(2,1)} %bitcast.178, bf16[64,128,128]{2,1,0:T(8,128)(2,1)} %bitcast.188, bf16[64,128,128]{2,1,0:T(8,128)(2,1)} %bitcast.186, ...), custom_call_target="tpu_custom_call" | custom-call | tf_op jit(solution)/shard_map/mix/pallas_call | solution.py:229
  235.0 100.2 %all_to_all.40 = bf16[16,512,256]{2,1,0:T(8,128)(2,1)} all-to-all(bf16[16,512,256]{2,1,0:T(8,128)(2,1)} %get-tuple-element.69), channel_id=1, replica_groups=mesh['dp'=2,'mp'=16] {'mp'}, dimensions={0} | all-to-all | bytes 8388608 | tf_op jit(solution)/shard_map/all_to_all | solution.py:344
  347.6 58.6 %feature.3 = (bf16[8192,256]{1,0:T(8,128)(2,1)}, bf16[8192,256]{1,0:T(8,128)(2,1)}, f32[64,128,128]{2,1,0:T(8,128)}, f32[64,128,128]{2,1,0:T(8,128)}) custom-call(bf16[8192,256]{1,0:T(8,128)(2,1)} %bitcast.191, bf16[8192,256]{1,0:T(8,128)(2,1)} %bitcast.27.above_ref, bf16[64,128,128]{2,1,0:T(8,128)(2,1)} %copy.154.right_ref, ...), custom_call_target="tpu_custom_call" | custom-call | tf_op jit(solution)/shard_map/feature/pallas_call | solution.py:251
  406.2 17.2 %all-to-all-done.3 = bf16[16,512,256]{2,1,0:T(8,128)(2,1)} async-done(((bf16[16,512,256]{2,1,0:T(8,128)(2,1)}), bf16[16,512,256]{2,1,0:T(8,128)(2,1)}, u32[]{:S(2)}, u32[]{:S(2)}) %all-to-all-start.3) | async-done | bytes 4194336 | tf_op jit(solution)/shard_map/all_to_all | solution.py:344
  423.4 14.3 %all-to-all-start.4 = ((bf16[16,512,256]{2,1,0:T(8,128)(2,1)}), bf16[16,512,256]{2,1,0:T(8,128)(2,1)}, u32[]{:S(2)}, u32[]{:S(2)}) async-start(bf16[16,512,256]{2,1,0:T(8,128)(2,1)} %bitcast.220), calls=%async_computation.4 | async-start | bytes 8388608 | tf_op jit(solution)/shard_map/all_to_all | solution.py:344
  437.7 58.5 %feature.2 = (bf16[8192,256]{1,0:T(8,128)(2,1)}, bf16[8192,256]{1,0:T(8,128)(2,1)}, f32[64,128,128]{2,1,0:T(8,128)}, f32[64,128,128]{2,1,0:T(8,128)}) custom-call(bf16[8192,256]{1,0:T(8,128)(2,1)} %bitcast.23.hidden_ref, bf16[8192,256]{1,0:T(8,128)(2,1)} %bitcast.24.above_ref, bf16[64,128,128]{2,1,0:T(8,128)(2,1)} %copy.154.right_ref, ...), custom_call_target="tpu_custom_call" | custom-call | tf_op jit(solution)/shard_map/feature/pallas_call | solution.py:251
  496.2 24.3 %all-to-all-done.4.refs_0_ = bf16[16,512,256]{2,1,0:T(8,128)(2,1)} async-done(((bf16[16,512,256]{2,1,0:T(8,128)(2,1)}), bf16[16,512,256]{2,1,0:T(8,128)(2,1)}, u32[]{:S(2)}, u32[]{:S(2)}) %all-to-all-start.4) | async-done | bytes 4194336 | tf_op jit(solution)/shard_map/all_to_all | solution.py:344
  520.5 15.0 %all-to-all-start.5 = ((bf16[16,512,256]{2,1,0:T(8,128)(2,1)}), bf16[16,512,256]{2,1,0:T(8,128)(2,1)}, u32[]{:S(2)}, u32[]{:S(2)}) async-start(bf16[16,512,256]{2,1,0:T(8,128)(2,1)} %bitcast.210), calls=%async_computation.5 | async-start | bytes 8388608 | tf_op jit(solution)/shard_map/all_to_all | solution.py:344
  553.3 8.4 collective-permute-done.6
  563.4 31.4 %collective-permute-done.1 = bf16[8,256,128]{2,1,0:T(8,128)(2,1)} collective-permute-done((bf16[8,256,128]{2,1,0:T(8,128)(2,1)S(1)}, bf16[8,256,128]{2,1,0:T(8,128)(2,1)}, u32[]{:S(2)}, u32[]{:S(2)}) %collective-permute-start.1) | collective-permute-done | bytes 524320 | tf_op jit(solution)/shard_map/ppermute | solution.py:313
  597.4 15.5 %collective-permute-done.2 = bf16[4,256,128]{2,1,0:T(8,128)(2,1)S(1)} collective-permute-done((bf16[4,256,128]{2,1,0:T(8,128)(2,1)S(1)}, bf16[4,256,128]{2,1,0:T(8,128)(2,1)S(1)}, u32[]{:S(2)}, u32[]{:S(2)}) %collective-permute-start.2) | collective-permute-done | bytes 262176 | tf_op jit(solution)/shard_map/ppermute | solution.py:313
  621.1 12.9 %collective-permute-done.9 = bf16[1,256,128]{2,1,0:T(8,128)(2,1)S(1)} collective-permute-done((bf16[1,256,128]{2,1,0:T(8,128)(2,1)S(1)}, bf16[1,256,128]{2,1,0:T(8,128)(2,1)S(1)}, u32[]{:S(2)}, u32[]{:S(2)}) %collective-permute-start.9) | collective-permute-done | bytes 65568 | tf_op jit(solution)/shard_map/ppermute | solution.py:313
  642.9 75.6 %back.1 = (bf16[512,8192]{1,0:T(8,128)(2,1)}, f32[64,128,128]{2,1,0:T(8,128)}, f32[64,128,128]{2,1,0:T(8,128)}) custom-call(bf16[512,8192]{1,0:T(8,128)(2,1)} %bitcast.179, bf16[512,8192]{1,0:T(8,128)(2,1)} %get-tuple-element.60.time_ref, bf16[64,128,512]{2,1,0:T(8,128)(2,1)} %get-tuple-element.61.first_ref, bf16[64,128,128]{2,1,0:T(8,128)(2,1)} %bitcast.189, ...), custom_call_target="tpu_custom_call" | custom-call | tf_op jit(solution)/shard_map/back/pallas_call | solution.py:270
  721.4 14.5 %all-to-all-start.7 = ((bf16[16,512,256]{2,1,0:T(8,128)(2,1)}), bf16[16,512,256]{2,1,0:T(8,128)(2,1)}, u32[]{:S(2)}, u32[]{:S(2)}) async-start(bf16[16,512,256]{2,1,0:T(8,128)(2,1)} %bitcast.208), calls=%async_computation.7 | async-start | bytes 8388608 | tf_op jit(solution)/shard_map/all_to_all | solution.py:344
  750.3 13.1 %collective-permute-done.16 = bf16[8,256,128]{2,1,0:T(8,128)(2,1)} collective-permute-done((bf16[8,256,128]{2,1,0:T(8,128)(2,1)S(1)}, bf16[8,256,128]{2,1,0:T(8,128)(2,1)}, u32[]{:S(2)}, u32[]{:S(2)}) %collective-permute-start.16) | collective-permute-done | bytes 524320 | tf_op jit(solution)/shard_map/ppermute | solution.py:313
  765.0 30.2 %collective-permute-done.11 = bf16[8,256,128]{2,1,0:T(8,128)(2,1)} collective-permute-done((bf16[8,256,128]{2,1,0:T(8,128)(2,1)}, bf16[8,256,128]{2,1,0:T(8,128)(2,1)}, u32[]{:S(2)}, u32[]{:S(2)}) %collective-permute-start.11) | collective-permute-done | bytes 524320 | tf_op jit(solution)/shard_map/ppermute | solution.py:313
  796.7 15.1 %collective-permute-done.12 = bf16[4,256,128]{2,1,0:T(8,128)(2,1)S(1)} collective-permute-done((bf16[4,256,128]{2,1,0:T(8,128)(2,1)S(1)}, bf16[4,256,128]{2,1,0:T(8,128)(2,1)S(1)}, u32[]{:S(2)}, u32[]{:S(2)}) %collective-permute-start.12) | collective-permute-done | bytes 262176 | tf_op jit(solution)/shard_map/ppermute | solution.py:313
  812.9 8.2 collective-permute-done.13
  821.2 13.2 %collective-permute-done.19 = bf16[1,256,128]{2,1,0:T(8,128)(2,1)S(1)} collective-permute-done((bf16[1,256,128]{2,1,0:T(8,128)(2,1)S(1)}, bf16[1,256,128]{2,1,0:T(8,128)(2,1)S(1)}, u32[]{:S(2)}, u32[]{:S(2)}) %collective-permute-start.19) | collective-permute-done | bytes 65568 | tf_op jit(solution)/shard_map/ppermute | solution.py:313
  836.8 11.8 %join.1 = bf16[512,8192]{1,0:T(8,128)(2,1)} custom-call(bf16[16,512,256]{2,1,0:T(8,128)(2,1)} %all-to-all-done.6.refs_0_, bf16[16,512,256]{2,1,0:T(8,128)(2,1)} %all-to-all-done.7.refs_1_), custom_call_target="tpu_custom_call" | custom-call | tf_op jit(solution)/shard_map/join/pallas_call | solution.py:214
  (144 shorter events, 105.7 us)
Async XLA Ops:
  19.0 103.7 %all-to-all-start = ((bf16[16,512,256]{2,1,0:T(8,128)(2,1)}), bf16[16,512,256]{2,1,0:T(8,128)(2,1)}, u32[]{:S(2)}, u32[]{:S(2)}) async-start(bf16[16,512,256]{2,1,0:T(8,128)(2,1)} %get-tuple-element.65), calls=%async_computation | async-start | bytes 8388608 | tf_op jit(solution)/shard_map/all_to_all | solution.py:344
  26.4 203.4 %all-gather.3.cloned.1.call-start = ((), (), s32[]{:S(2)}) async-start(), calls=%async_computation.8 | async-start | bytes 4325376 | tf_op jit(solution)/shard_map/all_gather | solution.py:329
  122.7 112.3 %all-to-all-start.1 = ((bf16[16,512,256]{2,1,0:T(8,128)(2,1)}), bf16[16,512,256]{2,1,0:T(8,128)(2,1)}, u32[]{:S(2)}, u32[]{:S(2)}) async-start(bf16[16,512,256]{2,1,0:T(8,128)(2,1)} %get-tuple-element.67), calls=%async_computation.1 | async-start | bytes 8388608 | tf_op jit(solution)/shard_map/all_to_all | solution.py:344
  335.2 88.1 %all-to-all-start.3 = ((bf16[16,512,256]{2,1,0:T(8,128)(2,1)}), bf16[16,512,256]{2,1,0:T(8,128)(2,1)}, u32[]{:S(2)}, u32[]{:S(2)}) async-start(bf16[16,512,256]{2,1,0:T(8,128)(2,1)} %get-tuple-element.70), calls=%async_computation.3 | async-start | bytes 8388608 | tf_op jit(solution)/shard_map/all_to_all | solution.py:344
  423.4 97.1 %all-to-all-start.4 = ((bf16[16,512,256]{2,1,0:T(8,128)(2,1)}), bf16[16,512,256]{2,1,0:T(8,128)(2,1)}, u32[]{:S(2)}, u32[]{:S(2)}) async-start(bf16[16,512,256]{2,1,0:T(8,128)(2,1)} %bitcast.220), calls=%async_computation.4 | async-start | bytes 8388608 | tf_op jit(solution)/shard_map/all_to_all | solution.py:344
  520.5 114.2 %all-to-all-start.5 = ((bf16[16,512,256]{2,1,0:T(8,128)(2,1)}), bf16[16,512,256]{2,1,0:T(8,128)(2,1)}, u32[]{:S(2)}, u32[]{:S(2)}) async-start(bf16[16,512,256]{2,1,0:T(8,128)(2,1)} %bitcast.210), calls=%async_computation.5 | async-start | bytes 8388608 | tf_op jit(solution)/shard_map/all_to_all | solution.py:344
  546.7 15.0 %collective-permute-start.6 = (bf16[8,256,128]{2,1,0:T(8,128)(2,1)S(1)}, bf16[8,256,128]{2,1,0:T(8,128)(2,1)}, u32[]{:S(2)}, u32[]{:S(2)}) collective-permute-start(bf16[8,256,128]{2,1,0:T(8,128)(2,1)S(1)} %fusion.7), channel_id=1, source_target_pairs={{0,1},{1,0},{2,3},{3,2},{4,5},{5,4},{6,7},{7,6},{8,9},{9,8},{10,11... | collective-permute-start | bytes 1572872 | tf_op jit(solution)/shard_map/ppermute | solution.py:313
  551.9 42.9 %collective-permute-start.1 = (bf16[8,256,128]{2,1,0:T(8,128)(2,1)S(1)}, bf16[8,256,128]{2,1,0:T(8,128)(2,1)}, u32[]{:S(2)}, u32[]{:S(2)}) collective-permute-start(bf16[8,256,128]{2,1,0:T(8,128)(2,1)S(1)} %fusion.6), channel_id=1, source_target_pairs={{0,1},{1,0},{2,3},{3,2},{4,5},{5,4},{6,7},{7,6},{8,9},{9,8},{10,11... | collective-permute-start | bytes 1572872 | tf_op jit(solution)/shard_map/ppermute | solution.py:313
  562.9 33.2 %collective-permute-start.7 = (bf16[4,256,128]{2,1,0:T(8,128)(2,1)S(1)}, bf16[4,256,128]{2,1,0:T(8,128)(2,1)S(1)}, u32[]{:S(2)}, u32[]{:S(2)}) collective-permute-start(bf16[4,256,128]{2,1,0:T(8,128)(2,1)S(1)} %fusion.11), channel_id=1, source_target_pairs={{0,2},{1,3},{2,0},{3,1},{4,6},{5,7},{6,4},{7,5},{8,10},{9,11},{10,... | collective-permute-start | bytes 786440 | tf_op jit(solution)/shard_map/ppermute | solution.py:313
  596.0 16.9 %collective-permute-start.2 = (bf16[4,256,128]{2,1,0:T(8,128)(2,1)S(1)}, bf16[4,256,128]{2,1,0:T(8,128)(2,1)S(1)}, u32[]{:S(2)}, u32[]{:S(2)}) collective-permute-start(bf16[4,256,128]{2,1,0:T(8,128)(2,1)S(1)} %fusion.10), channel_id=1, source_target_pairs={{0,2},{1,3},{2,0},{3,1},{4,6},{5,7},{6,4},{7,5},{8,10},{9,11},{10,... | collective-permute-start | bytes 786440 | tf_op jit(solution)/shard_map/ppermute | solution.py:313
  596.2 21.1 %collective-permute-start.8 = (bf16[2,256,128]{2,1,0:T(8,128)(2,1)S(1)}, bf16[2,256,128]{2,1,0:T(8,128)(2,1)S(1)}, u32[]{:S(2)}, u32[]{:S(2)}) collective-permute-start(bf16[2,256,128]{2,1,0:T(8,128)(2,1)S(1)} %fusion.15), channel_id=1, source_target_pairs={{0,4},{1,5},{2,6},{3,7},{4,0},{5,1},{6,2},{7,3},{8,12},{9,13},{10,... | collective-permute-start | bytes 393224 | tf_op jit(solution)/shard_map/ppermute | solution.py:313
  613.0 7.9 collective-permute-start.3
  617.3 16.7 %collective-permute-start.9 = (bf16[1,256,128]{2,1,0:T(8,128)(2,1)S(1)}, bf16[1,256,128]{2,1,0:T(8,128)(2,1)S(1)}, u32[]{:S(2)}, u32[]{:S(2)}) collective-permute-start(bf16[1,256,128]{2,1,0:T(8,128)(2,1)S(1)} %dynamic-slice_convert_fusion.13), channel_id=1, source_target_pairs={{0,8},{1,9},{2,10},{3,11},{4,12},{5,13},{6,14},{7,15},{8,0},{9,1},... | collective-permute-start | bytes 196616 | tf_op jit(solution)/shard_map/ppermute | solution.py:313
  621.0 13.7 %collective-permute-start.4 = (bf16[1,256,128]{2,1,0:T(8,128)(2,1)S(1)}, bf16[1,256,128]{2,1,0:T(8,128)(2,1)S(1)}, u32[]{:S(2)}, u32[]{:S(2)}) collective-permute-start(bf16[1,256,128]{2,1,0:T(8,128)(2,1)S(1)} %dynamic-slice_convert_fusion.14), channel_id=1, source_target_pairs={{0,8},{1,9},{2,10},{3,11},{4,12},{5,13},{6,14},{7,15},{8,0},{9,1},... | collective-permute-start | bytes 196616 | tf_op jit(solution)/shard_map/ppermute | solution.py:313
  634.7 86.7 %all-to-all-start.6 = ((bf16[16,512,256]{2,1,0:T(8,128)(2,1)}), bf16[16,512,256]{2,1,0:T(8,128)(2,1)}, u32[]{:S(2)}, u32[]{:S(2)}) async-start(bf16[16,512,256]{2,1,0:T(8,128)(2,1)} %bitcast.209), calls=%async_computation.6 | async-start | bytes 8388608 | tf_op jit(solution)/shard_map/all_to_all | solution.py:344
  721.4 115.5 %all-to-all-start.7 = ((bf16[16,512,256]{2,1,0:T(8,128)(2,1)}), bf16[16,512,256]{2,1,0:T(8,128)(2,1)}, u32[]{:S(2)}, u32[]{:S(2)}) async-start(bf16[16,512,256]{2,1,0:T(8,128)(2,1)} %bitcast.208), calls=%async_computation.7 | async-start | bytes 8388608 | tf_op jit(solution)/shard_map/all_to_all | solution.py:344
  742.7 20.7 %collective-permute-start.16 = (bf16[8,256,128]{2,1,0:T(8,128)(2,1)S(1)}, bf16[8,256,128]{2,1,0:T(8,128)(2,1)}, u32[]{:S(2)}, u32[]{:S(2)}) collective-permute-start(bf16[8,256,128]{2,1,0:T(8,128)(2,1)S(1)} %fusion.9), channel_id=1, source_target_pairs={{0,1},{1,0},{2,3},{3,2},{4,5},{5,4},{6,7},{7,6},{8,9},{9,8},{10,11... | collective-permute-start | bytes 1572872 | tf_op jit(solution)/shard_map/ppermute | solution.py:313
  746.4 48.8 %collective-permute-start.11 = (bf16[8,256,128]{2,1,0:T(8,128)(2,1)}, bf16[8,256,128]{2,1,0:T(8,128)(2,1)}, u32[]{:S(2)}, u32[]{:S(2)}) collective-permute-start(bf16[8,256,128]{2,1,0:T(8,128)(2,1)} %fusion.8), channel_id=1, source_target_pairs={{0,1},{1,0},{2,3},{3,2},{4,5},{5,4},{6,7},{7,6},{8,9},{9,8},{10,11... | collective-permute-start | bytes 1572872 | tf_op jit(solution)/shard_map/ppermute | solution.py:313
  764.9 31.6 %collective-permute-start.17 = (bf16[4,256,128]{2,1,0:T(8,128)(2,1)S(1)}, bf16[4,256,128]{2,1,0:T(8,128)(2,1)S(1)}, u32[]{:S(2)}, u32[]{:S(2)}) collective-permute-start(bf16[4,256,128]{2,1,0:T(8,128)(2,1)S(1)} %fusion.13), channel_id=1, source_target_pairs={{0,2},{1,3},{2,0},{3,1},{4,6},{5,7},{6,4},{7,5},{8,10},{9,11},{10,... | collective-permute-start | bytes 786440 | tf_op jit(solution)/shard_map/ppermute | solution.py:313
  796.4 15.4 %collective-permute-start.12 = (bf16[4,256,128]{2,1,0:T(8,128)(2,1)S(1)}, bf16[4,256,128]{2,1,0:T(8,128)(2,1)S(1)}, u32[]{:S(2)}, u32[]{:S(2)}) collective-permute-start(bf16[4,256,128]{2,1,0:T(8,128)(2,1)S(1)} %fusion.12), channel_id=1, source_target_pairs={{0,2},{1,3},{2,0},{3,1},{4,6},{5,7},{6,4},{7,5},{8,10},{9,11},{10,... | collective-permute-start | bytes 786440 | tf_op jit(solution)/shard_map/ppermute | solution.py:313
  796.6 16.1 %collective-permute-start.18 = (bf16[2,256,128]{2,1,0:T(8,128)(2,1)S(1)}, bf16[2,256,128]{2,1,0:T(8,128)(2,1)S(1)}, u32[]{:S(2)}, u32[]{:S(2)}) collective-permute-start(bf16[2,256,128]{2,1,0:T(8,128)(2,1)S(1)} %fusion.17), channel_id=1, source_target_pairs={{0,4},{1,5},{2,6},{3,7},{4,0},{5,1},{6,2},{7,3},{8,12},{9,13},{10,... | collective-permute-start | bytes 393224 | tf_op jit(solution)/shard_map/ppermute | solution.py:313
  811.9 9.2 %collective-permute-start.13 = (bf16[2,256,128]{2,1,0:T(8,128)(2,1)S(1)}, bf16[2,256,128]{2,1,0:T(8,128)(2,1)S(1)}, u32[]{:S(2)}, u32[]{:S(2)}) collective-permute-start(bf16[2,256,128]{2,1,0:T(8,128)(2,1)S(1)} %fusion.16), channel_id=1, source_target_pairs={{0,4},{1,5},{2,6},{3,7},{4,0},{5,1},{6,2},{7,3},{8,12},{9,13},{10,... | collective-permute-start | bytes 393224 | tf_op jit(solution)/shard_map/ppermute | solution.py:313
  812.8 21.6 %collective-permute-start.19 = (bf16[1,256,128]{2,1,0:T(8,128)(2,1)S(1)}, bf16[1,256,128]{2,1,0:T(8,128)(2,1)S(1)}, u32[]{:S(2)}, u32[]{:S(2)}) collective-permute-start(bf16[1,256,128]{2,1,0:T(8,128)(2,1)S(1)} %dynamic-slice_convert_fusion.11), channel_id=1, source_target_pairs={{0,8},{1,9},{2,10},{3,11},{4,12},{5,13},{6,14},{7,15},{8,0},{9,1},... | collective-permute-start | bytes 196616 | tf_op jit(solution)/shard_map/ppermute | solution.py:313
  821.1 14.6 %collective-permute-start.14 = (bf16[1,256,128]{2,1,0:T(8,128)(2,1)S(1)}, bf16[1,256,128]{2,1,0:T(8,128)(2,1)S(1)}, u32[]{:S(2)}, u32[]{:S(2)}) collective-permute-start(bf16[1,256,128]{2,1,0:T(8,128)(2,1)S(1)} %dynamic-slice_convert_fusion.12), channel_id=1, source_target_pairs={{0,8},{1,9},{2,10},{3,11},{4,12},{5,13},{6,14},{7,15},{8,0},{9,1},... | collective-permute-start | bytes 196616 | tf_op jit(solution)/shard_map/ppermute | solution.py:313
  (17 other events, 332.0 us)
Sparse Core Ops, SparseCore 0:
  30.8 105.9 all-gather.2

commit v2 on v1

--- a/solution.py
+++ b/solution.py
@@ -173,17 +173,9 @@
     each(LB, third, per_device)
 
 
-def split_kernel(whole_ref, *part_refs):
-    piece = part_refs[0].shape[-1]
-    for part, ref in enumerate(part_refs):
-        ref[0] = whole_ref[:, part * piece : (part + 1) * piece]
-
-
-def join_kernel(*refs):
-    whole_ref = refs[-1]
-    piece = refs[0].shape[-1]
-    for part, ref in enumerate(refs[:-1]):
-        whole_ref[:, part * piece : (part + 1) * piece] = ref[0]
+def copy_kernel(from_ref, *refs):
+    to_ref = refs[-1]
+    to_ref[...] = from_ref[...].reshape(to_ref.shape)
 
 
 def call(kernel, *args, **more):
@@ -196,29 +188,33 @@
     return pl.BlockSpec(shape, lambda i: (0,) * len(shape), pipeline_mode=pl.Buffered(1))
 
 
-def split(whole, devices):
+def split(whole, devices, part):
     chans, length = whole.shape
     piece = length // (devices * CHUNKS)
     return call(
-        split_kernel,
+        copy_kernel,
         grid=(devices,),
-        in_specs=[pl.BlockSpec((chans, piece * CHUNKS), lambda i: (0, i))],
-        out_specs=[pl.BlockSpec((1, chans, piece), lambda i: (i, 0, 0))] * CHUNKS,
-        out_shape=[jax.ShapeDtypeStruct((devices, chans, piece), whole.dtype)] * CHUNKS,
+        in_specs=[pl.BlockSpec((chans, piece), lambda i: (0, i * CHUNKS + part))],
+        out_specs=pl.BlockSpec((1, chans, piece), lambda i: (i, 0, 0)),
+        out_shape=jax.ShapeDtypeStruct((devices, chans, piece), whole.dtype),
         name="split",
     )(whole)
 
 
-def join(parts):
-    devices, chans, piece = parts[0].shape
+def join(piece_in, part, whole=None):
+    devices, chans, piece = piece_in.shape
+    shape = jax.ShapeDtypeStruct((chans, devices * CHUNKS * piece), piece_in.dtype)
+    more, alias = ([], {}) if whole is None else ([whole], {1: 0})
     return call(
-        join_kernel,
+        copy_kernel,
         grid=(devices,),
-        in_specs=[pl.BlockSpec((1, chans, piece), lambda i: (i, 0, 0))] * CHUNKS,
-        out_specs=pl.BlockSpec((chans, piece * CHUNKS), lambda i: (0, i)),
-        out_shape=jax.ShapeDtypeStruct((chans, devices * CHUNKS * piece), parts[0].dtype),
+        in_specs=[pl.BlockSpec((1, chans, piece), lambda i: (i, 0, 0))]
+        + [pl.BlockSpec(memory_space=pl.ANY) for _ in more],
+        out_specs=pl.BlockSpec((chans, piece), lambda i: (0, i * CHUNKS + part)),
+        out_shape=shape,
+        input_output_aliases=alias,
         name="join",
-    )(*parts)
+    )(piece_in, *more)
 
 
 def mix(inputs, right, left, order, devices):
@@ -324,11 +320,24 @@
     kinds = len(tables)
     share, size, width = tables[0].shape
     dp, mp = lax.axis_size("dp"), lax.axis_size("mp")
-    cut = jnp.stack(tables).reshape(kinds, share, dp, size // dp, width)
-    cut = lax.dynamic_index_in_dim(cut, lax.axis_index("dp"), 2, keepdims=False)
-    full = lax.all_gather(cut, ("dp", "mp"), axis=0, tiled=False)
-    full = full.reshape(dp, mp, kinds, share, size // dp, width).transpose(2, 1, 3, 0, 4, 5)
-    return full.reshape(kinds, mp * share, size, width)
+    rows = size // dp
+    cut = jnp.stack(tables).reshape(kinds * share, dp, rows, width)
+    cut = lax.dynamic_index_in_dim(cut, lax.axis_index("dp"), 1, keepdims=False)
+
+    def double(full, name, bit, axis):
+        count = lax.axis_size(name)
+        got = lax.ppermute(full, name, [(i, i ^ (1 << bit)) for i in range(count)])
+        upper = (lax.axis_index(name) >> bit) & 1 == 1
+        return jnp.where(upper, jnp.stack([got, full], axis), jnp.stack([full, got], axis))
+
+    full = cut[None]
+    for bit in reversed(range(log2(mp))):
+        full = double(full, "mp", bit, 1).reshape(-1, kinds * share, rows, width)
+    full = full.reshape(mp * kinds * share, 1, rows, width)
+    for bit in reversed(range(log2(dp))):
+        full = double(full, "dp", bit, 2).reshape(mp * kinds * share, -1, rows, width)
+    full = full.reshape(mp, kinds, share, size, width)
+    return [full[:, kind].reshape(mp * share, size, width) for kind in range(kinds)]
 
 
 def on_device(inputs, cotangent, mixer_right, mixer_left, dense_right, dense_left):
@@ -346,24 +355,25 @@
     def rows(part):
         return part.reshape(devices * chans, -1)
 
-    sent = split(cotangent, devices)
-    sent, inputs, mixer_right, mixer_left = lax.optimization_barrier(
-        (sent, inputs, mixer_right, mixer_left)
+    right_back, left_back = gathered_tables(
+        unfolded(dense_right, 2, NB), unfolded(unfolded(dense_left, 1, NB), 2, NB)
     )
     above = []
-    for part in sent:
-        if above:
-            part, above[-1] = lax.optimization_barrier((part, above[-1]))
-        above.append(exchange(part))
+    for part in range(CHUNKS):
+        sent = split(cotangent, devices, part)
+        if part:
+            sent, above[-1] = lax.optimization_barrier((sent, above[-1]))
+        else:
+            sent, cotangent, inputs, mixer_right, mixer_left = lax.optimization_barrier(
+                (sent, cotangent, inputs, mixer_right, mixer_left)
+            )
+        above.append(exchange(sent))
 
     eye = jnp.eye(LS, dtype=BF16)
     order = unfolded(eye, 0, LB)
     mix_right = unfolded(mixer_right, 2, LB).swapaxes(1, 2)
     mix_left_back = unfolded(unfolded(mixer_left, 1, LB), 2, LB)
     mix_left = mix_left_back.swapaxes(1, 2)
-    right_back, left_back = gathered_tables(
-        unfolded(dense_right, 2, NB), unfolded(unfolded(dense_left, 1, NB), 2, NB)
-    )
     right, left = right_back.swapaxes(1, 2), left_back.swapaxes(1, 2)
 
     hidden, time_mixed, first_mix = mix(inputs, mix_right, mix_left, order, devices)
@@ -403,7 +413,9 @@
         returned.append(exchange(part))
     mixer_rsum = scatter_sum([term_right], 1)
     mixer_lsum = scatter_sum([term_left], fold)
-    block_out = join(returned)
+    block_out = None
+    for part in range(CHUNKS):
+        block_out = join(returned[part], part, block_out)
 
     sequences = batch * lax.axis_size("dp")
     dense_scale = float(sequences * length) ** (-0.5)

time: 857 us -> 964 us (1.12)
  waiting for transfers between devices: 300 us -> 407 us
  Pallas kernels: 277 us -> 293 us
  between operations: 14.7 us -> 1.33 us
    ppermute x0 -> x5, waiting for transfers between devices: none -> 137 us  [double(): got = lax.ppermute(full, name, [(i, i ^ 1 << bit) for i in range(count)])]
    all_to_all x7, waiting for transfers between devices: 139 us -> 119 us  [exchange(): return lax.all_to_all(part, 'mp', 0, 0, tiled=True).reshape(shape)]
    pallas_call x2 -> x4, Pallas kernels: 23.6 us -> 40.5 us  [the longest x2 20.3 us: split(): call(copy_kernel, grid=(devices,), in_specs=[pl.BlockSpec((chans, piece),...]
    ppermute x20, waiting for transfers between devices: 162 us -> 151 us  [halve(): lax.ppermute(give.astype(kind), name, [(i, i ^ 1 << bit) for i in range(c...]
  transfers between devices with their start and end apart: 28 -> 32, of which waited for: 20 -> 24; matrix products, arithmetic and copies ran while one was open for 8% -> 7% of each run, Pallas kernels for 30% -> 28%
where the time goes in v2:
time: 964 us; the launch traced here: 962 us
  waiting for transfers between devices  407 us (42%)
  Pallas kernels  293 us (30%)
  blocking collectives  98 us (10%)
  starting transfers between devices  87.3 us (9%)
  local copies, waits for them, and re-layouts  50 us (5%)
  other arithmetic  24.6 us (3%)
    ppermute x20, waiting for transfers between devices, halve(): lax.ppermute(give.astype(kind), name, [(i, i ^ 1 << bit) for i in range(c...  151 us
    ppermute x5, waiting for transfers between devices, double(): got = lax.ppermute(full, name, [(i, i ^ 1 << bit) for i in range(count)])  137 us
    all_to_all x7, waiting for transfers between devices, exchange(): return lax.all_to_all(part, 'mp', 0, 0, tiled=True).reshape(shape)  119 us
    pallas_call x2, Pallas kernels, feature(): call(feature_kernel, grid=(piece // LANES,), in_specs=[strip, strip, tabl...  117 us
    all_to_all x1, blocking collectives, exchange(): return lax.all_to_all(part, 'mp', 0, 0, tiled=True).reshape(shape)  98 us
    all_to_all x7, starting transfers between devices, exchange(): return lax.all_to_all(part, 'mp', 0, 0, tiled=True).reshape(shape)  75.7 us
    pallas_call x1, Pallas kernels, back(): call(back_kernel, grid=(chans // LANES,), in_specs=[strip, strip, pl.Bloc...  75.6 us
    pallas_call x1, Pallas kernels, mix(): call(mix_kernel, grid=(chans // LANES,), in_specs=[strip, table, table, f...  60.4 us
  transfers between devices with their start and end apart: 32, of which 24 were waited for; matrix products, arithmetic and copies ran while one was open for 7% of the time, Pallas kernels for 28%

profile of v2, /device:TPU:4, one launch (start us, length us, event | category | flops | bytes accessed | tf_op | source)
XLA Modules:
  0.0 962.0 jit_solution(3906976848394031895)
XLA Ops:
  0.6 10.1 %split.2 = bf16[16,512,256]{2,1,0:T(8,128)(2,1)} custom-call(bf16[512,8192]{1,0:T(8,128)(2,1)} %bitcast.194), custom_call_target="tpu_custom_call" | custom-call | tf_op jit(solution)/shard_map/split/pallas_call | solution.py:194
  18.0 10.1 %split.3 = bf16[16,512,256]{2,1,0:T(8,128)(2,1)} custom-call(bf16[512,8192]{1,0:T(8,128)(2,1)} %bitcast.195), custom_call_target="tpu_custom_call" | custom-call | tf_op jit(solution)/shard_map/split/pallas_call | solution.py:194
  28.2 74.8 %all-to-all-done = bf16[16,512,256]{2,1,0:T(8,128)(2,1)} async-done(((bf16[16,512,256]{2,1,0:T(8,128)(2,1)}), bf16[16,512,256]{2,1,0:T(8,128)(2,1)}, u32[]{:S(2)}, u32[]{:S(2)}) %all-to-all-start) | async-done | bytes 4194336 | tf_op jit(solution)/shard_map/all_to_all | solution.py:353
  103.0 14.9 %all-to-all-start.1 = ((bf16[16,512,256]{2,1,0:T(8,128)(2,1)}), bf16[16,512,256]{2,1,0:T(8,128)(2,1)}, u32[]{:S(2)}, u32[]{:S(2)}) async-start(bf16[16,512,256]{2,1,0:T(8,128)(2,1)} %split.3), calls=%async_computation.1 | async-start | bytes 8388608 | tf_op jit(solution)/shard_map/all_to_all | solution.py:353
  121.1 95.5 %collective-permute-done = bf16[1,8,64,128]{3,2,1,0:T(8,128)(2,1)S(1)} collective-permute-done((bf16[1,8,64,128]{3,2,1,0:T(8,128)(2,1)S(1)}, bf16[1,8,64,128]{3,2,1,0:T(8,128)(2,1)S(1)}, u32[]{:S(2)}, u32[]{:S(2)}) %collective-permute-start) | collective-permute-done | bytes 131104 | tf_op jit(solution)/shard_map/ppermute | solution.py:329
  224.1 11.9 %collective-permute-done.2 = bf16[4,8,64,128]{3,2,1,0:T(8,128)(2,1)S(1)} collective-permute-done((bf16[4,8,64,128]{3,2,1,0:T(8,128)(2,1)S(1)}, bf16[4,8,64,128]{3,2,1,0:T(8,128)(2,1)S(1)}, u32[]{:S(2)}, u32[]{:S(2)}) %collective-permute-start.2) | collective-permute-done | bytes 524320 | tf_op jit(solution)/shard_map/ppermute | solution.py:329
  236.6 22.0 %collective-permute-done.3 = bf16[8,8,64,128]{3,2,1,0:T(8,128)(2,1)S(1)} collective-permute-done((bf16[8,8,64,128]{3,2,1,0:T(8,128)(2,1)S(1)}, bf16[8,8,64,128]{3,2,1,0:T(8,128)(2,1)S(1)}, u32[]{:S(2)}, u32[]{:S(2)}) %collective-permute-start.3) | collective-permute-done | bytes 1048608 | tf_op jit(solution)/shard_map/ppermute | solution.py:329
  284.9 60.4 %mix.1 = (bf16[16,512,256]{2,1,0:T(8,128)(2,1)}, bf16[16,512,256]{2,1,0:T(8,128)(2,1)}, bf16[512,8192]{1,0:T(8,128)(2,1)}, bf16[64,128,512]{2,1,0:T(8,128)(2,1)}) custom-call(bf16[512,8192]{1,0:T(8,128)(2,1)} %bitcast.197, bf16[64,128,128]{2,1,0:T(8,128)(2,1)} %bitcast.207, bf16[64,128,128]{2,1,0:T(8,128)(2,1)} %bitcast.205, ...), custom_call_target="tpu_custom_call" | custom-call | tf_op jit(solution)/shard_map/mix/pallas_call | solution.py:225
  352.5 98.0 %all_to_all.40 = bf16[16,512,256]{2,1,0:T(8,128)(2,1)} all-to-all(bf16[16,512,256]{2,1,0:T(8,128)(2,1)} %get-tuple-element.65), channel_id=1, replica_groups=mesh['dp'=2,'mp'=16] {'mp'}, dimensions={0} | all-to-all | bytes 8388608 | tf_op jit(solution)/shard_map/all_to_all | solution.py:353
  462.8 58.5 %feature.3 = (bf16[8192,256]{1,0:T(8,128)(2,1)}, bf16[8192,256]{1,0:T(8,128)(2,1)}, f32[64,128,128]{2,1,0:T(8,128)}, f32[64,128,128]{2,1,0:T(8,128)}) custom-call(bf16[8192,256]{1,0:T(8,128)(2,1)} %bitcast.211, bf16[8192,256]{1,0:T(8,128)(2,1)} %bitcast.41.above_ref, bf16[64,128,128]{2,1,0:T(8,128)(2,1)} %copy.124.right_ref, ...), custom_call_target="tpu_custom_call" | custom-call | tf_op jit(solution)/shard_map/feature/pallas_call | solution.py:247
  521.3 17.3 %all-to-all-done.3 = bf16[16,512,256]{2,1,0:T(8,128)(2,1)} async-done(((bf16[16,512,256]{2,1,0:T(8,128)(2,1)}), bf16[16,512,256]{2,1,0:T(8,128)(2,1)}, u32[]{:S(2)}, u32[]{:S(2)}) %all-to-all-start.3) | async-done | bytes 4194336 | tf_op jit(solution)/shard_map/all_to_all | solution.py:353
  538.6 14.1 %all-to-all-start.4 = ((bf16[16,512,256]{2,1,0:T(8,128)(2,1)}), bf16[16,512,256]{2,1,0:T(8,128)(2,1)}, u32[]{:S(2)}, u32[]{:S(2)}) async-start(bf16[16,512,256]{2,1,0:T(8,128)(2,1)} %bitcast.239), calls=%async_computation.4 | async-start | bytes 8388608 | tf_op jit(solution)/shard_map/all_to_all | solution.py:353
  552.8 58.5 %feature.2 = (bf16[8192,256]{1,0:T(8,128)(2,1)}, bf16[8192,256]{1,0:T(8,128)(2,1)}, f32[64,128,128]{2,1,0:T(8,128)}, f32[64,128,128]{2,1,0:T(8,128)}) custom-call(bf16[8192,256]{1,0:T(8,128)(2,1)} %bitcast.37.hidden_ref, bf16[8192,256]{1,0:T(8,128)(2,1)} %bitcast.38.above_ref, bf16[64,128,128]{2,1,0:T(8,128)(2,1)} %copy.124.right_ref, ...), custom_call_target="tpu_custom_call" | custom-call | tf_op jit(solution)/shard_map/feature/pallas_call | solution.py:247
  611.2 24.3 %all-to-all-done.4.refs_0_ = bf16[16,512,256]{2,1,0:T(8,128)(2,1)} async-done(((bf16[16,512,256]{2,1,0:T(8,128)(2,1)}), bf16[16,512,256]{2,1,0:T(8,128)(2,1)}, u32[]{:S(2)}, u32[]{:S(2)}) %all-to-all-start.4) | async-done | bytes 4194336 | tf_op jit(solution)/shard_map/all_to_all | solution.py:353
  635.6 15.0 %all-to-all-start.5 = ((bf16[16,512,256]{2,1,0:T(8,128)(2,1)}), bf16[16,512,256]{2,1,0:T(8,128)(2,1)}, u32[]{:S(2)}, u32[]{:S(2)}) async-start(bf16[16,512,256]{2,1,0:T(8,128)(2,1)} %bitcast.230), calls=%async_computation.5 | async-start | bytes 8388608 | tf_op jit(solution)/shard_map/all_to_all | solution.py:353
  678.5 31.4 %collective-permute-done.6 = bf16[8,256,128]{2,1,0:T(8,128)(2,1)} collective-permute-done((bf16[8,256,128]{2,1,0:T(8,128)(2,1)S(1)}, bf16[8,256,128]{2,1,0:T(8,128)(2,1)}, u32[]{:S(2)}, u32[]{:S(2)}) %collective-permute-start.6) | collective-permute-done | bytes 524320 | tf_op jit(solution)/shard_map/ppermute | solution.py:309
  712.5 15.5 %collective-permute-done.7 = bf16[4,256,128]{2,1,0:T(8,128)(2,1)S(1)} collective-permute-done((bf16[4,256,128]{2,1,0:T(8,128)(2,1)S(1)}, bf16[4,256,128]{2,1,0:T(8,128)(2,1)S(1)}, u32[]{:S(2)}, u32[]{:S(2)}) %collective-permute-start.7) | collective-permute-done | bytes 262176 | tf_op jit(solution)/shard_map/ppermute | solution.py:309
  736.1 12.9 %collective-permute-done.14 = bf16[1,256,128]{2,1,0:T(8,128)(2,1)S(1)} collective-permute-done((bf16[1,256,128]{2,1,0:T(8,128)(2,1)S(1)}, bf16[1,256,128]{2,1,0:T(8,128)(2,1)S(1)}, u32[]{:S(2)}, u32[]{:S(2)}) %collective-permute-start.14) | collective-permute-done | bytes 65568 | tf_op jit(solution)/shard_map/ppermute | solution.py:309
  757.9 75.6 %back.1 = (bf16[512,8192]{1,0:T(8,128)(2,1)}, f32[64,128,128]{2,1,0:T(8,128)}, f32[64,128,128]{2,1,0:T(8,128)}) custom-call(bf16[512,8192]{1,0:T(8,128)(2,1)} %bitcast.198, bf16[512,8192]{1,0:T(8,128)(2,1)} %get-tuple-element.56.time_ref, bf16[64,128,512]{2,1,0:T(8,128)(2,1)} %get-tuple-element.57.first_ref, bf16[64,128,128]{2,1,0:T(8,128)(2,1)} %bitcast.208, ...), custom_call_target="tpu_custom_call" | custom-call | tf_op jit(solution)/shard_map/back/pallas_call | solution.py:266
  836.4 14.5 %all-to-all-start.7 = ((bf16[16,512,256]{2,1,0:T(8,128)(2,1)}), bf16[16,512,256]{2,1,0:T(8,128)(2,1)}, u32[]{:S(2)}, u32[]{:S(2)}) async-start(bf16[16,512,256]{2,1,0:T(8,128)(2,1)} %bitcast.228), calls=%async_computation.7 | async-start | bytes 8388608 | tf_op jit(solution)/shard_map/all_to_all | solution.py:353
  880.1 30.2 %collective-permute-done.16 = bf16[8,256,128]{2,1,0:T(8,128)(2,1)} collective-permute-done((bf16[8,256,128]{2,1,0:T(8,128)(2,1)}, bf16[8,256,128]{2,1,0:T(8,128)(2,1)}, u32[]{:S(2)}, u32[]{:S(2)}) %collective-permute-start.16) | collective-permute-done | bytes 524320 | tf_op jit(solution)/shard_map/ppermute | solution.py:309
  911.7 15.1 %collective-permute-done.17 = bf16[4,256,128]{2,1,0:T(8,128)(2,1)S(1)} collective-permute-done((bf16[4,256,128]{2,1,0:T(8,128)(2,1)S(1)}, bf16[4,256,128]{2,1,0:T(8,128)(2,1)S(1)}, u32[]{:S(2)}, u32[]{:S(2)}) %collective-permute-start.17) | collective-permute-done | bytes 262176 | tf_op jit(solution)/shard_map/ppermute | solution.py:309
  936.2 13.2 %collective-permute-done.24 = bf16[1,256,128]{2,1,0:T(8,128)(2,1)S(1)} collective-permute-done((bf16[1,256,128]{2,1,0:T(8,128)(2,1)S(1)}, bf16[1,256,128]{2,1,0:T(8,128)(2,1)S(1)}, u32[]{:S(2)}, u32[]{:S(2)}) %collective-permute-start.24) | collective-permute-done | bytes 65568 | tf_op jit(solution)/shard_map/ppermute | solution.py:309
  951.9 10.1 %join.3 = bf16[512,8192]{1,0:T(8,128)(2,1)} custom-call(bf16[16,512,256]{2,1,0:T(8,128)(2,1)} %all-to-all-done.7.from_ref, bf16[512,8192]{1,0:T(8,128)(2,1)} %join.2.refs_0_), custom_call_target="tpu_custom_call", output_to_operand_aliasing={{}: (1, {})} | custom-call | tf_op jit(solution)/shard_map/join/pallas_call | solution.py:208
  (160 shorter events, 156.8 us)
Async XLA Ops:
  10.7 92.2 %all-to-all-start = ((bf16[16,512,256]{2,1,0:T(8,128)(2,1)}), bf16[16,512,256]{2,1,0:T(8,128)(2,1)}, u32[]{:S(2)}, u32[]{:S(2)}) async-start(bf16[16,512,256]{2,1,0:T(8,128)(2,1)} %split.2), calls=%async_computation | async-start | bytes 8388608 | tf_op jit(solution)/shard_map/all_to_all | solution.py:353
  103.0 249.6 %all-to-all-start.1 = ((bf16[16,512,256]{2,1,0:T(8,128)(2,1)}), bf16[16,512,256]{2,1,0:T(8,128)(2,1)}, u32[]{:S(2)}, u32[]{:S(2)}) async-start(bf16[16,512,256]{2,1,0:T(8,128)(2,1)} %split.3), calls=%async_computation.1 | async-start | bytes 8388608 | tf_op jit(solution)/shard_map/all_to_all | solution.py:353
  118.6 97.9 %collective-permute-start = (bf16[1,8,64,128]{3,2,1,0:T(8,128)(2,1)S(1)}, bf16[1,8,64,128]{3,2,1,0:T(8,128)(2,1)S(1)}, u32[]{:S(2)}, u32[]{:S(2)}) collective-permute-start(bf16[1,8,64,128]{3,2,1,0:T(8,128)(2,1)S(1)} %get-tuple-element.126), channel_id=1, source_target_pairs={{0,8},{1,9},{2,10},{3,11},{4,12},{5,13},{6,14},{7,15},{8,0},{9,1},... | collective-permute-start | bytes 393224 | tf_op jit(solution)/shard_map/ppermute | solution.py:329
  236.2 22.3 %collective-permute-start.3 = (bf16[8,8,64,128]{3,2,1,0:T(8,128)(2,1)S(1)}, bf16[8,8,64,128]{3,2,1,0:T(8,128)(2,1)S(1)}, u32[]{:S(2)}, u32[]{:S(2)}) collective-permute-start(bf16[8,8,64,128]{3,2,1,0:T(8,128)(2,1)S(1)} %bitcast.226), channel_id=1, source_target_pairs={{0,1},{1,0},{2,3},{3,2},{4,5},{5,4},{6,7},{7,6},{8,9},{9,8},{10,11... | collective-permute-start | bytes 3145736 | tf_op jit(solution)/shard_map/ppermute | solution.py:329
  260.5 84.8 %collective-permute-start.4 = (bf16[128,1,64,128]{3,2,0,1:T(8,128)(2,1)}, bf16[128,1,64,128]{3,2,0,1:T(8,128)(2,1)}, u32[]{:S(2)}, u32[]{:S(2)}) collective-permute-start(bf16[128,1,64,128]{3,2,0,1:T(8,128)(2,1)} %bitcast.29), channel_id=1, source_target_pairs={{0,16},{16,0},{1,17},{17,1},{2,18},{18,2},{3,19},{19,3},{4,20},{20... | collective-permute-start | bytes 6291464 | tf_op jit(solution)/shard_map/ppermute | solution.py:329
  450.5 88.1 %all-to-all-start.3 = ((bf16[16,512,256]{2,1,0:T(8,128)(2,1)}), bf16[16,512,256]{2,1,0:T(8,128)(2,1)}, u32[]{:S(2)}, u32[]{:S(2)}) async-start(bf16[16,512,256]{2,1,0:T(8,128)(2,1)} %get-tuple-element.66), calls=%async_computation.3 | async-start | bytes 8388608 | tf_op jit(solution)/shard_map/all_to_all | solution.py:353
  538.6 96.9 %all-to-all-start.4 = ((bf16[16,512,256]{2,1,0:T(8,128)(2,1)}), bf16[16,512,256]{2,1,0:T(8,128)(2,1)}, u32[]{:S(2)}, u32[]{:S(2)}) async-start(bf16[16,512,256]{2,1,0:T(8,128)(2,1)} %bitcast.239), calls=%async_computation.4 | async-start | bytes 8388608 | tf_op jit(solution)/shard_map/all_to_all | solution.py:353
  635.6 114.2 %all-to-all-start.5 = ((bf16[16,512,256]{2,1,0:T(8,128)(2,1)}), bf16[16,512,256]{2,1,0:T(8,128)(2,1)}, u32[]{:S(2)}, u32[]{:S(2)}) async-start(bf16[16,512,256]{2,1,0:T(8,128)(2,1)} %bitcast.230), calls=%async_computation.5 | async-start | bytes 8388608 | tf_op jit(solution)/shard_map/all_to_all | solution.py:353
  661.7 15.0 %collective-permute-start.11 = (bf16[8,256,128]{2,1,0:T(8,128)(2,1)S(1)}, bf16[8,256,128]{2,1,0:T(8,128)(2,1)}, u32[]{:S(2)}, u32[]{:S(2)}) collective-permute-start(bf16[8,256,128]{2,1,0:T(8,128)(2,1)S(1)} %fusion.7), channel_id=1, source_target_pairs={{0,1},{1,0},{2,3},{3,2},{4,5},{5,4},{6,7},{7,6},{8,9},{9,8},{10,11... | collective-permute-start | bytes 1572872 | tf_op jit(solution)/shard_map/ppermute | solution.py:309
  666.9 42.9 %collective-permute-start.6 = (bf16[8,256,128]{2,1,0:T(8,128)(2,1)S(1)}, bf16[8,256,128]{2,1,0:T(8,128)(2,1)}, u32[]{:S(2)}, u32[]{:S(2)}) collective-permute-start(bf16[8,256,128]{2,1,0:T(8,128)(2,1)S(1)} %fusion.6), channel_id=1, source_target_pairs={{0,1},{1,0},{2,3},{3,2},{4,5},{5,4},{6,7},{7,6},{8,9},{9,8},{10,11... | collective-permute-start | bytes 1572872 | tf_op jit(solution)/shard_map/ppermute | solution.py:309
  677.9 33.2 %collective-permute-start.12 = (bf16[4,256,128]{2,1,0:T(8,128)(2,1)S(1)}, bf16[4,256,128]{2,1,0:T(8,128)(2,1)S(1)}, u32[]{:S(2)}, u32[]{:S(2)}) collective-permute-start(bf16[4,256,128]{2,1,0:T(8,128)(2,1)S(1)} %fusion.11), channel_id=1, source_target_pairs={{0,2},{1,3},{2,0},{3,1},{4,6},{5,7},{6,4},{7,5},{8,10},{9,11},{10,... | collective-permute-start | bytes 786440 | tf_op jit(solution)/shard_map/ppermute | solution.py:309
  711.0 16.9 %collective-permute-start.7 = (bf16[4,256,128]{2,1,0:T(8,128)(2,1)S(1)}, bf16[4,256,128]{2,1,0:T(8,128)(2,1)S(1)}, u32[]{:S(2)}, u32[]{:S(2)}) collective-permute-start(bf16[4,256,128]{2,1,0:T(8,128)(2,1)S(1)} %fusion.10), channel_id=1, source_target_pairs={{0,2},{1,3},{2,0},{3,1},{4,6},{5,7},{6,4},{7,5},{8,10},{9,11},{10,... | collective-permute-start | bytes 786440 | tf_op jit(solution)/shard_map/ppermute | solution.py:309
  711.2 21.1 %collective-permute-start.13 = (bf16[2,256,128]{2,1,0:T(8,128)(2,1)S(1)}, bf16[2,256,128]{2,1,0:T(8,128)(2,1)S(1)}, u32[]{:S(2)}, u32[]{:S(2)}) collective-permute-start(bf16[2,256,128]{2,1,0:T(8,128)(2,1)S(1)} %fusion.15), channel_id=1, source_target_pairs={{0,4},{1,5},{2,6},{3,7},{4,0},{5,1},{6,2},{7,3},{8,12},{9,13},{10,... | collective-permute-start | bytes 393224 | tf_op jit(solution)/shard_map/ppermute | solution.py:309
  732.4 16.6 %collective-permute-start.14 = (bf16[1,256,128]{2,1,0:T(8,128)(2,1)S(1)}, bf16[1,256,128]{2,1,0:T(8,128)(2,1)S(1)}, u32[]{:S(2)}, u32[]{:S(2)}) collective-permute-start(bf16[1,256,128]{2,1,0:T(8,128)(2,1)S(1)} %dynamic-slice_convert_fusion.13), channel_id=1, source_target_pairs={{0,8},{1,9},{2,10},{3,11},{4,12},{5,13},{6,14},{7,15},{8,0},{9,1},... | collective-permute-start | bytes 196616 | tf_op jit(solution)/shard_map/ppermute | solution.py:309
  736.0 13.7 %collective-permute-start.9 = (bf16[1,256,128]{2,1,0:T(8,128)(2,1)S(1)}, bf16[1,256,128]{2,1,0:T(8,128)(2,1)S(1)}, u32[]{:S(2)}, u32[]{:S(2)}) collective-permute-start(bf16[1,256,128]{2,1,0:T(8,128)(2,1)S(1)} %dynamic-slice_convert_fusion.14), channel_id=1, source_target_pairs={{0,8},{1,9},{2,10},{3,11},{4,12},{5,13},{6,14},{7,15},{8,0},{9,1},... | collective-permute-start | bytes 196616 | tf_op jit(solution)/shard_map/ppermute | solution.py:309
  749.8 86.7 %all-to-all-start.6 = ((bf16[16,512,256]{2,1,0:T(8,128)(2,1)}), bf16[16,512,256]{2,1,0:T(8,128)(2,1)}, u32[]{:S(2)}, u32[]{:S(2)}) async-start(bf16[16,512,256]{2,1,0:T(8,128)(2,1)} %bitcast.229), calls=%async_computation.6 | async-start | bytes 8388608 | tf_op jit(solution)/shard_map/all_to_all | solution.py:353
  836.4 115.5 %all-to-all-start.7 = ((bf16[16,512,256]{2,1,0:T(8,128)(2,1)}), bf16[16,512,256]{2,1,0:T(8,128)(2,1)}, u32[]{:S(2)}, u32[]{:S(2)}) async-start(bf16[16,512,256]{2,1,0:T(8,128)(2,1)} %bitcast.228), calls=%async_computation.7 | async-start | bytes 8388608 | tf_op jit(solution)/shard_map/all_to_all | solution.py:353
  857.7 20.7 %collective-permute-start.21 = (bf16[8,256,128]{2,1,0:T(8,128)(2,1)S(1)}, bf16[8,256,128]{2,1,0:T(8,128)(2,1)}, u32[]{:S(2)}, u32[]{:S(2)}) collective-permute-start(bf16[8,256,128]{2,1,0:T(8,128)(2,1)S(1)} %fusion.9), channel_id=1, source_target_pairs={{0,1},{1,0},{2,3},{3,2},{4,5},{5,4},{6,7},{7,6},{8,9},{9,8},{10,11... | collective-permute-start | bytes 1572872 | tf_op jit(solution)/shard_map/ppermute | solution.py:309
  861.4 48.9 %collective-permute-start.16 = (bf16[8,256,128]{2,1,0:T(8,128)(2,1)}, bf16[8,256,128]{2,1,0:T(8,128)(2,1)}, u32[]{:S(2)}, u32[]{:S(2)}) collective-permute-start(bf16[8,256,128]{2,1,0:T(8,128)(2,1)} %fusion.8), channel_id=1, source_target_pairs={{0,1},{1,0},{2,3},{3,2},{4,5},{5,4},{6,7},{7,6},{8,9},{9,8},{10,11... | collective-permute-start | bytes 1572872 | tf_op jit(solution)/shard_map/ppermute | solution.py:309
  880.0 31.6 %collective-permute-start.22 = (bf16[4,256,128]{2,1,0:T(8,128)(2,1)S(1)}, bf16[4,256,128]{2,1,0:T(8,128)(2,1)S(1)}, u32[]{:S(2)}, u32[]{:S(2)}) collective-permute-start(bf16[4,256,128]{2,1,0:T(8,128)(2,1)S(1)} %fusion.13), channel_id=1, source_target_pairs={{0,2},{1,3},{2,0},{3,1},{4,6},{5,7},{6,4},{7,5},{8,10},{9,11},{10,... | collective-permute-start | bytes 786440 | tf_op jit(solution)/shard_map/ppermute | solution.py:309
  911.5 15.4 %collective-permute-start.17 = (bf16[4,256,128]{2,1,0:T(8,128)(2,1)S(1)}, bf16[4,256,128]{2,1,0:T(8,128)(2,1)S(1)}, u32[]{:S(2)}, u32[]{:S(2)}) collective-permute-start(bf16[4,256,128]{2,1,0:T(8,128)(2,1)S(1)} %fusion.12), channel_id=1, source_target_pairs={{0,2},{1,3},{2,0},{3,1},{4,6},{5,7},{6,4},{7,5},{8,10},{9,11},{10,... | collective-permute-start | bytes 786440 | tf_op jit(solution)/shard_map/ppermute | solution.py:309
  911.6 16.1 %collective-permute-start.23 = (bf16[2,256,128]{2,1,0:T(8,128)(2,1)S(1)}, bf16[2,256,128]{2,1,0:T(8,128)(2,1)S(1)}, u32[]{:S(2)}, u32[]{:S(2)}) collective-permute-start(bf16[2,256,128]{2,1,0:T(8,128)(2,1)S(1)} %fusion.17), channel_id=1, source_target_pairs={{0,4},{1,5},{2,6},{3,7},{4,0},{5,1},{6,2},{7,3},{8,12},{9,13},{10,... | collective-permute-start | bytes 393224 | tf_op jit(solution)/shard_map/ppermute | solution.py:309
  927.8 21.6 %collective-permute-start.24 = (bf16[1,256,128]{2,1,0:T(8,128)(2,1)S(1)}, bf16[1,256,128]{2,1,0:T(8,128)(2,1)S(1)}, u32[]{:S(2)}, u32[]{:S(2)}) collective-permute-start(bf16[1,256,128]{2,1,0:T(8,128)(2,1)S(1)} %dynamic-slice_convert_fusion.11), channel_id=1, source_target_pairs={{0,8},{1,9},{2,10},{3,11},{4,12},{5,13},{6,14},{7,15},{8,0},{9,1},... | collective-permute-start | bytes 196616 | tf_op jit(solution)/shard_map/ppermute | solution.py:309
  936.2 14.6 %collective-permute-start.19 = (bf16[1,256,128]{2,1,0:T(8,128)(2,1)S(1)}, bf16[1,256,128]{2,1,0:T(8,128)(2,1)S(1)}, u32[]{:S(2)}, u32[]{:S(2)}) collective-permute-start(bf16[1,256,128]{2,1,0:T(8,128)(2,1)S(1)} %dynamic-slice_convert_fusion.12), channel_id=1, source_target_pairs={{0,8},{1,9},{2,10},{3,11},{4,12},{5,13},{6,14},{7,15},{8,0},{9,1},... | collective-permute-start | bytes 196616 | tf_op jit(solution)/shard_map/ppermute | solution.py:309
  (21 other events, 417.4 us)

commit v3 on v2

--- a/solution.py
+++ b/solution.py
@@ -13,6 +13,7 @@
 LS = 128
 LANES = 128
 CHUNKS = 2
+NEAR = 4
 UNROLL = 4
 VMEM = 60 * 1024 * 1024
 F32 = jnp.float32
@@ -173,9 +174,34 @@
     each(LB, third, per_device)
 
 
-def copy_kernel(from_ref, *refs):
-    to_ref = refs[-1]
-    to_ref[...] = from_ref[...].reshape(to_ref.shape)
+def move(pairs, held, arrive_sems, leave_sems):
+    arrive, leave = [], []
+    for index, (source, _) in enumerate(pairs):
+        arrive.append(pltpu.make_async_copy(source, held.at[index], arrive_sems.at[index]))
+        arrive[-1].start()
+    for index, (_, target) in enumerate(pairs):
+        arrive[index].wait()
+        leave.append(pltpu.make_async_copy(held.at[index], target, leave_sems.at[index]))
+        leave[-1].start()
+    for copy in leave:
+        copy.wait()
+
+
+def places(whole_ref, part, devices, piece):
+    return [whole_ref.at[:, pl.ds((d * CHUNKS + part) * piece, piece)] for d in range(devices)]
+
+
+def split_kernel(part, whole_ref, part_ref, *scratch):
+    devices, _, piece = part_ref.shape
+    sources = places(whole_ref, part, devices, piece)
+    move([(sources[d], part_ref.at[d]) for d in range(devices)], *scratch)
+
+
+def join_kernel(part, part_ref, *refs):
+    whole_ref, scratch = refs[-4], refs[-3:]
+    devices, _, piece = part_ref.shape
+    targets = places(whole_ref, part, devices, piece)
+    move([(part_ref.at[d], targets[d]) for d in range(devices)], *scratch)
 
 
 def call(kernel, *args, **more):
@@ -186,35 +212,37 @@
 
 def fixed(shape):
     return pl.BlockSpec(shape, lambda i: (0,) * len(shape), pipeline_mode=pl.Buffered(1))
+
+
+def moving(devices, chans, piece):
+    return [pltpu.VMEM((devices, chans, piece), BF16)] + [pltpu.SemaphoreType.DMA((devices,))] * 2
 
 
 def split(whole, devices, part):
     chans, length = whole.shape
     piece = length // (devices * CHUNKS)
     return call(
-        copy_kernel,
-        grid=(devices,),
-        in_specs=[pl.BlockSpec((chans, piece), lambda i: (0, i * CHUNKS + part))],
-        out_specs=pl.BlockSpec((1, chans, piece), lambda i: (i, 0, 0)),
+        functools.partial(split_kernel, part),
+        in_specs=[pl.BlockSpec(memory_space=pl.ANY)],
+        out_specs=pl.BlockSpec(memory_space=pl.ANY),
         out_shape=jax.ShapeDtypeStruct((devices, chans, piece), whole.dtype),
+        scratch_shapes=moving(devices, chans, piece),
         name="split",
     )(whole)
 
 
 def join(piece_in, part, whole=None):
     devices, chans, piece = piece_in.shape
-    shape = jax.ShapeDtypeStruct((chans, devices * CHUNKS * piece), piece_in.dtype)
-    more, alias = ([], {}) if whole is None else ([whole], {1: 0})
+    args = [piece_in] if whole is None else [piece_in, whole]
     return call(
-        copy_kernel,
-        grid=(devices,),
-        in_specs=[pl.BlockSpec((1, chans, piece), lambda i: (i, 0, 0))]
-        + [pl.BlockSpec(memory_space=pl.ANY) for _ in more],
-        out_specs=pl.BlockSpec((chans, piece), lambda i: (0, i * CHUNKS + part)),
-        out_shape=shape,
-        input_output_aliases=alias,
+        functools.partial(join_kernel, part),
+        in_specs=[pl.BlockSpec(memory_space=pl.ANY)] * len(args),
+        out_specs=pl.BlockSpec(memory_space=pl.ANY),
+        out_shape=jax.ShapeDtypeStruct((chans, devices * CHUNKS * piece), piece_in.dtype),
+        scratch_shapes=moving(devices, chans, piece),
+        input_output_aliases={} if whole is None else {1: 0},
         name="join",
-    )(piece_in, *more)
+    )(*args)
 
 
 def mix(inputs, right, left, order, devices):
@@ -311,33 +339,46 @@
 
     for bit in range(log2(dp)):
         terms = halve(terms, "dp", bit, blocks * groups * (dp >> (bit + 1)), F32 if bit == 0 else BF16)
-    for bit in range(log2(mp)):
+    for bit in range(log2(NEAR)):
         terms = halve(terms, "mp", bit, mp >> (bit + 1), BF16)
-    return terms[0].reshape(blocks // mp, size // dp, width)
-
-
-def gathered_tables(*tables):
-    kinds = len(tables)
+    far = mp // NEAR
+    place = lax.axis_index("mp") // NEAR
+    parts = terms[0].reshape(far, blocks // mp * (size // dp), width)
+    total = lax.dynamic_index_in_dim(parts, place, 0, keepdims=False)
+    got = []
+    for step in range(1, far):
+        give = lax.dynamic_index_in_dim(parts, (place + step) % far, 0, keepdims=False)
+        got.append(lax.ppermute(give.astype(BF16), "mp", far_pairs(mp, step)))
+    for part in got:
+        total = total + part.astype(F32)
+    return total.reshape(blocks // mp, size // dp, width)
+
+
+def far_pairs(mp, step):
+    return [(i, (i // NEAR + step) % (mp // NEAR) * NEAR + i % NEAR) for i in range(mp)]
+
+
+def far_tables(*tables):
     share, size, width = tables[0].shape
     dp, mp = lax.axis_size("dp"), lax.axis_size("mp")
-    rows = size // dp
-    cut = jnp.stack(tables).reshape(kinds * share, dp, rows, width)
-    cut = lax.dynamic_index_in_dim(cut, lax.axis_index("dp"), 1, keepdims=False)
-
-    def double(full, name, bit, axis):
-        count = lax.axis_size(name)
-        got = lax.ppermute(full, name, [(i, i ^ (1 << bit)) for i in range(count)])
-        upper = (lax.axis_index(name) >> bit) & 1 == 1
-        return jnp.where(upper, jnp.stack([got, full], axis), jnp.stack([full, got], axis))
-
-    full = cut[None]
-    for bit in reversed(range(log2(mp))):
-        full = double(full, "mp", bit, 1).reshape(-1, kinds * share, rows, width)
-    full = full.reshape(mp * kinds * share, 1, rows, width)
-    for bit in reversed(range(log2(dp))):
-        full = double(full, "dp", bit, 2).reshape(mp * kinds * share, -1, rows, width)
-    full = full.reshape(mp, kinds, share, size, width)
-    return [full[:, kind].reshape(mp * share, size, width) for kind in range(kinds)]
+    cut = jnp.stack(tables).reshape(len(tables), share, dp, size // dp, width)
+    cut = lax.dynamic_index_in_dim(cut, lax.axis_index("dp"), 2, keepdims=False)
+    return [cut] + [lax.ppermute(cut, "mp", far_pairs(mp, k)) for k in range(1, mp // NEAR)]
+
+
+def all_tables(parts):
+    dp, mp = lax.axis_size("dp"), lax.axis_size("mp")
+    far, place = mp // NEAR, lax.axis_index("mp") // NEAR
+    kinds, share, rows, width = parts[0].shape
+    parts = jnp.stack(parts)
+    full = [
+        lax.dynamic_index_in_dim(parts, (place - z) % far, 0, keepdims=False) for z in range(far)
+    ]
+    planes = [[z * NEAR + n for n in range(NEAR)] for z in range(far)]
+    full = lax.all_gather(jnp.stack(full), "mp", axis=0, tiled=False, axis_index_groups=planes)
+    full = lax.all_gather(full, "dp", axis=0, tiled=False)
+    full = full.transpose(3, 2, 1, 4, 0, 5, 6)
+    return full.reshape(kinds, mp * share, dp * rows, width)
 
 
 def on_device(inputs, cotangent, mixer_right, mixer_left, dense_right, dense_left):
@@ -355,29 +396,29 @@
     def rows(part):
         return part.reshape(devices * chans, -1)
 
-    right_back, left_back = gathered_tables(
-        unfolded(dense_right, 2, NB), unfolded(unfolded(dense_left, 1, NB), 2, NB)
-    )
-    above = []
-    for part in range(CHUNKS):
-        sent = split(cotangent, devices, part)
-        if part:
-            sent, above[-1] = lax.optimization_barrier((sent, above[-1]))
-        else:
-            sent, cotangent, inputs, mixer_right, mixer_left = lax.optimization_barrier(
-                (sent, cotangent, inputs, mixer_right, mixer_left)
-            )
-        above.append(exchange(sent))
+    tables = far_tables(dense_right, dense_left)
+    sent = split(cotangent, devices, 0)
+    sent, tables, cotangent, inputs, mixer_right, mixer_left = lax.optimization_barrier(
+        (sent, tables, cotangent, inputs, mixer_right, mixer_left)
+    )
+    above = [exchange(sent)]
 
     eye = jnp.eye(LS, dtype=BF16)
     order = unfolded(eye, 0, LB)
     mix_right = unfolded(mixer_right, 2, LB).swapaxes(1, 2)
     mix_left_back = unfolded(unfolded(mixer_left, 1, LB), 2, LB)
     mix_left = mix_left_back.swapaxes(1, 2)
-    right, left = right_back.swapaxes(1, 2), left_back.swapaxes(1, 2)
-
     hidden, time_mixed, first_mix = mix(inputs, mix_right, mix_left, order, devices)
-    tables = (right, right_back, left, left_back)
+    for part in range(1, CHUNKS):
+        sent = split(cotangent, devices, part)
+        sent, above[-1], hidden, tables = lax.optimization_barrier(
+            (sent, above[-1], hidden, tables)
+        )
+        above.append(exchange(sent))
+    dense_right, dense_left = all_tables(tables)
+    right_back = unfolded(dense_right, 2, NB)
+    left_back = unfolded(unfolded(dense_left, 1, NB), 2, NB)
+    tables = (right_back.swapaxes(1, 2), right_back, left_back.swapaxes(1, 2), left_back)
     hidden, above, tables = lax.optimization_barrier((hidden, above, tables))
     arrived = []
     for part in hidden:

time: 964 us -> 899 us (0.933)
  waiting for transfers between devices: 407 us -> 301 us
  local copies, waits for them, and re-layouts: 50 us -> 90.4 us
  Pallas kernels: 293 us -> 269 us
  between operations: 1.33 us -> 14.6 us
  starting transfers between devices: 87.3 us -> 100 us
    all_gather x0 -> x2, waiting for transfers between devices: none -> 99.7 us  [the longest x1 65.7 us: all_tables(): lax.all_gather(jnp.stack(full), 'mp', axis=0, tiled=False, axis_index_gro...]
    ppermute x5 -> x15, waiting for transfers between devices: 137 us -> 56.4 us  [the longest x12 53.2 us: scatter_sum(): got.append(lax.ppermute(give.astype(BF16), 'mp', far_pairs(mp, step)))]
    all_to_all x7, waiting for transfers between devices: 119 us -> 42.8 us  [exchange(): return lax.all_to_all(part, 'mp', 0, 0, tiled=True).reshape(shape)]
    ppermute x20 -> x12, waiting for transfers between devices: 151 us -> 102 us  [halve(): lax.ppermute(give.astype(kind), name, [(i, i ^ 1 << bit) for i in range(c...]
    pallas_call x4, Pallas kernels: 40.5 us -> 15.8 us  [the longest x2 8.15 us: split(): call(functools.partial(split_kernel, part), in_specs=[pl.BlockSpec(memory...]
    ppermute x5 -> x15, starting transfers between devices: 2.91 us -> 19.1 us  [the longest x12 13.5 us: scatter_sum(): got.append(lax.ppermute(give.astype(BF16), 'mp', far_pairs(mp, step)))]
    another operation x1 -> x3, local copies, waits for them, and re-layouts: 0.18 us -> 16.1 us  [on_device(): dense_right, dense_left = all_tables(tables)]
    another operation x2 -> x3, local copies, waits for them, and re-layouts: 6.93 us -> 22.4 us  [unfolded(): cut = table.reshape(shape[:axis] + (blocks, fold) + shape[axis + 1:])]
  transfers between devices with their start and end apart: 32 -> 36, of which waited for: 24 -> 21; matrix products, arithmetic and copies ran while one was open for 7% -> 12% of each run, Pallas kernels for 28% -> 30%
where the time goes in v3:
time: 899 us; the launch traced here: 897 us
  waiting for transfers between devices  301 us (33%)
  Pallas kernels  269 us (30%)
  starting transfers between devices  100 us (11%)
  blocking collectives  100 us (11%)
  local copies, waits for them, and re-layouts  90.4 us (10%)
  other arithmetic  21.6 us (2%)
  between operations  14.6 us (2%)
    pallas_call x2, Pallas kernels, feature(): call(feature_kernel, grid=(piece // LANES,), in_specs=[strip, strip, tabl...  117 us
    ppermute x12, waiting for transfers between devices, halve(): lax.ppermute(give.astype(kind), name, [(i, i ^ 1 << bit) for i in range(c...  102 us
    all_to_all x1, blocking collectives, exchange(): return lax.all_to_all(part, 'mp', 0, 0, tiled=True).reshape(shape)  100 us
    pallas_call x1, Pallas kernels, back(): call(back_kernel, grid=(chans // LANES,), in_specs=[strip, strip, pl.Bloc...  75.5 us
    all_to_all x7, starting transfers between devices, exchange(): return lax.all_to_all(part, 'mp', 0, 0, tiled=True).reshape(shape)  73.8 us
    all_gather x1, waiting for transfers between devices, all_tables(): lax.all_gather(jnp.stack(full), 'mp', axis=0, tiled=False, axis_index_gro...  65.7 us
    pallas_call x1, Pallas kernels, mix(): call(mix_kernel, grid=(chans // LANES,), in_specs=[strip, table, table, f...  60.5 us
    ppermute x12, waiting for transfers between devices, scatter_sum(): got.append(lax.ppermute(give.astype(BF16), 'mp', far_pairs(mp, step)))  53.2 us
  transfers between devices with their start and end apart: 36, of which 21 were waited for; matrix products, arithmetic and copies ran while one was open for 12% of the time, Pallas kernels for 30%

profile of v3, /device:TPU:4, one launch (start us, length us, event | category | flops | bytes accessed | tf_op | source)
XLA Modules:
  0.0 896.7 jit_solution(15217200948737453017)
XLA Ops:
  20.9 8.2 all-to-all-start
  56.8 60.5 %mix.1 = (bf16[16,512,256]{2,1,0:T(8,128)(2,1)}, bf16[16,512,256]{2,1,0:T(8,128)(2,1)}, bf16[512,8192]{1,0:T(8,128)(2,1)}, bf16[64,128,512]{2,1,0:T(8,128)(2,1)}) custom-call(bf16[512,8192]{1,0:T(8,128)(2,1)} %bitcast.225, bf16[64,128,128]{2,1,0:T(8,128)(2,1)} %bitcast.235, bf16[64,128,128]{2,1,0:T(8,128)(2,1)} %bitcast.233, ...), custom_call_target="tpu_custom_call" | custom-call | tf_op jit(solution)/shard_map/mix/pallas_call | solution.py:253
  117.2 9.5 %all-to-all-start.1 = ((bf16[16,512,256]{2,1,0:T(8,128)(2,1)}), bf16[16,512,256]{2,1,0:T(8,128)(2,1)}, u32[]{:S(2)}, u32[]{:S(2)}) async-start(bf16[16,512,256]{2,1,0:T(8,128)(2,1)} %split.3), calls=%async_computation.1 | async-start | bytes 8388608 | tf_op jit(solution)/shard_map/all_to_all | solution.py:394
  128.0 65.7 %all-gather.5.cloned.1.call-done = bf16[16,2,4,64,128]{4,3,2,1,0:T(8,128)(2,1)} async-done(((bf16[4,2,4,64,128]{4,3,2,1,0:T(8,128)(2,1)}), bf16[16,2,4,64,128]{4,3,2,1,0:T(8,128)(2,1)}) %all-gather.5.cloned.1.call-update) | async-done | bytes 2097168 | tf_op jit(solution)/shard_map/all_gather | solution.py:378
  193.7 34.0 %all-gather.7.cloned.1.call-done = bf16[8,4,2,4,64,128]{5,4,3,2,1,0:T(8,128)(2,1)} async-done(((bf16[4,4,2,4,64,128]{5,4,3,2,1,0:T(8,128)(2,1)}), bf16[8,4,2,4,64,128]{5,4,3,2,1,0:T(8,128)(2,1)}) %all-gather.7.cloned.1.call-update) | async-done | bytes 4194320 | tf_op jit(solution)/shard_map/all_gather | solution.py:379
  240.4 7.8 reshape_reshape.13
  251.2 11.1 %copy.117 = bf16[1,4,4,4,2,64,128]{5,4,3,2,1,6,0:T(2,128)(2,1)} copy(bf16[1,4,4,4,2,64,128]{6,5,3,0,1,2,4:T(8,128)(2,1)} %get-tuple-element.145) | data formatting | bytes 4194304 | tf_op jit(solution)/shard_map/unstack | solution.py:418
  274.4 100.3 %all_to_all.40 = bf16[16,512,256]{2,1,0:T(8,128)(2,1)} all-to-all(bf16[16,512,256]{2,1,0:T(8,128)(2,1)} %get-tuple-element.85), channel_id=1, replica_groups=mesh['dp'=2,'mp'=16] {'mp'}, dimensions={0} | all-to-all | bytes 8388608 | tf_op jit(solution)/shard_map/all_to_all | solution.py:394
  386.9 58.5 %feature.3 = (bf16[8192,256]{1,0:T(8,128)(2,1)}, bf16[8192,256]{1,0:T(8,128)(2,1)}, f32[64,128,128]{2,1,0:T(8,128)}, f32[64,128,128]{2,1,0:T(8,128)}) custom-call(bf16[8192,256]{1,0:T(8,128)(2,1)} %bitcast.238, bf16[8192,256]{1,0:T(8,128)(2,1)} %bitcast.34.above_ref, bf16[64,128,128]{2,1,0:T(8,128)(2,1)} %bitcast.231, ...), custom_call_target="tpu_custom_call" | custom-call | tf_op jit(solution)/shard_map/feature/pallas_call | solution.py:275
  445.4 17.3 %all-to-all-done.3 = bf16[16,512,256]{2,1,0:T(8,128)(2,1)} async-done(((bf16[16,512,256]{2,1,0:T(8,128)(2,1)}), bf16[16,512,256]{2,1,0:T(8,128)(2,1)}, u32[]{:S(2)}, u32[]{:S(2)}) %all-to-all-start.3) | async-done | bytes 4194336 | tf_op jit(solution)/shard_map/all_to_all | solution.py:394
  462.8 14.5 %all-to-all-start.4 = ((bf16[16,512,256]{2,1,0:T(8,128)(2,1)}), bf16[16,512,256]{2,1,0:T(8,128)(2,1)}, u32[]{:S(2)}, u32[]{:S(2)}) async-start(bf16[16,512,256]{2,1,0:T(8,128)(2,1)} %bitcast.267), calls=%async_computation.4 | async-start | bytes 8388608 | tf_op jit(solution)/shard_map/all_to_all | solution.py:394
  477.2 58.5 %feature.2 = (bf16[8192,256]{1,0:T(8,128)(2,1)}, bf16[8192,256]{1,0:T(8,128)(2,1)}, f32[64,128,128]{2,1,0:T(8,128)}, f32[64,128,128]{2,1,0:T(8,128)}) custom-call(bf16[8192,256]{1,0:T(8,128)(2,1)} %bitcast.30.hidden_ref, bf16[8192,256]{1,0:T(8,128)(2,1)} %bitcast.31.above_ref, bf16[64,128,128]{2,1,0:T(8,128)(2,1)} %bitcast.232, ...), custom_call_target="tpu_custom_call" | custom-call | tf_op jit(solution)/shard_map/feature/pallas_call | solution.py:275
  535.7 24.3 %all-to-all-done.4.refs_0_ = bf16[16,512,256]{2,1,0:T(8,128)(2,1)} async-done(((bf16[16,512,256]{2,1,0:T(8,128)(2,1)}), bf16[16,512,256]{2,1,0:T(8,128)(2,1)}, u32[]{:S(2)}, u32[]{:S(2)}) %all-to-all-start.4) | async-done | bytes 4194336 | tf_op jit(solution)/shard_map/all_to_all | solution.py:394
  560.0 15.0 %all-to-all-start.5 = ((bf16[16,512,256]{2,1,0:T(8,128)(2,1)}), bf16[16,512,256]{2,1,0:T(8,128)(2,1)}, u32[]{:S(2)}, u32[]{:S(2)}) async-start(bf16[16,512,256]{2,1,0:T(8,128)(2,1)} %bitcast.258), calls=%async_computation.5 | async-start | bytes 8388608 | tf_op jit(solution)/shard_map/all_to_all | solution.py:394
  592.8 8.4 collective-permute-done.10
  602.9 31.4 %collective-permute-done.4 = bf16[8,256,128]{2,1,0:T(8,128)(2,1)} collective-permute-done((bf16[8,256,128]{2,1,0:T(8,128)(2,1)S(1)}, bf16[8,256,128]{2,1,0:T(8,128)(2,1)}, u32[]{:S(2)}, u32[]{:S(2)}) %collective-permute-start.4) | collective-permute-done | bytes 524320 | tf_op jit(solution)/shard_map/ppermute | solution.py:337
  639.6 9.8 %collective-permute-done.5 = bf16[4,256,128]{2,1,0:T(8,128)(2,1)S(1)} collective-permute-done((bf16[4,256,128]{2,1,0:T(8,128)(2,1)S(1)}, bf16[4,256,128]{2,1,0:T(8,128)(2,1)S(1)}, u32[]{:S(2)}, u32[]{:S(2)}) %collective-permute-start.5) | collective-permute-done | bytes 262176 | tf_op jit(solution)/shard_map/ppermute | solution.py:337
  653.4 23.2 %collective-permute-done.13 = bf16[256,128]{1,0:T(8,128)(2,1)S(1)} collective-permute-done((bf16[256,128]{1,0:T(8,128)(2,1)S(1)}, bf16[256,128]{1,0:T(8,128)(2,1)S(1)}, u32[]{:S(2)}, u32[]{:S(2)}) %collective-permute-start.13) | collective-permute-done | bytes 65568 | tf_op jit(solution)/shard_map/ppermute | solution.py:351
  689.2 75.5 %back.1 = (bf16[512,8192]{1,0:T(8,128)(2,1)}, f32[64,128,128]{2,1,0:T(8,128)}, f32[64,128,128]{2,1,0:T(8,128)}) custom-call(bf16[512,8192]{1,0:T(8,128)(2,1)} %bitcast.226, bf16[512,8192]{1,0:T(8,128)(2,1)} %get-tuple-element.66.time_ref, bf16[64,128,512]{2,1,0:T(8,128)(2,1)} %get-tuple-element.67.first_ref, bf16[64,128,128]{2,1,0:T(8,128)(2,1)} %bitcast.236, ...), custom_call_target="tpu_custom_call" | custom-call | tf_op jit(solution)/shard_map/back/pallas_call | solution.py:294
  765.9 14.9 %all-to-all-start.7 = ((bf16[16,512,256]{2,1,0:T(8,128)(2,1)}), bf16[16,512,256]{2,1,0:T(8,128)(2,1)}, u32[]{:S(2)}, u32[]{:S(2)}) async-start(bf16[16,512,256]{2,1,0:T(8,128)(2,1)} %bitcast.256), calls=%async_computation.7 | async-start | bytes 8388608 | tf_op jit(solution)/shard_map/all_to_all | solution.py:394
  799.0 9.2 %collective-permute-done.22 = bf16[8,256,128]{2,1,0:T(8,128)(2,1)} collective-permute-done((bf16[8,256,128]{2,1,0:T(8,128)(2,1)S(1)}, bf16[8,256,128]{2,1,0:T(8,128)(2,1)}, u32[]{:S(2)}, u32[]{:S(2)}) %collective-permute-start.22) | collective-permute-done | bytes 524320 | tf_op jit(solution)/shard_map/ppermute | solution.py:337
  809.9 30.3 %collective-permute-done.16 = bf16[8,256,128]{2,1,0:T(8,128)(2,1)} collective-permute-done((bf16[8,256,128]{2,1,0:T(8,128)(2,1)}, bf16[8,256,128]{2,1,0:T(8,128)(2,1)}, u32[]{:S(2)}, u32[]{:S(2)}) %collective-permute-start.16) | collective-permute-done | bytes 524320 | tf_op jit(solution)/shard_map/ppermute | solution.py:337
  845.4 8.5 collective-permute-done.17
  857.8 24.5 %collective-permute-done.25 = bf16[256,128]{1,0:T(8,128)(2,1)S(1)} collective-permute-done((bf16[256,128]{1,0:T(8,128)(2,1)S(1)}, bf16[256,128]{1,0:T(8,128)(2,1)S(1)}, u32[]{:S(2)}, u32[]{:S(2)}) %collective-permute-start.25) | collective-permute-done | bytes 65568 | tf_op jit(solution)/shard_map/ppermute | solution.py:351
  (152 shorter events, 161.3 us)
Async XLA Ops:
  20.9 96.3 %all-to-all-start = ((bf16[16,512,256]{2,1,0:T(8,128)(2,1)}), bf16[16,512,256]{2,1,0:T(8,128)(2,1)}, u32[]{:S(2)}, u32[]{:S(2)}) async-start(bf16[16,512,256]{2,1,0:T(8,128)(2,1)} %split.2), calls=%async_computation | async-start | bytes 8388608 | tf_op jit(solution)/shard_map/all_to_all | solution.py:394
  117.2 157.1 %all-to-all-start.1 = ((bf16[16,512,256]{2,1,0:T(8,128)(2,1)}), bf16[16,512,256]{2,1,0:T(8,128)(2,1)}, u32[]{:S(2)}, u32[]{:S(2)}) async-start(bf16[16,512,256]{2,1,0:T(8,128)(2,1)} %split.3), calls=%async_computation.1 | async-start | bytes 8388608 | tf_op jit(solution)/shard_map/all_to_all | solution.py:394
  126.7 67.0 %all-gather.5.cloned.1.call-start = ((), (), s32[]{:S(2)}) async-start(), calls=%async_computation.8 | async-start | bytes 2621440 | tf_op jit(solution)/shard_map/all_gather | solution.py:378
  127.8 100.0 %all-gather.7.cloned.1.call-start = ((), (), s32[]{:S(2)}) async-start(), calls=%async_computation.9 | async-start | bytes 6291456 | tf_op jit(solution)/shard_map/all_gather | solution.py:379
  374.7 88.1 %all-to-all-start.3 = ((bf16[16,512,256]{2,1,0:T(8,128)(2,1)}), bf16[16,512,256]{2,1,0:T(8,128)(2,1)}, u32[]{:S(2)}, u32[]{:S(2)}) async-start(bf16[16,512,256]{2,1,0:T(8,128)(2,1)} %get-tuple-element.86), calls=%async_computation.3 | async-start | bytes 8388608 | tf_op jit(solution)/shard_map/all_to_all | solution.py:394
  462.8 97.3 %all-to-all-start.4 = ((bf16[16,512,256]{2,1,0:T(8,128)(2,1)}), bf16[16,512,256]{2,1,0:T(8,128)(2,1)}, u32[]{:S(2)}, u32[]{:S(2)}) async-start(bf16[16,512,256]{2,1,0:T(8,128)(2,1)} %bitcast.267), calls=%async_computation.4 | async-start | bytes 8388608 | tf_op jit(solution)/shard_map/all_to_all | solution.py:394
  560.0 119.0 %all-to-all-start.5 = ((bf16[16,512,256]{2,1,0:T(8,128)(2,1)}), bf16[16,512,256]{2,1,0:T(8,128)(2,1)}, u32[]{:S(2)}, u32[]{:S(2)}) async-start(bf16[16,512,256]{2,1,0:T(8,128)(2,1)} %bitcast.258), calls=%async_computation.5 | async-start | bytes 8388608 | tf_op jit(solution)/shard_map/all_to_all | solution.py:394
  591.4 42.9 %collective-permute-start.4 = (bf16[8,256,128]{2,1,0:T(8,128)(2,1)S(1)}, bf16[8,256,128]{2,1,0:T(8,128)(2,1)}, u32[]{:S(2)}, u32[]{:S(2)}) collective-permute-start(bf16[8,256,128]{2,1,0:T(8,128)(2,1)S(1)} %fusion.6), channel_id=1, source_target_pairs={{0,1},{1,0},{2,3},{3,2},{4,5},{5,4},{6,7},{7,6},{8,9},{9,8},{10,11... | collective-permute-start | bytes 1572872 | tf_op jit(solution)/shard_map/ppermute | solution.py:337
  602.4 33.2 %collective-permute-start.11 = (bf16[4,256,128]{2,1,0:T(8,128)(2,1)S(1)}, bf16[4,256,128]{2,1,0:T(8,128)(2,1)S(1)}, u32[]{:S(2)}, u32[]{:S(2)}) collective-permute-start(bf16[4,256,128]{2,1,0:T(8,128)(2,1)S(1)} %fusion.11), channel_id=1, source_target_pairs={{0,2},{1,3},{2,0},{3,1},{4,6},{5,7},{6,4},{7,5},{8,10},{9,11},{10,... | collective-permute-start | bytes 786440 | tf_op jit(solution)/shard_map/ppermute | solution.py:337
  636.9 39.7 %collective-permute-start.13 = (bf16[256,128]{1,0:T(8,128)(2,1)S(1)}, bf16[256,128]{1,0:T(8,128)(2,1)S(1)}, u32[]{:S(2)}, u32[]{:S(2)}) collective-permute-start(bf16[256,128]{1,0:T(8,128)(2,1)S(1)} %get-tuple-element.154), channel_id=1, source_target_pairs={{0,8},{1,9},{2,10},{3,11},{4,12},{5,13},{6,14},{7,15},{8,0},{9,1},... | collective-permute-start | bytes 196616 | tf_op jit(solution)/shard_map/ppermute | solution.py:351
  636.9 39.7 %collective-permute-start.14 = (bf16[256,128]{1,0:T(8,128)(2,1)S(1)}, bf16[256,128]{1,0:T(8,128)(2,1)S(1)}, u32[]{:S(2)}, u32[]{:S(2)}) collective-permute-start(bf16[256,128]{1,0:T(8,128)(2,1)S(1)} %get-tuple-element.153), channel_id=1, source_target_pairs={{0,12},{1,13},{2,14},{3,15},{4,0},{5,1},{6,2},{7,3},{8,4},{9,5},{1... | collective-permute-start | bytes 196616 | tf_op jit(solution)/shard_map/ppermute | solution.py:351
  649.5 27.1 %collective-permute-start.6 = (bf16[256,128]{1,0:T(8,128)(2,1)S(1)}, bf16[256,128]{1,0:T(8,128)(2,1)S(1)}, u32[]{:S(2)}, u32[]{:S(2)}) collective-permute-start(bf16[256,128]{1,0:T(8,128)(2,1)S(1)} %get-tuple-element.155), channel_id=1, source_target_pairs={{0,4},{1,5},{2,6},{3,7},{4,8},{5,9},{6,10},{7,11},{8,12},{9,13},{1... | collective-permute-start | bytes 196616 | tf_op jit(solution)/shard_map/ppermute | solution.py:351
  649.9 29.2 %collective-permute-start.7 = (bf16[256,128]{1,0:T(8,128)(2,1)S(1)}, bf16[256,128]{1,0:T(8,128)(2,1)S(1)}, u32[]{:S(2)}, u32[]{:S(2)}) collective-permute-start(bf16[256,128]{1,0:T(8,128)(2,1)S(1)} %get-tuple-element.157), channel_id=1, source_target_pairs={{0,8},{1,9},{2,10},{3,11},{4,12},{5,13},{6,14},{7,15},{8,0},{9,1},... | collective-permute-start | bytes 196616 | tf_op jit(solution)/shard_map/ppermute | solution.py:351
  650.0 29.0 %collective-permute-start.8 = (bf16[256,128]{1,0:T(8,128)(2,1)S(1)}, bf16[256,128]{1,0:T(8,128)(2,1)S(1)}, u32[]{:S(2)}, u32[]{:S(2)}) collective-permute-start(bf16[256,128]{1,0:T(8,128)(2,1)S(1)} %get-tuple-element.156), channel_id=1, source_target_pairs={{0,12},{1,13},{2,14},{3,15},{4,0},{5,1},{6,2},{7,3},{8,4},{9,5},{1... | collective-permute-start | bytes 196616 | tf_op jit(solution)/shard_map/ppermute | solution.py:351
  679.1 86.8 %all-to-all-start.6 = ((bf16[16,512,256]{2,1,0:T(8,128)(2,1)}), bf16[16,512,256]{2,1,0:T(8,128)(2,1)}, u32[]{:S(2)}, u32[]{:S(2)}) async-start(bf16[16,512,256]{2,1,0:T(8,128)(2,1)} %bitcast.257), calls=%async_computation.6 | async-start | bytes 8388608 | tf_op jit(solution)/shard_map/all_to_all | solution.py:394
  765.9 120.1 %all-to-all-start.7 = ((bf16[16,512,256]{2,1,0:T(8,128)(2,1)}), bf16[16,512,256]{2,1,0:T(8,128)(2,1)}, u32[]{:S(2)}, u32[]{:S(2)}) async-start(bf16[16,512,256]{2,1,0:T(8,128)(2,1)} %bitcast.256), calls=%async_computation.7 | async-start | bytes 8388608 | tf_op jit(solution)/shard_map/all_to_all | solution.py:394
  787.6 20.7 %collective-permute-start.22 = (bf16[8,256,128]{2,1,0:T(8,128)(2,1)S(1)}, bf16[8,256,128]{2,1,0:T(8,128)(2,1)}, u32[]{:S(2)}, u32[]{:S(2)}) collective-permute-start(bf16[8,256,128]{2,1,0:T(8,128)(2,1)S(1)} %fusion.9), channel_id=1, source_target_pairs={{0,1},{1,0},{2,3},{3,2},{4,5},{5,4},{6,7},{7,6},{8,9},{9,8},{10,11... | collective-permute-start | bytes 1572872 | tf_op jit(solution)/shard_map/ppermute | solution.py:337
  791.2 48.9 %collective-permute-start.16 = (bf16[8,256,128]{2,1,0:T(8,128)(2,1)}, bf16[8,256,128]{2,1,0:T(8,128)(2,1)}, u32[]{:S(2)}, u32[]{:S(2)}) collective-permute-start(bf16[8,256,128]{2,1,0:T(8,128)(2,1)} %fusion.8), channel_id=1, source_target_pairs={{0,1},{1,0},{2,3},{3,2},{4,5},{5,4},{6,7},{7,6},{8,9},{9,8},{10,11... | collective-permute-start | bytes 1572872 | tf_op jit(solution)/shard_map/ppermute | solution.py:337
  809.8 31.6 %collective-permute-start.23 = (bf16[4,256,128]{2,1,0:T(8,128)(2,1)S(1)}, bf16[4,256,128]{2,1,0:T(8,128)(2,1)S(1)}, u32[]{:S(2)}, u32[]{:S(2)}) collective-permute-start(bf16[4,256,128]{2,1,0:T(8,128)(2,1)S(1)} %fusion.13), channel_id=1, source_target_pairs={{0,2},{1,3},{2,0},{3,1},{4,6},{5,7},{6,4},{7,5},{8,10},{9,11},{10,... | collective-permute-start | bytes 786440 | tf_op jit(solution)/shard_map/ppermute | solution.py:337
  841.6 40.8 %collective-permute-start.25 = (bf16[256,128]{1,0:T(8,128)(2,1)S(1)}, bf16[256,128]{1,0:T(8,128)(2,1)S(1)}, u32[]{:S(2)}, u32[]{:S(2)}) collective-permute-start(bf16[256,128]{1,0:T(8,128)(2,1)S(1)} %get-tuple-element.148), channel_id=1, source_target_pairs={{0,8},{1,9},{2,10},{3,11},{4,12},{5,13},{6,14},{7,15},{8,0},{9,1},... | collective-permute-start | bytes 196616 | tf_op jit(solution)/shard_map/ppermute | solution.py:351
  841.7 40.7 %collective-permute-start.26 = (bf16[256,128]{1,0:T(8,128)(2,1)S(1)}, bf16[256,128]{1,0:T(8,128)(2,1)S(1)}, u32[]{:S(2)}, u32[]{:S(2)}) collective-permute-start(bf16[256,128]{1,0:T(8,128)(2,1)S(1)} %get-tuple-element.147), channel_id=1, source_target_pairs={{0,12},{1,13},{2,14},{3,15},{4,0},{5,1},{6,2},{7,3},{8,4},{9,5},{1... | collective-permute-start | bytes 196616 | tf_op jit(solution)/shard_map/ppermute | solution.py:351
  854.0 29.8 %collective-permute-start.18 = (bf16[256,128]{1,0:T(8,128)(2,1)S(1)}, bf16[256,128]{1,0:T(8,128)(2,1)S(1)}, u32[]{:S(2)}, u32[]{:S(2)}) collective-permute-start(bf16[256,128]{1,0:T(8,128)(2,1)S(1)} %get-tuple-element.149), channel_id=1, source_target_pairs={{0,4},{1,5},{2,6},{3,7},{4,8},{5,9},{6,10},{7,11},{8,12},{9,13},{1... | collective-permute-start | bytes 196616 | tf_op jit(solution)/shard_map/ppermute | solution.py:351
  854.0 30.8 %collective-permute-start.19 = (bf16[256,128]{1,0:T(8,128)(2,1)S(1)}, bf16[256,128]{1,0:T(8,128)(2,1)S(1)}, u32[]{:S(2)}, u32[]{:S(2)}) collective-permute-start(bf16[256,128]{1,0:T(8,128)(2,1)S(1)} %get-tuple-element.151), channel_id=1, source_target_pairs={{0,8},{1,9},{2,10},{3,11},{4,12},{5,13},{6,14},{7,15},{8,0},{9,1},... | collective-permute-start | bytes 196616 | tf_op jit(solution)/shard_map/ppermute | solution.py:351
  855.9 28.9 %collective-permute-start.20 = (bf16[256,128]{1,0:T(8,128)(2,1)S(1)}, bf16[256,128]{1,0:T(8,128)(2,1)S(1)}, u32[]{:S(2)}, u32[]{:S(2)}) collective-permute-start(bf16[256,128]{1,0:T(8,128)(2,1)S(1)} %get-tuple-element.150), channel_id=1, source_target_pairs={{0,12},{1,13},{2,14},{3,15},{4,0},{5,1},{6,2},{7,3},{8,4},{9,5},{1... | collective-permute-start | bytes 196616 | tf_op jit(solution)/shard_map/ppermute | solution.py:351
  (23 other events, 335.7 us)
Sparse Core Ops, SparseCore 0:
  129.4 64.2 all-gather.4
  195.2 32.4 all-gather.6

commit v4 on v3

--- a/solution.py
+++ b/solution.py
@@ -339,19 +339,9 @@
 
     for bit in range(log2(dp)):
         terms = halve(terms, "dp", bit, blocks * groups * (dp >> (bit + 1)), F32 if bit == 0 else BF16)
-    for bit in range(log2(NEAR)):
+    for bit in range(log2(mp)):
         terms = halve(terms, "mp", bit, mp >> (bit + 1), BF16)
-    far = mp // NEAR
-    place = lax.axis_index("mp") // NEAR
-    parts = terms[0].reshape(far, blocks // mp * (size // dp), width)
-    total = lax.dynamic_index_in_dim(parts, place, 0, keepdims=False)
-    got = []
-    for step in range(1, far):
-        give = lax.dynamic_index_in_dim(parts, (place + step) % far, 0, keepdims=False)
-        got.append(lax.ppermute(give.astype(BF16), "mp", far_pairs(mp, step)))
-    for part in got:
-        total = total + part.astype(F32)
-    return total.reshape(blocks // mp, size // dp, width)
+    return terms[0].reshape(blocks // mp, size // dp, width)
 
 
 def far_pairs(mp, step):
@@ -366,19 +356,22 @@
     return [cut] + [lax.ppermute(cut, "mp", far_pairs(mp, k)) for k in range(1, mp // NEAR)]
 
 
-def all_tables(parts):
-    dp, mp = lax.axis_size("dp"), lax.axis_size("mp")
+def near_tables(parts):
+    mp = lax.axis_size("mp")
     far, place = mp // NEAR, lax.axis_index("mp") // NEAR
-    kinds, share, rows, width = parts[0].shape
     parts = jnp.stack(parts)
     full = [
         lax.dynamic_index_in_dim(parts, (place - z) % far, 0, keepdims=False) for z in range(far)
     ]
     planes = [[z * NEAR + n for n in range(NEAR)] for z in range(far)]
-    full = lax.all_gather(jnp.stack(full), "mp", axis=0, tiled=False, axis_index_groups=planes)
+    return lax.all_gather(jnp.stack(full), "mp", axis=0, tiled=False, axis_index_groups=planes)
+
+
+def all_tables(full):
     full = lax.all_gather(full, "dp", axis=0, tiled=False)
+    dp, near, far, kinds, share, rows, width = full.shape
     full = full.transpose(3, 2, 1, 4, 0, 5, 6)
-    return full.reshape(kinds, mp * share, dp * rows, width)
+    return full.reshape(kinds, near * far * share, dp * rows, width)
 
 
 def on_device(inputs, cotangent, mixer_right, mixer_left, dense_right, dense_left):
@@ -415,15 +408,15 @@
             (sent, above[-1], hidden, tables)
         )
         above.append(exchange(sent))
+    hidden, above, tables = lax.optimization_barrier((hidden, above, near_tables(tables)))
     dense_right, dense_left = all_tables(tables)
     right_back = unfolded(dense_right, 2, NB)
     left_back = unfolded(unfolded(dense_left, 1, NB), 2, NB)
     tables = (right_back.swapaxes(1, 2), right_back, left_back.swapaxes(1, 2), left_back)
-    hidden, above, tables = lax.optimization_barrier((hidden, above, tables))
     arrived = []
     for part in hidden:
         if arrived:
-            part, arrived[-1] = lax.optimization_barrier((part, arrived[-1]))
+            part, arrived[-1], tables = lax.optimization_barrier((part, arrived[-1], tables))
         arrived.append(exchange(part))
     outs, grads, rights, lefts = [], [], [], []
     for part in range(CHUNKS):

time: 899 us -> 832 us (0.925)
  blocking collectives: 100 us -> 0 us
  waiting for transfers between devices: 301 us -> 323 us
  starting transfers between devices: 100 us -> 111 us
    all_to_all x1 -> x0, blocking collectives: 100 us -> none  [exchange(): return lax.all_to_all(part, 'mp', 0, 0, tiled=True).reshape(shape)]
    ppermute x12 -> x20, waiting for transfers between devices: 102 us -> 158 us  [halve(): lax.ppermute(give.astype(kind), name, [(i, i ^ 1 << bit) for i in range(c...]
    ppermute x12 -> x0, waiting for transfers between devices: 53.2 us -> none  [scatter_sum(): got.append(lax.ppermute(give.astype(BF16), 'mp', far_pairs(mp, step)))]
    all_to_all x7 -> x8, waiting for transfers between devices: 42.8 us -> 79.4 us  [exchange(): return lax.all_to_all(part, 'mp', 0, 0, tiled=True).reshape(shape)]
    all_to_all x7 -> x8, starting transfers between devices: 73.8 us -> 96.7 us  [exchange(): return lax.all_to_all(part, 'mp', 0, 0, tiled=True).reshape(shape)]
    all_gather x1, waiting for transfers between devices: 34 us -> 16.4 us  [all_tables(): full = lax.all_gather(full, 'dp', axis=0, tiled=False)]
    ppermute x12 -> x0, starting transfers between devices: 13.5 us -> none  [scatter_sum(): got.append(lax.ppermute(give.astype(BF16), 'mp', far_pairs(mp, step)))]
  transfers between devices with their start and end apart: 36 -> 33, of which waited for: 21 -> 24; matrix products, arithmetic and copies ran while one was open for 12% -> 13% of each run, Pallas kernels for 30% -> 32%
where the time goes in v4:
time: 832 us; the launch traced here: 830 us
  waiting for transfers between devices  323 us (39%)
  Pallas kernels  269 us (32%)
  starting transfers between devices  111 us (13%)
  local copies, waits for them, and re-layouts  90.5 us (11%)
  other arithmetic  21.6 us (3%)
  between operations  14.8 us (2%)
    ppermute x20, waiting for transfers between devices, halve(): lax.ppermute(give.astype(kind), name, [(i, i ^ 1 << bit) for i in range(c...  158 us
    pallas_call x2, Pallas kernels, feature(): call(feature_kernel, grid=(piece // LANES,), in_specs=[strip, strip, tabl...  117 us
    all_to_all x8, starting transfers between devices, exchange(): return lax.all_to_all(part, 'mp', 0, 0, tiled=True).reshape(shape)  96.7 us
    all_to_all x8, waiting for transfers between devices, exchange(): return lax.all_to_all(part, 'mp', 0, 0, tiled=True).reshape(shape)  79.4 us
    pallas_call x1, Pallas kernels, back(): call(back_kernel, grid=(chans // LANES,), in_specs=[strip, strip, pl.Bloc...  75.6 us
    all_gather x1, waiting for transfers between devices, near_tables(): lax.all_gather(jnp.stack(full), 'mp', axis=0, tiled=False, axis_index_gro...  65.8 us
    pallas_call x1, Pallas kernels, mix(): call(mix_kernel, grid=(chans // LANES,), in_specs=[strip, table, table, f...  60.5 us
    another operation x3, local copies, waits for them, and re-layouts, unfolded(): cut = table.reshape(shape[:axis] + (blocks, fold) + shape[axis + 1:])  22.4 us
  transfers between devices with their start and end apart: 33, of which 24 were waited for; matrix products, arithmetic and copies ran while one was open for 13% of the time, Pallas kernels for 32%

profile of v4, /device:TPU:4, one launch (start us, length us, event | category | flops | bytes accessed | tf_op | source)
XLA Modules:
  0.0 829.9 jit_solution(11455372020943064500)
XLA Ops:
  56.8 60.5 %mix.1 = (bf16[16,512,256]{2,1,0:T(8,128)(2,1)}, bf16[16,512,256]{2,1,0:T(8,128)(2,1)}, bf16[512,8192]{1,0:T(8,128)(2,1)}, bf16[64,128,512]{2,1,0:T(8,128)(2,1)}) custom-call(bf16[512,8192]{1,0:T(8,128)(2,1)} %bitcast.193, bf16[64,128,128]{2,1,0:T(8,128)(2,1)} %bitcast.203, bf16[64,128,128]{2,1,0:T(8,128)(2,1)} %bitcast.201, ...), custom_call_target="tpu_custom_call" | custom-call | tf_op jit(solution)/shard_map/mix/pallas_call | solution.py:253
  117.3 9.5 %all-to-all-start.1 = ((bf16[16,512,256]{2,1,0:T(8,128)(2,1)}), bf16[16,512,256]{2,1,0:T(8,128)(2,1)}, u32[]{:S(2)}, u32[]{:S(2)}) async-start(bf16[16,512,256]{2,1,0:T(8,128)(2,1)} %split.3), calls=%async_computation.1 | async-start | bytes 8388608 | tf_op jit(solution)/shard_map/all_to_all | solution.py:387
  127.9 65.8 %all-gather.5.cloned.1.call-done = bf16[16,2,4,64,128]{4,3,2,1,0:T(8,128)(2,1)} async-done(((bf16[4,2,4,64,128]{4,3,2,1,0:T(8,128)(2,1)}), bf16[16,2,4,64,128]{4,3,2,1,0:T(8,128)(2,1)}) %all-gather.5.cloned.1.call-update) | async-done | bytes 2097168 | tf_op jit(solution)/shard_map/all_gather | solution.py:367
  193.7 15.8 %all-to-all-done.1 = bf16[16,512,256]{2,1,0:T(8,128)(2,1)} async-done(((bf16[16,512,256]{2,1,0:T(8,128)(2,1)}), bf16[16,512,256]{2,1,0:T(8,128)(2,1)}, u32[]{:S(2)}, u32[]{:S(2)}) %all-to-all-start.1) | async-done | bytes 4194336 | tf_op jit(solution)/shard_map/all_to_all | solution.py:387
  209.5 15.1 %all-to-all-start.2 = ((bf16[16,512,256]{2,1,0:T(8,128)(2,1)}), bf16[16,512,256]{2,1,0:T(8,128)(2,1)}, u32[]{:S(2)}, u32[]{:S(2)}) async-start(bf16[16,512,256]{2,1,0:T(8,128)(2,1)} %get-tuple-element.86), calls=%async_computation.2 | async-start | bytes 8388608 | tf_op jit(solution)/shard_map/all_to_all | solution.py:387
  225.3 16.4 %all-gather.7.cloned.1.call-done = bf16[8,4,2,4,64,128]{5,4,3,2,1,0:T(8,128)(2,1)} async-done(((bf16[4,4,2,4,64,128]{5,4,3,2,1,0:T(8,128)(2,1)}), bf16[8,4,2,4,64,128]{5,4,3,2,1,0:T(8,128)(2,1)}) %all-gather.7.cloned.1.call-update) | async-done | bytes 4194320 | tf_op jit(solution)/shard_map/all_gather | solution.py:371
  265.2 11.1 %copy.146 = bf16[1,4,4,4,2,64,128]{5,4,3,2,1,6,0:T(2,128)(2,1)} copy(bf16[1,4,4,4,2,64,128]{6,5,3,0,1,2,4:T(8,128)(2,1)} %get-tuple-element.153) | data formatting | bytes 4194304 | tf_op jit(solution)/shard_map/unstack | solution.py:412
  288.4 19.0 %all-to-all-done.2 = bf16[16,512,256]{2,1,0:T(8,128)(2,1)} async-done(((bf16[16,512,256]{2,1,0:T(8,128)(2,1)}), bf16[16,512,256]{2,1,0:T(8,128)(2,1)}, u32[]{:S(2)}, u32[]{:S(2)}) %all-to-all-start.2) | async-done | bytes 4194336 | tf_op jit(solution)/shard_map/all_to_all | solution.py:387
  307.4 15.0 %all-to-all-start.3 = ((bf16[16,512,256]{2,1,0:T(8,128)(2,1)}), bf16[16,512,256]{2,1,0:T(8,128)(2,1)}, u32[]{:S(2)}, u32[]{:S(2)}) async-start(bf16[16,512,256]{2,1,0:T(8,128)(2,1)} %get-tuple-element.88), calls=%async_computation.3 | async-start | bytes 8388608 | tf_op jit(solution)/shard_map/all_to_all | solution.py:387
  329.3 58.5 %feature.3 = (bf16[8192,256]{1,0:T(8,128)(2,1)}, bf16[8192,256]{1,0:T(8,128)(2,1)}, f32[64,128,128]{2,1,0:T(8,128)}, f32[64,128,128]{2,1,0:T(8,128)}) custom-call(bf16[8192,256]{1,0:T(8,128)(2,1)} %bitcast.33.hidden_ref, bf16[8192,256]{1,0:T(8,128)(2,1)} %bitcast.34.above_ref, bf16[64,128,128]{2,1,0:T(8,128)(2,1)} %bitcast.199, ...), custom_call_target="tpu_custom_call" | custom-call | tf_op jit(solution)/shard_map/feature/pallas_call | solution.py:275
  387.8 17.4 %all-to-all-done.3 = bf16[16,512,256]{2,1,0:T(8,128)(2,1)} async-done(((bf16[16,512,256]{2,1,0:T(8,128)(2,1)}), bf16[16,512,256]{2,1,0:T(8,128)(2,1)}, u32[]{:S(2)}, u32[]{:S(2)}) %all-to-all-start.3) | async-done | bytes 4194336 | tf_op jit(solution)/shard_map/all_to_all | solution.py:387
  405.1 15.0 %all-to-all-start.4 = ((bf16[16,512,256]{2,1,0:T(8,128)(2,1)}), bf16[16,512,256]{2,1,0:T(8,128)(2,1)}, u32[]{:S(2)}, u32[]{:S(2)}) async-start(bf16[16,512,256]{2,1,0:T(8,128)(2,1)} %bitcast.234), calls=%async_computation.4 | async-start | bytes 8388608 | tf_op jit(solution)/shard_map/all_to_all | solution.py:387
  420.1 58.5 %feature.2 = (bf16[8192,256]{1,0:T(8,128)(2,1)}, bf16[8192,256]{1,0:T(8,128)(2,1)}, f32[64,128,128]{2,1,0:T(8,128)}, f32[64,128,128]{2,1,0:T(8,128)}) custom-call(bf16[8192,256]{1,0:T(8,128)(2,1)} %bitcast.30.hidden_ref, bf16[8192,256]{1,0:T(8,128)(2,1)} %bitcast.31.above_ref, bf16[64,128,128]{2,1,0:T(8,128)(2,1)} %bitcast.200, ...), custom_call_target="tpu_custom_call" | custom-call | tf_op jit(solution)/shard_map/feature/pallas_call | solution.py:275
  478.6 24.3 %all-to-all-done.4.refs_0_ = bf16[16,512,256]{2,1,0:T(8,128)(2,1)} async-done(((bf16[16,512,256]{2,1,0:T(8,128)(2,1)}), bf16[16,512,256]{2,1,0:T(8,128)(2,1)}, u32[]{:S(2)}, u32[]{:S(2)}) %all-to-all-start.4) | async-done | bytes 4194336 | tf_op jit(solution)/shard_map/all_to_all | solution.py:387
  502.9 15.0 %all-to-all-start.5 = ((bf16[16,512,256]{2,1,0:T(8,128)(2,1)}), bf16[16,512,256]{2,1,0:T(8,128)(2,1)}, u32[]{:S(2)}, u32[]{:S(2)}) async-start(bf16[16,512,256]{2,1,0:T(8,128)(2,1)} %bitcast.225), calls=%async_computation.5 | async-start | bytes 8388608 | tf_op jit(solution)/shard_map/all_to_all | solution.py:387
  545.8 31.4 %collective-permute-done.4 = bf16[8,256,128]{2,1,0:T(8,128)(2,1)} collective-permute-done((bf16[8,256,128]{2,1,0:T(8,128)(2,1)S(1)}, bf16[8,256,128]{2,1,0:T(8,128)(2,1)}, u32[]{:S(2)}, u32[]{:S(2)}) %collective-permute-start.4) | collective-permute-done | bytes 524320 | tf_op jit(solution)/shard_map/ppermute | solution.py:337
  579.8 15.5 %collective-permute-done.5 = bf16[4,256,128]{2,1,0:T(8,128)(2,1)S(1)} collective-permute-done((bf16[4,256,128]{2,1,0:T(8,128)(2,1)S(1)}, bf16[4,256,128]{2,1,0:T(8,128)(2,1)S(1)}, u32[]{:S(2)}, u32[]{:S(2)}) %collective-permute-start.5) | collective-permute-done | bytes 262176 | tf_op jit(solution)/shard_map/ppermute | solution.py:337
  603.4 12.9 %collective-permute-done.12 = bf16[1,256,128]{2,1,0:T(8,128)(2,1)S(1)} collective-permute-done((bf16[1,256,128]{2,1,0:T(8,128)(2,1)S(1)}, bf16[1,256,128]{2,1,0:T(8,128)(2,1)S(1)}, u32[]{:S(2)}, u32[]{:S(2)}) %collective-permute-start.12) | collective-permute-done | bytes 65568 | tf_op jit(solution)/shard_map/ppermute | solution.py:337
  625.2 75.6 %back.1 = (bf16[512,8192]{1,0:T(8,128)(2,1)}, f32[64,128,128]{2,1,0:T(8,128)}, f32[64,128,128]{2,1,0:T(8,128)}) custom-call(bf16[512,8192]{1,0:T(8,128)(2,1)} %bitcast.194, bf16[512,8192]{1,0:T(8,128)(2,1)} %get-tuple-element.67.time_ref, bf16[64,128,512]{2,1,0:T(8,128)(2,1)} %get-tuple-element.68.first_ref, bf16[64,128,128]{2,1,0:T(8,128)(2,1)} %bitcast.204, ...), custom_call_target="tpu_custom_call" | custom-call | tf_op jit(solution)/shard_map/back/pallas_call | solution.py:294
  703.8 14.5 %all-to-all-start.7 = ((bf16[16,512,256]{2,1,0:T(8,128)(2,1)}), bf16[16,512,256]{2,1,0:T(8,128)(2,1)}, u32[]{:S(2)}, u32[]{:S(2)}) async-start(bf16[16,512,256]{2,1,0:T(8,128)(2,1)} %bitcast.223), calls=%async_computation.7 | async-start | bytes 8388608 | tf_op jit(solution)/shard_map/all_to_all | solution.py:387
  736.5 9.2 %collective-permute-done.19 = bf16[8,256,128]{2,1,0:T(8,128)(2,1)} collective-permute-done((bf16[8,256,128]{2,1,0:T(8,128)(2,1)S(1)}, bf16[8,256,128]{2,1,0:T(8,128)(2,1)}, u32[]{:S(2)}, u32[]{:S(2)}) %collective-permute-start.19) | collective-permute-done | bytes 524320 | tf_op jit(solution)/shard_map/ppermute | solution.py:337
  747.3 30.3 %collective-permute-done.14 = bf16[8,256,128]{2,1,0:T(8,128)(2,1)} collective-permute-done((bf16[8,256,128]{2,1,0:T(8,128)(2,1)}, bf16[8,256,128]{2,1,0:T(8,128)(2,1)}, u32[]{:S(2)}, u32[]{:S(2)}) %collective-permute-start.14) | collective-permute-done | bytes 524320 | tf_op jit(solution)/shard_map/ppermute | solution.py:337
  779.1 15.1 %collective-permute-done.15 = bf16[4,256,128]{2,1,0:T(8,128)(2,1)S(1)} collective-permute-done((bf16[4,256,128]{2,1,0:T(8,128)(2,1)S(1)}, bf16[4,256,128]{2,1,0:T(8,128)(2,1)S(1)}, u32[]{:S(2)}, u32[]{:S(2)}) %collective-permute-start.15) | collective-permute-done | bytes 262176 | tf_op jit(solution)/shard_map/ppermute | solution.py:337
  803.6 13.1 %collective-permute-done.22 = bf16[1,256,128]{2,1,0:T(8,128)(2,1)S(1)} collective-permute-done((bf16[1,256,128]{2,1,0:T(8,128)(2,1)S(1)}, bf16[1,256,128]{2,1,0:T(8,128)(2,1)S(1)}, u32[]{:S(2)}, u32[]{:S(2)}) %collective-permute-start.22) | collective-permute-done | bytes 65568 | tf_op jit(solution)/shard_map/ppermute | solution.py:337
  (153 shorter events, 180.9 us)
Async XLA Ops:
  20.9 96.3 %all-to-all-start = ((bf16[16,512,256]{2,1,0:T(8,128)(2,1)}), bf16[16,512,256]{2,1,0:T(8,128)(2,1)}, u32[]{:S(2)}, u32[]{:S(2)}) async-start(bf16[16,512,256]{2,1,0:T(8,128)(2,1)} %split.2), calls=%async_computation | async-start | bytes 8388608 | tf_op jit(solution)/shard_map/all_to_all | solution.py:387
  117.3 92.2 %all-to-all-start.1 = ((bf16[16,512,256]{2,1,0:T(8,128)(2,1)}), bf16[16,512,256]{2,1,0:T(8,128)(2,1)}, u32[]{:S(2)}, u32[]{:S(2)}) async-start(bf16[16,512,256]{2,1,0:T(8,128)(2,1)} %split.3), calls=%async_computation.1 | async-start | bytes 8388608 | tf_op jit(solution)/shard_map/all_to_all | solution.py:387
  126.7 67.0 %all-gather.5.cloned.1.call-start = ((), (), s32[]{:S(2)}) async-start(), calls=%async_computation.8 | async-start | bytes 2621440 | tf_op jit(solution)/shard_map/all_gather | solution.py:367
  209.5 97.9 %all-to-all-start.2 = ((bf16[16,512,256]{2,1,0:T(8,128)(2,1)}), bf16[16,512,256]{2,1,0:T(8,128)(2,1)}, u32[]{:S(2)}, u32[]{:S(2)}) async-start(bf16[16,512,256]{2,1,0:T(8,128)(2,1)} %get-tuple-element.86), calls=%async_computation.2 | async-start | bytes 8388608 | tf_op jit(solution)/shard_map/all_to_all | solution.py:387
  224.6 17.2 %all-gather.7.cloned.1.call-start = ((), (), s32[]{:S(2)}) async-start(), calls=%async_computation.9 | async-start | bytes 6291456 | tf_op jit(solution)/shard_map/all_gather | solution.py:371
  307.4 97.8 %all-to-all-start.3 = ((bf16[16,512,256]{2,1,0:T(8,128)(2,1)}), bf16[16,512,256]{2,1,0:T(8,128)(2,1)}, u32[]{:S(2)}, u32[]{:S(2)}) async-start(bf16[16,512,256]{2,1,0:T(8,128)(2,1)} %get-tuple-element.88), calls=%async_computation.3 | async-start | bytes 8388608 | tf_op jit(solution)/shard_map/all_to_all | solution.py:387
  405.1 97.8 %all-to-all-start.4 = ((bf16[16,512,256]{2,1,0:T(8,128)(2,1)}), bf16[16,512,256]{2,1,0:T(8,128)(2,1)}, u32[]{:S(2)}, u32[]{:S(2)}) async-start(bf16[16,512,256]{2,1,0:T(8,128)(2,1)} %bitcast.234), calls=%async_computation.4 | async-start | bytes 8388608 | tf_op jit(solution)/shard_map/all_to_all | solution.py:387
  502.9 114.2 %all-to-all-start.5 = ((bf16[16,512,256]{2,1,0:T(8,128)(2,1)}), bf16[16,512,256]{2,1,0:T(8,128)(2,1)}, u32[]{:S(2)}, u32[]{:S(2)}) async-start(bf16[16,512,256]{2,1,0:T(8,128)(2,1)} %bitcast.225), calls=%async_computation.5 | async-start | bytes 8388608 | tf_op jit(solution)/shard_map/all_to_all | solution.py:387
  529.0 15.0 %collective-permute-start.9 = (bf16[8,256,128]{2,1,0:T(8,128)(2,1)S(1)}, bf16[8,256,128]{2,1,0:T(8,128)(2,1)}, u32[]{:S(2)}, u32[]{:S(2)}) collective-permute-start(bf16[8,256,128]{2,1,0:T(8,128)(2,1)S(1)} %fusion.7), channel_id=1, source_target_pairs={{0,1},{1,0},{2,3},{3,2},{4,5},{5,4},{6,7},{7,6},{8,9},{9,8},{10,11... | collective-permute-start | bytes 1572872 | tf_op jit(solution)/shard_map/ppermute | solution.py:337
  534.3 42.9 %collective-permute-start.4 = (bf16[8,256,128]{2,1,0:T(8,128)(2,1)S(1)}, bf16[8,256,128]{2,1,0:T(8,128)(2,1)}, u32[]{:S(2)}, u32[]{:S(2)}) collective-permute-start(bf16[8,256,128]{2,1,0:T(8,128)(2,1)S(1)} %fusion.6), channel_id=1, source_target_pairs={{0,1},{1,0},{2,3},{3,2},{4,5},{5,4},{6,7},{7,6},{8,9},{9,8},{10,11... | collective-permute-start | bytes 1572872 | tf_op jit(solution)/shard_map/ppermute | solution.py:337
  545.2 33.2 %collective-permute-start.10 = (bf16[4,256,128]{2,1,0:T(8,128)(2,1)S(1)}, bf16[4,256,128]{2,1,0:T(8,128)(2,1)S(1)}, u32[]{:S(2)}, u32[]{:S(2)}) collective-permute-start(bf16[4,256,128]{2,1,0:T(8,128)(2,1)S(1)} %fusion.11), channel_id=1, source_target_pairs={{0,2},{1,3},{2,0},{3,1},{4,6},{5,7},{6,4},{7,5},{8,10},{9,11},{10,... | collective-permute-start | bytes 786440 | tf_op jit(solution)/shard_map/ppermute | solution.py:337
  578.4 16.9 %collective-permute-start.5 = (bf16[4,256,128]{2,1,0:T(8,128)(2,1)S(1)}, bf16[4,256,128]{2,1,0:T(8,128)(2,1)S(1)}, u32[]{:S(2)}, u32[]{:S(2)}) collective-permute-start(bf16[4,256,128]{2,1,0:T(8,128)(2,1)S(1)} %fusion.10), channel_id=1, source_target_pairs={{0,2},{1,3},{2,0},{3,1},{4,6},{5,7},{6,4},{7,5},{8,10},{9,11},{10,... | collective-permute-start | bytes 786440 | tf_op jit(solution)/shard_map/ppermute | solution.py:337
  578.6 21.1 %collective-permute-start.11 = (bf16[2,256,128]{2,1,0:T(8,128)(2,1)S(1)}, bf16[2,256,128]{2,1,0:T(8,128)(2,1)S(1)}, u32[]{:S(2)}, u32[]{:S(2)}) collective-permute-start(bf16[2,256,128]{2,1,0:T(8,128)(2,1)S(1)} %fusion.15), channel_id=1, source_target_pairs={{0,4},{1,5},{2,6},{3,7},{4,0},{5,1},{6,2},{7,3},{8,12},{9,13},{10,... | collective-permute-start | bytes 393224 | tf_op jit(solution)/shard_map/ppermute | solution.py:337
  599.7 16.7 %collective-permute-start.12 = (bf16[1,256,128]{2,1,0:T(8,128)(2,1)S(1)}, bf16[1,256,128]{2,1,0:T(8,128)(2,1)S(1)}, u32[]{:S(2)}, u32[]{:S(2)}) collective-permute-start(bf16[1,256,128]{2,1,0:T(8,128)(2,1)S(1)} %dynamic-slice_convert_fusion.13), channel_id=1, source_target_pairs={{0,8},{1,9},{2,10},{3,11},{4,12},{5,13},{6,14},{7,15},{8,0},{9,1},... | collective-permute-start | bytes 196616 | tf_op jit(solution)/shard_map/ppermute | solution.py:337
  603.4 13.7 %collective-permute-start.7 = (bf16[1,256,128]{2,1,0:T(8,128)(2,1)S(1)}, bf16[1,256,128]{2,1,0:T(8,128)(2,1)S(1)}, u32[]{:S(2)}, u32[]{:S(2)}) collective-permute-start(bf16[1,256,128]{2,1,0:T(8,128)(2,1)S(1)} %dynamic-slice_convert_fusion.14), channel_id=1, source_target_pairs={{0,8},{1,9},{2,10},{3,11},{4,12},{5,13},{6,14},{7,15},{8,0},{9,1},... | collective-permute-start | bytes 196616 | tf_op jit(solution)/shard_map/ppermute | solution.py:337
  617.1 86.7 %all-to-all-start.6 = ((bf16[16,512,256]{2,1,0:T(8,128)(2,1)}), bf16[16,512,256]{2,1,0:T(8,128)(2,1)}, u32[]{:S(2)}, u32[]{:S(2)}) async-start(bf16[16,512,256]{2,1,0:T(8,128)(2,1)} %bitcast.224), calls=%async_computation.6 | async-start | bytes 8388608 | tf_op jit(solution)/shard_map/all_to_all | solution.py:387
  703.8 115.4 %all-to-all-start.7 = ((bf16[16,512,256]{2,1,0:T(8,128)(2,1)}), bf16[16,512,256]{2,1,0:T(8,128)(2,1)}, u32[]{:S(2)}, u32[]{:S(2)}) async-start(bf16[16,512,256]{2,1,0:T(8,128)(2,1)} %bitcast.223), calls=%async_computation.7 | async-start | bytes 8388608 | tf_op jit(solution)/shard_map/all_to_all | solution.py:387
  725.1 20.7 %collective-permute-start.19 = (bf16[8,256,128]{2,1,0:T(8,128)(2,1)S(1)}, bf16[8,256,128]{2,1,0:T(8,128)(2,1)}, u32[]{:S(2)}, u32[]{:S(2)}) collective-permute-start(bf16[8,256,128]{2,1,0:T(8,128)(2,1)S(1)} %fusion.9), channel_id=1, source_target_pairs={{0,1},{1,0},{2,3},{3,2},{4,5},{5,4},{6,7},{7,6},{8,9},{9,8},{10,11... | collective-permute-start | bytes 1572872 | tf_op jit(solution)/shard_map/ppermute | solution.py:337
  728.8 48.9 %collective-permute-start.14 = (bf16[8,256,128]{2,1,0:T(8,128)(2,1)}, bf16[8,256,128]{2,1,0:T(8,128)(2,1)}, u32[]{:S(2)}, u32[]{:S(2)}) collective-permute-start(bf16[8,256,128]{2,1,0:T(8,128)(2,1)} %fusion.8), channel_id=1, source_target_pairs={{0,1},{1,0},{2,3},{3,2},{4,5},{5,4},{6,7},{7,6},{8,9},{9,8},{10,11... | collective-permute-start | bytes 1572872 | tf_op jit(solution)/shard_map/ppermute | solution.py:337
  747.3 31.6 %collective-permute-start.20 = (bf16[4,256,128]{2,1,0:T(8,128)(2,1)S(1)}, bf16[4,256,128]{2,1,0:T(8,128)(2,1)S(1)}, u32[]{:S(2)}, u32[]{:S(2)}) collective-permute-start(bf16[4,256,128]{2,1,0:T(8,128)(2,1)S(1)} %fusion.13), channel_id=1, source_target_pairs={{0,2},{1,3},{2,0},{3,1},{4,6},{5,7},{6,4},{7,5},{8,10},{9,11},{10,... | collective-permute-start | bytes 786440 | tf_op jit(solution)/shard_map/ppermute | solution.py:337
  778.8 15.4 %collective-permute-start.15 = (bf16[4,256,128]{2,1,0:T(8,128)(2,1)S(1)}, bf16[4,256,128]{2,1,0:T(8,128)(2,1)S(1)}, u32[]{:S(2)}, u32[]{:S(2)}) collective-permute-start(bf16[4,256,128]{2,1,0:T(8,128)(2,1)S(1)} %fusion.12), channel_id=1, source_target_pairs={{0,2},{1,3},{2,0},{3,1},{4,6},{5,7},{6,4},{7,5},{8,10},{9,11},{10,... | collective-permute-start | bytes 786440 | tf_op jit(solution)/shard_map/ppermute | solution.py:337
  779.0 16.2 %collective-permute-start.21 = (bf16[2,256,128]{2,1,0:T(8,128)(2,1)S(1)}, bf16[2,256,128]{2,1,0:T(8,128)(2,1)S(1)}, u32[]{:S(2)}, u32[]{:S(2)}) collective-permute-start(bf16[2,256,128]{2,1,0:T(8,128)(2,1)S(1)} %fusion.17), channel_id=1, source_target_pairs={{0,4},{1,5},{2,6},{3,7},{4,0},{5,1},{6,2},{7,3},{8,12},{9,13},{10,... | collective-permute-start | bytes 393224 | tf_op jit(solution)/shard_map/ppermute | solution.py:337
  795.3 21.4 %collective-permute-start.22 = (bf16[1,256,128]{2,1,0:T(8,128)(2,1)S(1)}, bf16[1,256,128]{2,1,0:T(8,128)(2,1)S(1)}, u32[]{:S(2)}, u32[]{:S(2)}) collective-permute-start(bf16[1,256,128]{2,1,0:T(8,128)(2,1)S(1)} %dynamic-slice_convert_fusion.11), channel_id=1, source_target_pairs={{0,8},{1,9},{2,10},{3,11},{4,12},{5,13},{6,14},{7,15},{8,0},{9,1},... | collective-permute-start | bytes 196616 | tf_op jit(solution)/shard_map/ppermute | solution.py:337
  803.5 14.5 %collective-permute-start.17 = (bf16[1,256,128]{2,1,0:T(8,128)(2,1)S(1)}, bf16[1,256,128]{2,1,0:T(8,128)(2,1)S(1)}, u32[]{:S(2)}, u32[]{:S(2)}) collective-permute-start(bf16[1,256,128]{2,1,0:T(8,128)(2,1)S(1)} %dynamic-slice_convert_fusion.12), channel_id=1, source_target_pairs={{0,8},{1,9},{2,10},{3,11},{4,12},{5,13},{6,14},{7,15},{8,0},{9,1},... | collective-permute-start | bytes 196616 | tf_op jit(solution)/shard_map/ppermute | solution.py:337
  (20 other events, 208.9 us)
Sparse Core Ops, SparseCore 0:
  129.4 64.2 all-gather.4
  227.0 14.7 all-gather.6

commit v5 on v4

--- a/solution.py
+++ b/solution.py
@@ -344,27 +344,37 @@
     return terms[0].reshape(blocks // mp, size // dp, width)
 
 
-def far_pairs(mp, step):
-    return [(i, (i // NEAR + step) % (mp // NEAR) * NEAR + i % NEAR) for i in range(mp)]
+def swapped(full, bit):
+    mp = lax.axis_size("mp")
+    return lax.ppermute(full, "mp", [(i, i ^ (1 << bit)) for i in range(mp)])
+
+
+def doubled(full, got, bit):
+    upper = (lax.axis_index("mp") >> bit) & 1 == 1
+    both = jnp.where(upper, jnp.stack([got, full], 1), jnp.stack([full, got], 1))
+    return both.reshape((-1,) + full.shape[1:])
 
 
 def far_tables(*tables):
     share, size, width = tables[0].shape
     dp, mp = lax.axis_size("dp"), lax.axis_size("mp")
     cut = jnp.stack(tables).reshape(len(tables), share, dp, size // dp, width)
-    cut = lax.dynamic_index_in_dim(cut, lax.axis_index("dp"), 2, keepdims=False)
-    return [cut] + [lax.ppermute(cut, "mp", far_pairs(mp, k)) for k in range(1, mp // NEAR)]
-
-
-def near_tables(parts):
-    mp = lax.axis_size("mp")
-    far, place = mp // NEAR, lax.axis_index("mp") // NEAR
-    parts = jnp.stack(parts)
-    full = [
-        lax.dynamic_index_in_dim(parts, (place - z) % far, 0, keepdims=False) for z in range(far)
-    ]
+    cut = lax.dynamic_index_in_dim(cut, lax.axis_index("dp"), 2, keepdims=False)[None]
+    return cut, swapped(cut, log2(mp) - 1)
+
+
+def column_tables(cut, got):
+    top = log2(lax.axis_size("mp")) - 1
+    full = doubled(cut, got, top)
+    for bit in reversed(range(log2(NEAR), top)):
+        full = doubled(full, swapped(full, bit), bit)
+    return full
+
+
+def near_tables(full):
+    far = lax.axis_size("mp") // NEAR
     planes = [[z * NEAR + n for n in range(NEAR)] for z in range(far)]
-    return lax.all_gather(jnp.stack(full), "mp", axis=0, tiled=False, axis_index_groups=planes)
+    return lax.all_gather(full, "mp", axis=0, tiled=False, axis_index_groups=planes)
 
 
 def all_tables(full):
@@ -395,6 +405,7 @@
         (sent, tables, cotangent, inputs, mixer_right, mixer_left)
     )
     above = [exchange(sent)]
+    tables = column_tables(*tables)
 
     eye = jnp.eye(LS, dtype=BF16)
     order = unfolded(eye, 0, LB)

time: 832 us -> 830 us (level)
  transfers between devices with their start and end apart: 33 -> 32, of which waited for: 24 -> 24; matrix products, arithmetic and copies ran while one was open for 13% -> 13% of each run, Pallas kernels for 32% -> 32%
where the time goes in v5:
time: 830 us; the launch traced here: 828 us
  waiting for transfers between devices  323 us (39%)
  Pallas kernels  269 us (32%)
  starting transfers between devices  109 us (13%)
  local copies, waits for them, and re-layouts  90.4 us (11%)
  other arithmetic  21.6 us (3%)
  between operations  14.7 us (2%)
    ppermute x20, waiting for transfers between devices, halve(): lax.ppermute(give.astype(kind), name, [(i, i ^ 1 << bit) for i in range(c...  158 us
    pallas_call x2, Pallas kernels, feature(): call(feature_kernel, grid=(piece // LANES,), in_specs=[strip, strip, tabl...  117 us
    all_to_all x8, starting transfers between devices, exchange(): return lax.all_to_all(part, 'mp', 0, 0, tiled=True).reshape(shape)  96.1 us
    all_to_all x8, waiting for transfers between devices, exchange(): return lax.all_to_all(part, 'mp', 0, 0, tiled=True).reshape(shape)  79.5 us
    pallas_call x1, Pallas kernels, back(): call(back_kernel, grid=(chans // LANES,), in_specs=[strip, strip, pl.Bloc...  75.6 us
    all_gather x1, waiting for transfers between devices, near_tables(): lax.all_gather(full, 'mp', axis=0, tiled=False, axis_index_groups=planes)  66.4 us
    pallas_call x1, Pallas kernels, mix(): call(mix_kernel, grid=(chans // LANES,), in_specs=[strip, table, table, f...  60.5 us
    another operation x3, local copies, waits for them, and re-layouts, unfolded(): cut = table.reshape(shape[:axis] + (blocks, fold) + shape[axis + 1:])  22.4 us
  transfers between devices with their start and end apart: 32, of which 24 were waited for; matrix products, arithmetic and copies ran while one was open for 13% of the time, Pallas kernels for 32%

profile of v5, /device:TPU:4, one launch (start us, length us, event | category | flops | bytes accessed | tf_op | source)
XLA Modules:
  0.0 828.1 jit_solution(8279832466263205578)
XLA Ops:
  53.6 60.5 %mix.1 = (bf16[16,512,256]{2,1,0:T(8,128)(2,1)}, bf16[16,512,256]{2,1,0:T(8,128)(2,1)}, bf16[512,8192]{1,0:T(8,128)(2,1)}, bf16[64,128,512]{2,1,0:T(8,128)(2,1)}) custom-call(bf16[512,8192]{1,0:T(8,128)(2,1)} %bitcast.191, bf16[64,128,128]{2,1,0:T(8,128)(2,1)} %bitcast.201, bf16[64,128,128]{2,1,0:T(8,128)(2,1)} %bitcast.199, ...), custom_call_target="tpu_custom_call" | custom-call | tf_op jit(solution)/shard_map/mix/pallas_call | solution.py:253
  115.0 9.9 %all-to-all-start.1 = ((bf16[16,512,256]{2,1,0:T(8,128)(2,1)}), bf16[16,512,256]{2,1,0:T(8,128)(2,1)}, u32[]{:S(2)}, u32[]{:S(2)}) async-start(bf16[16,512,256]{2,1,0:T(8,128)(2,1)} %split.3), calls=%async_computation.1 | async-start | bytes 8388608 | tf_op jit(solution)/shard_map/all_to_all | solution.py:397
  125.6 66.4 %all-gather.5.cloned.1.call-done = bf16[16,2,4,64,128]{4,3,2,1,0:T(8,128)(2,1)} async-done(((bf16[4,2,4,64,128]{4,3,2,1,0:T(8,128)(2,1)}), bf16[16,2,4,64,128]{4,3,2,1,0:T(8,128)(2,1)}) %all-gather.5.cloned.1.call-update) | async-done | bytes 2097168 | tf_op jit(solution)/shard_map/all_gather | solution.py:377
  191.9 15.8 %all-to-all-done.1 = bf16[16,512,256]{2,1,0:T(8,128)(2,1)} async-done(((bf16[16,512,256]{2,1,0:T(8,128)(2,1)}), bf16[16,512,256]{2,1,0:T(8,128)(2,1)}, u32[]{:S(2)}, u32[]{:S(2)}) %all-to-all-start.1) | async-done | bytes 4194336 | tf_op jit(solution)/shard_map/all_to_all | solution.py:397
  207.7 15.0 %all-to-all-start.2 = ((bf16[16,512,256]{2,1,0:T(8,128)(2,1)}), bf16[16,512,256]{2,1,0:T(8,128)(2,1)}, u32[]{:S(2)}, u32[]{:S(2)}) async-start(bf16[16,512,256]{2,1,0:T(8,128)(2,1)} %get-tuple-element.76), calls=%async_computation.2 | async-start | bytes 8388608 | tf_op jit(solution)/shard_map/all_to_all | solution.py:397
  223.5 16.4 %all-gather.7.cloned.1.call-done = bf16[8,4,2,4,64,128]{5,4,3,2,1,0:T(8,128)(2,1)} async-done(((bf16[4,4,2,4,64,128]{5,4,3,2,1,0:T(8,128)(2,1)}), bf16[8,4,2,4,64,128]{5,4,3,2,1,0:T(8,128)(2,1)}) %all-gather.7.cloned.1.call-update) | async-done | bytes 4194320 | tf_op jit(solution)/shard_map/all_gather | solution.py:381
  263.4 11.0 %copy.144 = bf16[1,4,4,4,2,64,128]{5,4,3,2,1,6,0:T(2,128)(2,1)} copy(bf16[1,4,4,4,2,64,128]{6,5,3,0,1,2,4:T(8,128)(2,1)} %get-tuple-element.143) | data formatting | bytes 4194304 | tf_op jit(solution)/shard_map/unstack | solution.py:423
  286.5 19.0 %all-to-all-done.2 = bf16[16,512,256]{2,1,0:T(8,128)(2,1)} async-done(((bf16[16,512,256]{2,1,0:T(8,128)(2,1)}), bf16[16,512,256]{2,1,0:T(8,128)(2,1)}, u32[]{:S(2)}, u32[]{:S(2)}) %all-to-all-start.2) | async-done | bytes 4194336 | tf_op jit(solution)/shard_map/all_to_all | solution.py:397
  305.5 15.0 %all-to-all-start.3 = ((bf16[16,512,256]{2,1,0:T(8,128)(2,1)}), bf16[16,512,256]{2,1,0:T(8,128)(2,1)}, u32[]{:S(2)}, u32[]{:S(2)}) async-start(bf16[16,512,256]{2,1,0:T(8,128)(2,1)} %get-tuple-element.78), calls=%async_computation.3 | async-start | bytes 8388608 | tf_op jit(solution)/shard_map/all_to_all | solution.py:397
  327.4 58.5 %feature.3 = (bf16[8192,256]{1,0:T(8,128)(2,1)}, bf16[8192,256]{1,0:T(8,128)(2,1)}, f32[64,128,128]{2,1,0:T(8,128)}, f32[64,128,128]{2,1,0:T(8,128)}) custom-call(bf16[8192,256]{1,0:T(8,128)(2,1)} %bitcast.33.hidden_ref, bf16[8192,256]{1,0:T(8,128)(2,1)} %bitcast.34.above_ref, bf16[64,128,128]{2,1,0:T(8,128)(2,1)} %bitcast.197, ...), custom_call_target="tpu_custom_call" | custom-call | tf_op jit(solution)/shard_map/feature/pallas_call | solution.py:275
  385.9 17.4 %all-to-all-done.3 = bf16[16,512,256]{2,1,0:T(8,128)(2,1)} async-done(((bf16[16,512,256]{2,1,0:T(8,128)(2,1)}), bf16[16,512,256]{2,1,0:T(8,128)(2,1)}, u32[]{:S(2)}, u32[]{:S(2)}) %all-to-all-start.3) | async-done | bytes 4194336 | tf_op jit(solution)/shard_map/all_to_all | solution.py:397
  403.3 15.0 %all-to-all-start.4 = ((bf16[16,512,256]{2,1,0:T(8,128)(2,1)}), bf16[16,512,256]{2,1,0:T(8,128)(2,1)}, u32[]{:S(2)}, u32[]{:S(2)}) async-start(bf16[16,512,256]{2,1,0:T(8,128)(2,1)} %bitcast.232), calls=%async_computation.4 | async-start | bytes 8388608 | tf_op jit(solution)/shard_map/all_to_all | solution.py:397
  418.2 58.5 %feature.2 = (bf16[8192,256]{1,0:T(8,128)(2,1)}, bf16[8192,256]{1,0:T(8,128)(2,1)}, f32[64,128,128]{2,1,0:T(8,128)}, f32[64,128,128]{2,1,0:T(8,128)}) custom-call(bf16[8192,256]{1,0:T(8,128)(2,1)} %bitcast.30.hidden_ref, bf16[8192,256]{1,0:T(8,128)(2,1)} %bitcast.31.above_ref, bf16[64,128,128]{2,1,0:T(8,128)(2,1)} %bitcast.198, ...), custom_call_target="tpu_custom_call" | custom-call | tf_op jit(solution)/shard_map/feature/pallas_call | solution.py:275
  476.7 24.3 %all-to-all-done.4.refs_0_ = bf16[16,512,256]{2,1,0:T(8,128)(2,1)} async-done(((bf16[16,512,256]{2,1,0:T(8,128)(2,1)}), bf16[16,512,256]{2,1,0:T(8,128)(2,1)}, u32[]{:S(2)}, u32[]{:S(2)}) %all-to-all-start.4) | async-done | bytes 4194336 | tf_op jit(solution)/shard_map/all_to_all | solution.py:397
  501.1 15.0 %all-to-all-start.5 = ((bf16[16,512,256]{2,1,0:T(8,128)(2,1)}), bf16[16,512,256]{2,1,0:T(8,128)(2,1)}, u32[]{:S(2)}, u32[]{:S(2)}) async-start(bf16[16,512,256]{2,1,0:T(8,128)(2,1)} %bitcast.223), calls=%async_computation.5 | async-start | bytes 8388608 | tf_op jit(solution)/shard_map/all_to_all | solution.py:397
  544.0 31.4 %collective-permute-done.3 = bf16[8,256,128]{2,1,0:T(8,128)(2,1)} collective-permute-done((bf16[8,256,128]{2,1,0:T(8,128)(2,1)S(1)}, bf16[8,256,128]{2,1,0:T(8,128)(2,1)}, u32[]{:S(2)}, u32[]{:S(2)}) %collective-permute-start.3) | collective-permute-done | bytes 524320 | tf_op jit(solution)/shard_map/ppermute | solution.py:337
  577.9 15.5 %collective-permute-done.4 = bf16[4,256,128]{2,1,0:T(8,128)(2,1)S(1)} collective-permute-done((bf16[4,256,128]{2,1,0:T(8,128)(2,1)S(1)}, bf16[4,256,128]{2,1,0:T(8,128)(2,1)S(1)}, u32[]{:S(2)}, u32[]{:S(2)}) %collective-permute-start.4) | collective-permute-done | bytes 262176 | tf_op jit(solution)/shard_map/ppermute | solution.py:337
  601.6 12.9 %collective-permute-done.11 = bf16[1,256,128]{2,1,0:T(8,128)(2,1)S(1)} collective-permute-done((bf16[1,256,128]{2,1,0:T(8,128)(2,1)S(1)}, bf16[1,256,128]{2,1,0:T(8,128)(2,1)S(1)}, u32[]{:S(2)}, u32[]{:S(2)}) %collective-permute-start.11) | collective-permute-done | bytes 65568 | tf_op jit(solution)/shard_map/ppermute | solution.py:337
  623.4 75.6 %back.1 = (bf16[512,8192]{1,0:T(8,128)(2,1)}, f32[64,128,128]{2,1,0:T(8,128)}, f32[64,128,128]{2,1,0:T(8,128)}) custom-call(bf16[512,8192]{1,0:T(8,128)(2,1)} %bitcast.192, bf16[512,8192]{1,0:T(8,128)(2,1)} %get-tuple-element.62.time_ref, bf16[64,128,512]{2,1,0:T(8,128)(2,1)} %get-tuple-element.63.first_ref, bf16[64,128,128]{2,1,0:T(8,128)(2,1)} %bitcast.202, ...), custom_call_target="tpu_custom_call" | custom-call | tf_op jit(solution)/shard_map/back/pallas_call | solution.py:294
  701.9 14.5 %all-to-all-start.7 = ((bf16[16,512,256]{2,1,0:T(8,128)(2,1)}), bf16[16,512,256]{2,1,0:T(8,128)(2,1)}, u32[]{:S(2)}, u32[]{:S(2)}) async-start(bf16[16,512,256]{2,1,0:T(8,128)(2,1)} %bitcast.221), calls=%async_computation.7 | async-start | bytes 8388608 | tf_op jit(solution)/shard_map/all_to_all | solution.py:397
  734.7 9.2 %collective-permute-done.18 = bf16[8,256,128]{2,1,0:T(8,128)(2,1)} collective-permute-done((bf16[8,256,128]{2,1,0:T(8,128)(2,1)S(1)}, bf16[8,256,128]{2,1,0:T(8,128)(2,1)}, u32[]{:S(2)}, u32[]{:S(2)}) %collective-permute-start.18) | collective-permute-done | bytes 524320 | tf_op jit(solution)/shard_map/ppermute | solution.py:337
  745.5 30.3 %collective-permute-done.13 = bf16[8,256,128]{2,1,0:T(8,128)(2,1)} collective-permute-done((bf16[8,256,128]{2,1,0:T(8,128)(2,1)}, bf16[8,256,128]{2,1,0:T(8,128)(2,1)}, u32[]{:S(2)}, u32[]{:S(2)}) %collective-permute-start.13) | collective-permute-done | bytes 524320 | tf_op jit(solution)/shard_map/ppermute | solution.py:337
  777.2 15.1 %collective-permute-done.14 = bf16[4,256,128]{2,1,0:T(8,128)(2,1)S(1)} collective-permute-done((bf16[4,256,128]{2,1,0:T(8,128)(2,1)S(1)}, bf16[4,256,128]{2,1,0:T(8,128)(2,1)S(1)}, u32[]{:S(2)}, u32[]{:S(2)}) %collective-permute-start.14) | collective-permute-done | bytes 262176 | tf_op jit(solution)/shard_map/ppermute | solution.py:337
  801.7 13.1 %collective-permute-done.21 = bf16[1,256,128]{2,1,0:T(8,128)(2,1)S(1)} collective-permute-done((bf16[1,256,128]{2,1,0:T(8,128)(2,1)S(1)}, bf16[1,256,128]{2,1,0:T(8,128)(2,1)S(1)}, u32[]{:S(2)}, u32[]{:S(2)}) %collective-permute-start.21) | collective-permute-done | bytes 65568 | tf_op jit(solution)/shard_map/ppermute | solution.py:337
  (151 shorter events, 178.3 us)
Async XLA Ops:
  17.1 97.9 %all-to-all-start = ((bf16[16,512,256]{2,1,0:T(8,128)(2,1)}), bf16[16,512,256]{2,1,0:T(8,128)(2,1)}, u32[]{:S(2)}, u32[]{:S(2)}) async-start(bf16[16,512,256]{2,1,0:T(8,128)(2,1)} %split.2), calls=%async_computation | async-start | bytes 8388608 | tf_op jit(solution)/shard_map/all_to_all | solution.py:397
  24.5 89.6 %collective-permute-start.1 = (bf16[2,2,4,64,128]{4,3,2,1,0:T(8,128)(2,1)S(1)}, bf16[2,2,4,64,128]{4,3,2,1,0:T(8,128)(2,1)S(1)}, u32[]{:S(2)}, u32[]{:S(2)}) collective-permute-start(bf16[2,2,4,64,128]{4,3,2,1,0:T(8,128)(2,1)S(1)} %maximum_select_fusion.1), channel_id=1, source_target_pairs={{0,4},{1,5},{2,6},{3,7},{4,0},{5,1},{6,2},{7,3},{8,12},{9,13},{10,... | collective-permute-start | bytes 786440 | tf_op jit(solution)/shard_map/ppermute | solution.py:349
  115.0 92.7 %all-to-all-start.1 = ((bf16[16,512,256]{2,1,0:T(8,128)(2,1)}), bf16[16,512,256]{2,1,0:T(8,128)(2,1)}, u32[]{:S(2)}, u32[]{:S(2)}) async-start(bf16[16,512,256]{2,1,0:T(8,128)(2,1)} %split.3), calls=%async_computation.1 | async-start | bytes 8388608 | tf_op jit(solution)/shard_map/all_to_all | solution.py:397
  124.8 67.1 %all-gather.5.cloned.1.call-start = ((), (), s32[]{:S(2)}) async-start(), calls=%async_computation.8 | async-start | bytes 2621440 | tf_op jit(solution)/shard_map/all_gather | solution.py:377
  207.7 97.8 %all-to-all-start.2 = ((bf16[16,512,256]{2,1,0:T(8,128)(2,1)}), bf16[16,512,256]{2,1,0:T(8,128)(2,1)}, u32[]{:S(2)}, u32[]{:S(2)}) async-start(bf16[16,512,256]{2,1,0:T(8,128)(2,1)} %get-tuple-element.76), calls=%async_computation.2 | async-start | bytes 8388608 | tf_op jit(solution)/shard_map/all_to_all | solution.py:397
  222.7 17.2 %all-gather.7.cloned.1.call-start = ((), (), s32[]{:S(2)}) async-start(), calls=%async_computation.9 | async-start | bytes 6291456 | tf_op jit(solution)/shard_map/all_gather | solution.py:381
  305.5 97.8 %all-to-all-start.3 = ((bf16[16,512,256]{2,1,0:T(8,128)(2,1)}), bf16[16,512,256]{2,1,0:T(8,128)(2,1)}, u32[]{:S(2)}, u32[]{:S(2)}) async-start(bf16[16,512,256]{2,1,0:T(8,128)(2,1)} %get-tuple-element.78), calls=%async_computation.3 | async-start | bytes 8388608 | tf_op jit(solution)/shard_map/all_to_all | solution.py:397
  403.3 97.8 %all-to-all-start.4 = ((bf16[16,512,256]{2,1,0:T(8,128)(2,1)}), bf16[16,512,256]{2,1,0:T(8,128)(2,1)}, u32[]{:S(2)}, u32[]{:S(2)}) async-start(bf16[16,512,256]{2,1,0:T(8,128)(2,1)} %bitcast.232), calls=%async_computation.4 | async-start | bytes 8388608 | tf_op jit(solution)/shard_map/all_to_all | solution.py:397
  501.1 114.2 %all-to-all-start.5 = ((bf16[16,512,256]{2,1,0:T(8,128)(2,1)}), bf16[16,512,256]{2,1,0:T(8,128)(2,1)}, u32[]{:S(2)}, u32[]{:S(2)}) async-start(bf16[16,512,256]{2,1,0:T(8,128)(2,1)} %bitcast.223), calls=%async_computation.5 | async-start | bytes 8388608 | tf_op jit(solution)/shard_map/all_to_all | solution.py:397
  527.2 15.0 %collective-permute-start.8 = (bf16[8,256,128]{2,1,0:T(8,128)(2,1)S(1)}, bf16[8,256,128]{2,1,0:T(8,128)(2,1)}, u32[]{:S(2)}, u32[]{:S(2)}) collective-permute-start(bf16[8,256,128]{2,1,0:T(8,128)(2,1)S(1)} %fusion.7), channel_id=1, source_target_pairs={{0,1},{1,0},{2,3},{3,2},{4,5},{5,4},{6,7},{7,6},{8,9},{9,8},{10,11... | collective-permute-start | bytes 1572872 | tf_op jit(solution)/shard_map/ppermute | solution.py:337
  532.4 42.9 %collective-permute-start.3 = (bf16[8,256,128]{2,1,0:T(8,128)(2,1)S(1)}, bf16[8,256,128]{2,1,0:T(8,128)(2,1)}, u32[]{:S(2)}, u32[]{:S(2)}) collective-permute-start(bf16[8,256,128]{2,1,0:T(8,128)(2,1)S(1)} %fusion.6), channel_id=1, source_target_pairs={{0,1},{1,0},{2,3},{3,2},{4,5},{5,4},{6,7},{7,6},{8,9},{9,8},{10,11... | collective-permute-start | bytes 1572872 | tf_op jit(solution)/shard_map/ppermute | solution.py:337
  543.4 33.2 %collective-permute-start.9 = (bf16[4,256,128]{2,1,0:T(8,128)(2,1)S(1)}, bf16[4,256,128]{2,1,0:T(8,128)(2,1)S(1)}, u32[]{:S(2)}, u32[]{:S(2)}) collective-permute-start(bf16[4,256,128]{2,1,0:T(8,128)(2,1)S(1)} %fusion.11), channel_id=1, source_target_pairs={{0,2},{1,3},{2,0},{3,1},{4,6},{5,7},{6,4},{7,5},{8,10},{9,11},{10,... | collective-permute-start | bytes 786440 | tf_op jit(solution)/shard_map/ppermute | solution.py:337
  576.5 16.9 %collective-permute-start.4 = (bf16[4,256,128]{2,1,0:T(8,128)(2,1)S(1)}, bf16[4,256,128]{2,1,0:T(8,128)(2,1)S(1)}, u32[]{:S(2)}, u32[]{:S(2)}) collective-permute-start(bf16[4,256,128]{2,1,0:T(8,128)(2,1)S(1)} %fusion.10), channel_id=1, source_target_pairs={{0,2},{1,3},{2,0},{3,1},{4,6},{5,7},{6,4},{7,5},{8,10},{9,11},{10,... | collective-permute-start | bytes 786440 | tf_op jit(solution)/shard_map/ppermute | solution.py:337
  576.7 21.1 %collective-permute-start.10 = (bf16[2,256,128]{2,1,0:T(8,128)(2,1)S(1)}, bf16[2,256,128]{2,1,0:T(8,128)(2,1)S(1)}, u32[]{:S(2)}, u32[]{:S(2)}) collective-permute-start(bf16[2,256,128]{2,1,0:T(8,128)(2,1)S(1)} %fusion.15), channel_id=1, source_target_pairs={{0,4},{1,5},{2,6},{3,7},{4,0},{5,1},{6,2},{7,3},{8,12},{9,13},{10,... | collective-permute-start | bytes 393224 | tf_op jit(solution)/shard_map/ppermute | solution.py:337
  597.9 16.7 %collective-permute-start.11 = (bf16[1,256,128]{2,1,0:T(8,128)(2,1)S(1)}, bf16[1,256,128]{2,1,0:T(8,128)(2,1)S(1)}, u32[]{:S(2)}, u32[]{:S(2)}) collective-permute-start(bf16[1,256,128]{2,1,0:T(8,128)(2,1)S(1)} %dynamic-slice_convert_fusion.13), channel_id=1, source_target_pairs={{0,8},{1,9},{2,10},{3,11},{4,12},{5,13},{6,14},{7,15},{8,0},{9,1},... | collective-permute-start | bytes 196616 | tf_op jit(solution)/shard_map/ppermute | solution.py:337
  615.3 86.7 %all-to-all-start.6 = ((bf16[16,512,256]{2,1,0:T(8,128)(2,1)}), bf16[16,512,256]{2,1,0:T(8,128)(2,1)}, u32[]{:S(2)}, u32[]{:S(2)}) async-start(bf16[16,512,256]{2,1,0:T(8,128)(2,1)} %bitcast.222), calls=%async_computation.6 | async-start | bytes 8388608 | tf_op jit(solution)/shard_map/all_to_all | solution.py:397
  701.9 115.4 %all-to-all-start.7 = ((bf16[16,512,256]{2,1,0:T(8,128)(2,1)}), bf16[16,512,256]{2,1,0:T(8,128)(2,1)}, u32[]{:S(2)}, u32[]{:S(2)}) async-start(bf16[16,512,256]{2,1,0:T(8,128)(2,1)} %bitcast.221), calls=%async_computation.7 | async-start | bytes 8388608 | tf_op jit(solution)/shard_map/all_to_all | solution.py:397
  723.2 20.7 %collective-permute-start.18 = (bf16[8,256,128]{2,1,0:T(8,128)(2,1)S(1)}, bf16[8,256,128]{2,1,0:T(8,128)(2,1)}, u32[]{:S(2)}, u32[]{:S(2)}) collective-permute-start(bf16[8,256,128]{2,1,0:T(8,128)(2,1)S(1)} %fusion.9), channel_id=1, source_target_pairs={{0,1},{1,0},{2,3},{3,2},{4,5},{5,4},{6,7},{7,6},{8,9},{9,8},{10,11... | collective-permute-start | bytes 1572872 | tf_op jit(solution)/shard_map/ppermute | solution.py:337
  726.9 48.8 %collective-permute-start.13 = (bf16[8,256,128]{2,1,0:T(8,128)(2,1)}, bf16[8,256,128]{2,1,0:T(8,128)(2,1)}, u32[]{:S(2)}, u32[]{:S(2)}) collective-permute-start(bf16[8,256,128]{2,1,0:T(8,128)(2,1)} %fusion.8), channel_id=1, source_target_pairs={{0,1},{1,0},{2,3},{3,2},{4,5},{5,4},{6,7},{7,6},{8,9},{9,8},{10,11... | collective-permute-start | bytes 1572872 | tf_op jit(solution)/shard_map/ppermute | solution.py:337
  745.4 31.6 %collective-permute-start.19 = (bf16[4,256,128]{2,1,0:T(8,128)(2,1)S(1)}, bf16[4,256,128]{2,1,0:T(8,128)(2,1)S(1)}, u32[]{:S(2)}, u32[]{:S(2)}) collective-permute-start(bf16[4,256,128]{2,1,0:T(8,128)(2,1)S(1)} %fusion.13), channel_id=1, source_target_pairs={{0,2},{1,3},{2,0},{3,1},{4,6},{5,7},{6,4},{7,5},{8,10},{9,11},{10,... | collective-permute-start | bytes 786440 | tf_op jit(solution)/shard_map/ppermute | solution.py:337
  777.0 15.4 %collective-permute-start.14 = (bf16[4,256,128]{2,1,0:T(8,128)(2,1)S(1)}, bf16[4,256,128]{2,1,0:T(8,128)(2,1)S(1)}, u32[]{:S(2)}, u32[]{:S(2)}) collective-permute-start(bf16[4,256,128]{2,1,0:T(8,128)(2,1)S(1)} %fusion.12), channel_id=1, source_target_pairs={{0,2},{1,3},{2,0},{3,1},{4,6},{5,7},{6,4},{7,5},{8,10},{9,11},{10,... | collective-permute-start | bytes 786440 | tf_op jit(solution)/shard_map/ppermute | solution.py:337
  777.1 16.2 %collective-permute-start.20 = (bf16[2,256,128]{2,1,0:T(8,128)(2,1)S(1)}, bf16[2,256,128]{2,1,0:T(8,128)(2,1)S(1)}, u32[]{:S(2)}, u32[]{:S(2)}) collective-permute-start(bf16[2,256,128]{2,1,0:T(8,128)(2,1)S(1)} %fusion.17), channel_id=1, source_target_pairs={{0,4},{1,5},{2,6},{3,7},{4,0},{5,1},{6,2},{7,3},{8,12},{9,13},{10,... | collective-permute-start | bytes 393224 | tf_op jit(solution)/shard_map/ppermute | solution.py:337
  793.4 21.5 %collective-permute-start.21 = (bf16[1,256,128]{2,1,0:T(8,128)(2,1)S(1)}, bf16[1,256,128]{2,1,0:T(8,128)(2,1)S(1)}, u32[]{:S(2)}, u32[]{:S(2)}) collective-permute-start(bf16[1,256,128]{2,1,0:T(8,128)(2,1)S(1)} %dynamic-slice_convert_fusion.11), channel_id=1, source_target_pairs={{0,8},{1,9},{2,10},{3,11},{4,12},{5,13},{6,14},{7,15},{8,0},{9,1},... | collective-permute-start | bytes 196616 | tf_op jit(solution)/shard_map/ppermute | solution.py:337
  801.6 14.5 %collective-permute-start.16 = (bf16[1,256,128]{2,1,0:T(8,128)(2,1)S(1)}, bf16[1,256,128]{2,1,0:T(8,128)(2,1)S(1)}, u32[]{:S(2)}, u32[]{:S(2)}) collective-permute-start(bf16[1,256,128]{2,1,0:T(8,128)(2,1)S(1)} %dynamic-slice_convert_fusion.12), channel_id=1, source_target_pairs={{0,8},{1,9},{2,10},{3,11},{4,12},{5,13},{6,14},{7,15},{8,0},{9,1},... | collective-permute-start | bytes 196616 | tf_op jit(solution)/shard_map/ppermute | solution.py:337
  (19 other events, 202.8 us)
Sparse Core Ops, SparseCore 0:
  127.5 64.3 all-gather.4
  225.1 14.7 all-gather.6

commit v6 on v5

--- a/solution.py
+++ b/solution.py
@@ -338,7 +338,7 @@
         return [keep + got.astype(F32)]
 
     for bit in range(log2(dp)):
-        terms = halve(terms, "dp", bit, blocks * groups * (dp >> (bit + 1)), F32 if bit == 0 else BF16)
+        terms = halve(terms, "dp", bit, blocks * groups * (dp >> (bit + 1)), BF16)
     for bit in range(log2(mp)):
         terms = halve(terms, "mp", bit, mp >> (bit + 1), BF16)
     return terms[0].reshape(blocks // mp, size // dp, width)

time: 830 us -> 830 us (level)
  transfers between devices with their start and end apart: 32 -> 32, of which waited for: 24 -> 22; matrix products, arithmetic and copies ran while one was open for 13% -> 13% of each run, Pallas kernels for 32% -> 32%
where the time goes in v6:
time: 830 us; the launch traced here: 828 us
  waiting for transfers between devices  325 us (39%)
  Pallas kernels  269 us (32%)
  starting transfers between devices  109 us (13%)
  local copies, waits for them, and re-layouts  92 us (11%)
  other arithmetic  18.3 us (2%)
  between operations  14.7 us (2%)
    ppermute x20, waiting for transfers between devices, halve(): lax.ppermute(give.astype(kind), name, [(i, i ^ 1 << bit) for i in range(c...  159 us
    pallas_call x2, Pallas kernels, feature(): call(feature_kernel, grid=(piece // LANES,), in_specs=[strip, strip, tabl...  117 us
    all_to_all x8, starting transfers between devices, exchange(): return lax.all_to_all(part, 'mp', 0, 0, tiled=True).reshape(shape)  96.3 us
    all_to_all x8, waiting for transfers between devices, exchange(): return lax.all_to_all(part, 'mp', 0, 0, tiled=True).reshape(shape)  79.5 us
    pallas_call x1, Pallas kernels, back(): call(back_kernel, grid=(chans // LANES,), in_specs=[strip, strip, pl.Bloc...  75.6 us
    all_gather x1, waiting for transfers between devices, near_tables(): lax.all_gather(full, 'mp', axis=0, tiled=False, axis_index_groups=planes)  66.4 us
    pallas_call x1, Pallas kernels, mix(): call(mix_kernel, grid=(chans // LANES,), in_specs=[strip, table, table, f...  60.5 us
    another operation x3, local copies, waits for them, and re-layouts, unfolded(): cut = table.reshape(shape[:axis] + (blocks, fold) + shape[axis + 1:])  22.4 us
  transfers between devices with their start and end apart: 32, of which 22 were waited for; matrix products, arithmetic and copies ran while one was open for 13% of the time, Pallas kernels for 32%

profile of v6, /device:TPU:4, one launch (start us, length us, event | category | flops | bytes accessed | tf_op | source)
XLA Modules:
  0.0 828.2 jit_solution(2716283028943339135)
XLA Ops:
  53.6 60.5 %mix.1 = (bf16[16,512,256]{2,1,0:T(8,128)(2,1)}, bf16[16,512,256]{2,1,0:T(8,128)(2,1)}, bf16[512,8192]{1,0:T(8,128)(2,1)}, bf16[64,128,512]{2,1,0:T(8,128)(2,1)}) custom-call(bf16[512,8192]{1,0:T(8,128)(2,1)} %bitcast.206, bf16[64,128,128]{2,1,0:T(8,128)(2,1)} %bitcast.216, bf16[64,128,128]{2,1,0:T(8,128)(2,1)} %bitcast.214, ...), custom_call_target="tpu_custom_call" | custom-call | tf_op jit(solution)/shard_map/mix/pallas_call | solution.py:253
  125.6 66.4 %all-gather.5.cloned.1.call-done = bf16[16,2,4,64,128]{4,3,2,1,0:T(8,128)(2,1)} async-done(((bf16[4,2,4,64,128]{4,3,2,1,0:T(8,128)(2,1)}), bf16[16,2,4,64,128]{4,3,2,1,0:T(8,128)(2,1)}) %all-gather.5.cloned.1.call-update) | async-done | bytes 2097168 | tf_op jit(solution)/shard_map/all_gather | solution.py:377
  191.9 15.8 %all-to-all-done.1 = bf16[16,512,256]{2,1,0:T(8,128)(2,1)} async-done(((bf16[16,512,256]{2,1,0:T(8,128)(2,1)}), bf16[16,512,256]{2,1,0:T(8,128)(2,1)}, u32[]{:S(2)}, u32[]{:S(2)}) %all-to-all-start.1) | async-done | bytes 4194336 | tf_op jit(solution)/shard_map/all_to_all | solution.py:397
  207.7 15.0 %all-to-all-start.2 = ((bf16[16,512,256]{2,1,0:T(8,128)(2,1)}), bf16[16,512,256]{2,1,0:T(8,128)(2,1)}, u32[]{:S(2)}, u32[]{:S(2)}) async-start(bf16[16,512,256]{2,1,0:T(8,128)(2,1)} %get-tuple-element.76), calls=%async_computation.2 | async-start | bytes 8388608 | tf_op jit(solution)/shard_map/all_to_all | solution.py:397
  223.5 16.4 %all-gather.7.cloned.1.call-done = bf16[8,4,2,4,64,128]{5,4,3,2,1,0:T(8,128)(2,1)} async-done(((bf16[4,4,2,4,64,128]{5,4,3,2,1,0:T(8,128)(2,1)}), bf16[8,4,2,4,64,128]{5,4,3,2,1,0:T(8,128)(2,1)}) %all-gather.7.cloned.1.call-update) | async-done | bytes 4194320 | tf_op jit(solution)/shard_map/all_gather | solution.py:381
  263.3 11.0 %copy.146 = bf16[1,4,4,4,2,64,128]{5,4,3,2,1,6,0:T(2,128)(2,1)} copy(bf16[1,4,4,4,2,64,128]{6,5,3,0,1,2,4:T(8,128)(2,1)} %get-tuple-element.143) | data formatting | bytes 4194304 | tf_op jit(solution)/shard_map/unstack | solution.py:423
  286.5 19.1 %all-to-all-done.2 = bf16[16,512,256]{2,1,0:T(8,128)(2,1)} async-done(((bf16[16,512,256]{2,1,0:T(8,128)(2,1)}), bf16[16,512,256]{2,1,0:T(8,128)(2,1)}, u32[]{:S(2)}, u32[]{:S(2)}) %all-to-all-start.2) | async-done | bytes 4194336 | tf_op jit(solution)/shard_map/all_to_all | solution.py:397
  305.5 15.0 %all-to-all-start.3 = ((bf16[16,512,256]{2,1,0:T(8,128)(2,1)}), bf16[16,512,256]{2,1,0:T(8,128)(2,1)}, u32[]{:S(2)}, u32[]{:S(2)}) async-start(bf16[16,512,256]{2,1,0:T(8,128)(2,1)} %get-tuple-element.78), calls=%async_computation.3 | async-start | bytes 8388608 | tf_op jit(solution)/shard_map/all_to_all | solution.py:397
  327.4 58.5 %feature.3 = (bf16[8192,256]{1,0:T(8,128)(2,1)}, bf16[8192,256]{1,0:T(8,128)(2,1)}, f32[64,128,128]{2,1,0:T(8,128)}, f32[64,128,128]{2,1,0:T(8,128)}) custom-call(bf16[8192,256]{1,0:T(8,128)(2,1)} %bitcast.33.hidden_ref, bf16[8192,256]{1,0:T(8,128)(2,1)} %bitcast.34.above_ref, bf16[64,128,128]{2,1,0:T(8,128)(2,1)} %bitcast.212, ...), custom_call_target="tpu_custom_call" | custom-call | tf_op jit(solution)/shard_map/feature/pallas_call | solution.py:275
  385.9 17.4 %all-to-all-done.3 = bf16[16,512,256]{2,1,0:T(8,128)(2,1)} async-done(((bf16[16,512,256]{2,1,0:T(8,128)(2,1)}), bf16[16,512,256]{2,1,0:T(8,128)(2,1)}, u32[]{:S(2)}, u32[]{:S(2)}) %all-to-all-start.3) | async-done | bytes 4194336 | tf_op jit(solution)/shard_map/all_to_all | solution.py:397
  403.3 15.0 %all-to-all-start.4 = ((bf16[16,512,256]{2,1,0:T(8,128)(2,1)}), bf16[16,512,256]{2,1,0:T(8,128)(2,1)}, u32[]{:S(2)}, u32[]{:S(2)}) async-start(bf16[16,512,256]{2,1,0:T(8,128)(2,1)} %bitcast.235), calls=%async_computation.4 | async-start | bytes 8388608 | tf_op jit(solution)/shard_map/all_to_all | solution.py:397
  418.2 58.5 %feature.2 = (bf16[8192,256]{1,0:T(8,128)(2,1)}, bf16[8192,256]{1,0:T(8,128)(2,1)}, f32[64,128,128]{2,1,0:T(8,128)}, f32[64,128,128]{2,1,0:T(8,128)}) custom-call(bf16[8192,256]{1,0:T(8,128)(2,1)} %bitcast.30.hidden_ref, bf16[8192,256]{1,0:T(8,128)(2,1)} %bitcast.31.above_ref, bf16[64,128,128]{2,1,0:T(8,128)(2,1)} %bitcast.213, ...), custom_call_target="tpu_custom_call" | custom-call | tf_op jit(solution)/shard_map/feature/pallas_call | solution.py:275
  476.7 24.3 %all-to-all-done.4.refs_0_ = bf16[16,512,256]{2,1,0:T(8,128)(2,1)} async-done(((bf16[16,512,256]{2,1,0:T(8,128)(2,1)}), bf16[16,512,256]{2,1,0:T(8,128)(2,1)}, u32[]{:S(2)}, u32[]{:S(2)}) %all-to-all-start.4) | async-done | bytes 4194336 | tf_op jit(solution)/shard_map/all_to_all | solution.py:397
  501.1 15.0 %all-to-all-start.5 = ((bf16[16,512,256]{2,1,0:T(8,128)(2,1)}), bf16[16,512,256]{2,1,0:T(8,128)(2,1)}, u32[]{:S(2)}, u32[]{:S(2)}) async-start(bf16[16,512,256]{2,1,0:T(8,128)(2,1)} %bitcast.234), calls=%async_computation.5 | async-start | bytes 8388608 | tf_op jit(solution)/shard_map/all_to_all | solution.py:397
  532.0 10.9 %collective-permute-done.8 = bf16[8,256,128]{2,1,0:T(8,128)(2,1)} collective-permute-done((bf16[8,256,128]{2,1,0:T(8,128)(2,1)}, bf16[8,256,128]{2,1,0:T(8,128)(2,1)}, u32[]{:S(2)}, u32[]{:S(2)}) %collective-permute-start.8) | collective-permute-done | bytes 524320 | tf_op jit(solution)/shard_map/ppermute | solution.py:337
  544.1 31.1 %collective-permute-done.3 = bf16[8,256,128]{2,1,0:T(8,128)(2,1)S(1)} collective-permute-done((bf16[8,256,128]{2,1,0:T(8,128)(2,1)S(1)}, bf16[8,256,128]{2,1,0:T(8,128)(2,1)S(1)}, u32[]{:S(2)}, u32[]{:S(2)}) %collective-permute-start.3) | collective-permute-done | bytes 524320 | tf_op jit(solution)/shard_map/ppermute | solution.py:337
  575.9 15.3 %collective-permute-done.4 = bf16[4,256,128]{2,1,0:T(8,128)(2,1)S(1)} collective-permute-done((bf16[4,256,128]{2,1,0:T(8,128)(2,1)S(1)}, bf16[4,256,128]{2,1,0:T(8,128)(2,1)S(1)}, u32[]{:S(2)}, u32[]{:S(2)}) %collective-permute-start.4) | collective-permute-done | bytes 262176 | tf_op jit(solution)/shard_map/ppermute | solution.py:337
  601.3 13.2 %collective-permute-done.11 = bf16[1,256,128]{2,1,0:T(8,128)(2,1)S(1)} collective-permute-done((bf16[1,256,128]{2,1,0:T(8,128)(2,1)S(1)}, bf16[1,256,128]{2,1,0:T(8,128)(2,1)S(1)}, u32[]{:S(2)}, u32[]{:S(2)}) %collective-permute-start.11) | collective-permute-done | bytes 65568 | tf_op jit(solution)/shard_map/ppermute | solution.py:337
  623.4 75.6 %back.1 = (bf16[512,8192]{1,0:T(8,128)(2,1)}, f32[64,128,128]{2,1,0:T(8,128)}, f32[64,128,128]{2,1,0:T(8,128)}) custom-call(bf16[512,8192]{1,0:T(8,128)(2,1)} %bitcast.207, bf16[512,8192]{1,0:T(8,128)(2,1)} %get-tuple-element.62.time_ref, bf16[64,128,512]{2,1,0:T(8,128)(2,1)} %get-tuple-element.63.first_ref, bf16[64,128,128]{2,1,0:T(8,128)(2,1)} %bitcast.217, ...), custom_call_target="tpu_custom_call" | custom-call | tf_op jit(solution)/shard_map/back/pallas_call | solution.py:294
  702.0 14.5 %all-to-all-start.7 = ((bf16[16,512,256]{2,1,0:T(8,128)(2,1)}), bf16[16,512,256]{2,1,0:T(8,128)(2,1)}, u32[]{:S(2)}, u32[]{:S(2)}) async-start(bf16[16,512,256]{2,1,0:T(8,128)(2,1)} %bitcast.232), calls=%async_computation.7 | async-start | bytes 8388608 | tf_op jit(solution)/shard_map/all_to_all | solution.py:397
  732.3 11.8 %collective-permute-done.18 = bf16[8,256,128]{2,1,0:T(8,128)(2,1)} collective-permute-done((bf16[8,256,128]{2,1,0:T(8,128)(2,1)S(1)}, bf16[8,256,128]{2,1,0:T(8,128)(2,1)}, u32[]{:S(2)}, u32[]{:S(2)}) %collective-permute-start.18) | collective-permute-done | bytes 524320 | tf_op jit(solution)/shard_map/ppermute | solution.py:337
  745.7 30.1 %collective-permute-done.13 = bf16[8,256,128]{2,1,0:T(8,128)(2,1)} collective-permute-done((bf16[8,256,128]{2,1,0:T(8,128)(2,1)}, bf16[8,256,128]{2,1,0:T(8,128)(2,1)}, u32[]{:S(2)}, u32[]{:S(2)}) %collective-permute-start.13) | collective-permute-done | bytes 524320 | tf_op jit(solution)/shard_map/ppermute | solution.py:337
  777.3 15.1 %collective-permute-done.14 = bf16[4,256,128]{2,1,0:T(8,128)(2,1)S(1)} collective-permute-done((bf16[4,256,128]{2,1,0:T(8,128)(2,1)S(1)}, bf16[4,256,128]{2,1,0:T(8,128)(2,1)S(1)}, u32[]{:S(2)}, u32[]{:S(2)}) %collective-permute-start.14) | collective-permute-done | bytes 262176 | tf_op jit(solution)/shard_map/ppermute | solution.py:337
  801.9 13.1 %collective-permute-done.21 = bf16[1,256,128]{2,1,0:T(8,128)(2,1)S(1)} collective-permute-done((bf16[1,256,128]{2,1,0:T(8,128)(2,1)S(1)}, bf16[1,256,128]{2,1,0:T(8,128)(2,1)S(1)}, u32[]{:S(2)}, u32[]{:S(2)}) %collective-permute-start.21) | collective-permute-done | bytes 65568 | tf_op jit(solution)/shard_map/ppermute | solution.py:337
  (151 shorter events, 175.0 us)
Async XLA Ops:
  17.1 97.9 %all-to-all-start = ((bf16[16,512,256]{2,1,0:T(8,128)(2,1)}), bf16[16,512,256]{2,1,0:T(8,128)(2,1)}, u32[]{:S(2)}, u32[]{:S(2)}) async-start(bf16[16,512,256]{2,1,0:T(8,128)(2,1)} %split.2), calls=%async_computation | async-start | bytes 8388608 | tf_op jit(solution)/shard_map/all_to_all | solution.py:397
  24.5 89.6 %collective-permute-start.1 = (bf16[2,2,4,64,128]{4,3,2,1,0:T(8,128)(2,1)S(1)}, bf16[2,2,4,64,128]{4,3,2,1,0:T(8,128)(2,1)S(1)}, u32[]{:S(2)}, u32[]{:S(2)}) collective-permute-start(bf16[2,2,4,64,128]{4,3,2,1,0:T(8,128)(2,1)S(1)} %maximum_select_fusion.1), channel_id=1, source_target_pairs={{0,4},{1,5},{2,6},{3,7},{4,0},{5,1},{6,2},{7,3},{8,12},{9,13},{10,... | collective-permute-start | bytes 786440 | tf_op jit(solution)/shard_map/ppermute | solution.py:349
  115.0 92.7 %all-to-all-start.1 = ((bf16[16,512,256]{2,1,0:T(8,128)(2,1)}), bf16[16,512,256]{2,1,0:T(8,128)(2,1)}, u32[]{:S(2)}, u32[]{:S(2)}) async-start(bf16[16,512,256]{2,1,0:T(8,128)(2,1)} %split.3), calls=%async_computation.1 | async-start | bytes 8388608 | tf_op jit(solution)/shard_map/all_to_all | solution.py:397
  124.8 67.1 %all-gather.5.cloned.1.call-start = ((), (), s32[]{:S(2)}) async-start(), calls=%async_computation.8 | async-start | bytes 2621440 | tf_op jit(solution)/shard_map/all_gather | solution.py:377
  207.7 97.8 %all-to-all-start.2 = ((bf16[16,512,256]{2,1,0:T(8,128)(2,1)}), bf16[16,512,256]{2,1,0:T(8,128)(2,1)}, u32[]{:S(2)}, u32[]{:S(2)}) async-start(bf16[16,512,256]{2,1,0:T(8,128)(2,1)} %get-tuple-element.76), calls=%async_computation.2 | async-start | bytes 8388608 | tf_op jit(solution)/shard_map/all_to_all | solution.py:397
  222.7 17.2 %all-gather.7.cloned.1.call-start = ((), (), s32[]{:S(2)}) async-start(), calls=%async_computation.9 | async-start | bytes 6291456 | tf_op jit(solution)/shard_map/all_gather | solution.py:381
  305.5 97.8 %all-to-all-start.3 = ((bf16[16,512,256]{2,1,0:T(8,128)(2,1)}), bf16[16,512,256]{2,1,0:T(8,128)(2,1)}, u32[]{:S(2)}, u32[]{:S(2)}) async-start(bf16[16,512,256]{2,1,0:T(8,128)(2,1)} %get-tuple-element.78), calls=%async_computation.3 | async-start | bytes 8388608 | tf_op jit(solution)/shard_map/all_to_all | solution.py:397
  403.3 97.8 %all-to-all-start.4 = ((bf16[16,512,256]{2,1,0:T(8,128)(2,1)}), bf16[16,512,256]{2,1,0:T(8,128)(2,1)}, u32[]{:S(2)}, u32[]{:S(2)}) async-start(bf16[16,512,256]{2,1,0:T(8,128)(2,1)} %bitcast.235), calls=%async_computation.4 | async-start | bytes 8388608 | tf_op jit(solution)/shard_map/all_to_all | solution.py:397
  501.1 114.1 %all-to-all-start.5 = ((bf16[16,512,256]{2,1,0:T(8,128)(2,1)}), bf16[16,512,256]{2,1,0:T(8,128)(2,1)}, u32[]{:S(2)}, u32[]{:S(2)}) async-start(bf16[16,512,256]{2,1,0:T(8,128)(2,1)} %bitcast.234), calls=%async_computation.5 | async-start | bytes 8388608 | tf_op jit(solution)/shard_map/all_to_all | solution.py:397
  526.0 16.8 %collective-permute-start.8 = (bf16[8,256,128]{2,1,0:T(8,128)(2,1)}, bf16[8,256,128]{2,1,0:T(8,128)(2,1)}, u32[]{:S(2)}, u32[]{:S(2)}) collective-permute-start(bf16[8,256,128]{2,1,0:T(8,128)(2,1)} %fusion.11), channel_id=1, source_target_pairs={{0,1},{1,0},{2,3},{3,2},{4,5},{5,4},{6,7},{7,6},{8,9},{9,8},{10,11... | collective-permute-start | bytes 1572872 | tf_op jit(solution)/shard_map/ppermute | solution.py:337
  530.9 44.4 %collective-permute-start.3 = (bf16[8,256,128]{2,1,0:T(8,128)(2,1)S(1)}, bf16[8,256,128]{2,1,0:T(8,128)(2,1)S(1)}, u32[]{:S(2)}, u32[]{:S(2)}) collective-permute-start(bf16[8,256,128]{2,1,0:T(8,128)(2,1)S(1)} %fusion.10), channel_id=1, source_target_pairs={{0,1},{1,0},{2,3},{3,2},{4,5},{5,4},{6,7},{7,6},{8,9},{9,8},{10,11... | collective-permute-start | bytes 1572872 | tf_op jit(solution)/shard_map/ppermute | solution.py:337
  544.0 31.4 %collective-permute-start.9 = (bf16[4,256,128]{2,1,0:T(8,128)(2,1)S(1)}, bf16[4,256,128]{2,1,0:T(8,128)(2,1)S(1)}, u32[]{:S(2)}, u32[]{:S(2)}) collective-permute-start(bf16[4,256,128]{2,1,0:T(8,128)(2,1)S(1)} %fusion.15), channel_id=1, source_target_pairs={{0,2},{1,3},{2,0},{3,1},{4,6},{5,7},{6,4},{7,5},{8,10},{9,11},{10,... | collective-permute-start | bytes 786440 | tf_op jit(solution)/shard_map/ppermute | solution.py:337
  575.4 15.9 %collective-permute-start.4 = (bf16[4,256,128]{2,1,0:T(8,128)(2,1)S(1)}, bf16[4,256,128]{2,1,0:T(8,128)(2,1)S(1)}, u32[]{:S(2)}, u32[]{:S(2)}) collective-permute-start(bf16[4,256,128]{2,1,0:T(8,128)(2,1)S(1)} %fusion.14), channel_id=1, source_target_pairs={{0,2},{1,3},{2,0},{3,1},{4,6},{5,7},{6,4},{7,5},{8,10},{9,11},{10,... | collective-permute-start | bytes 786440 | tf_op jit(solution)/shard_map/ppermute | solution.py:337
  575.6 15.9 %collective-permute-start.10 = (bf16[2,256,128]{2,1,0:T(8,128)(2,1)S(1)}, bf16[2,256,128]{2,1,0:T(8,128)(2,1)S(1)}, u32[]{:S(2)}, u32[]{:S(2)}) collective-permute-start(bf16[2,256,128]{2,1,0:T(8,128)(2,1)S(1)} %fusion.19), channel_id=1, source_target_pairs={{0,4},{1,5},{2,6},{3,7},{4,0},{5,1},{6,2},{7,3},{8,12},{9,13},{10,... | collective-permute-start | bytes 393224 | tf_op jit(solution)/shard_map/ppermute | solution.py:337
  591.5 22.9 %collective-permute-start.11 = (bf16[1,256,128]{2,1,0:T(8,128)(2,1)S(1)}, bf16[1,256,128]{2,1,0:T(8,128)(2,1)S(1)}, u32[]{:S(2)}, u32[]{:S(2)}) collective-permute-start(bf16[1,256,128]{2,1,0:T(8,128)(2,1)S(1)} %dynamic-slice_convert_fusion.13), channel_id=1, source_target_pairs={{0,8},{1,9},{2,10},{3,11},{4,12},{5,13},{6,14},{7,15},{8,0},{9,1},... | collective-permute-start | bytes 196616 | tf_op jit(solution)/shard_map/ppermute | solution.py:337
  615.2 86.8 %all-to-all-start.6 = ((bf16[16,512,256]{2,1,0:T(8,128)(2,1)}), bf16[16,512,256]{2,1,0:T(8,128)(2,1)}, u32[]{:S(2)}, u32[]{:S(2)}) async-start(bf16[16,512,256]{2,1,0:T(8,128)(2,1)} %bitcast.233), calls=%async_computation.6 | async-start | bytes 8388608 | tf_op jit(solution)/shard_map/all_to_all | solution.py:397
  702.0 115.5 %all-to-all-start.7 = ((bf16[16,512,256]{2,1,0:T(8,128)(2,1)}), bf16[16,512,256]{2,1,0:T(8,128)(2,1)}, u32[]{:S(2)}, u32[]{:S(2)}) async-start(bf16[16,512,256]{2,1,0:T(8,128)(2,1)} %bitcast.232), calls=%async_computation.7 | async-start | bytes 8388608 | tf_op jit(solution)/shard_map/all_to_all | solution.py:397
  721.8 22.3 %collective-permute-start.18 = (bf16[8,256,128]{2,1,0:T(8,128)(2,1)S(1)}, bf16[8,256,128]{2,1,0:T(8,128)(2,1)}, u32[]{:S(2)}, u32[]{:S(2)}) collective-permute-start(bf16[8,256,128]{2,1,0:T(8,128)(2,1)S(1)} %fusion.13), channel_id=1, source_target_pairs={{0,1},{1,0},{2,3},{3,2},{4,5},{5,4},{6,7},{7,6},{8,9},{9,8},{10,11... | collective-permute-start | bytes 1572872 | tf_op jit(solution)/shard_map/ppermute | solution.py:337
  724.5 51.3 %collective-permute-start.13 = (bf16[8,256,128]{2,1,0:T(8,128)(2,1)}, bf16[8,256,128]{2,1,0:T(8,128)(2,1)}, u32[]{:S(2)}, u32[]{:S(2)}) collective-permute-start(bf16[8,256,128]{2,1,0:T(8,128)(2,1)} %fusion.12), channel_id=1, source_target_pairs={{0,1},{1,0},{2,3},{3,2},{4,5},{5,4},{6,7},{7,6},{8,9},{9,8},{10,11... | collective-permute-start | bytes 1572872 | tf_op jit(solution)/shard_map/ppermute | solution.py:337
  745.6 31.5 %collective-permute-start.19 = (bf16[4,256,128]{2,1,0:T(8,128)(2,1)S(1)}, bf16[4,256,128]{2,1,0:T(8,128)(2,1)S(1)}, u32[]{:S(2)}, u32[]{:S(2)}) collective-permute-start(bf16[4,256,128]{2,1,0:T(8,128)(2,1)S(1)} %fusion.17), channel_id=1, source_target_pairs={{0,2},{1,3},{2,0},{3,1},{4,6},{5,7},{6,4},{7,5},{8,10},{9,11},{10,... | collective-permute-start | bytes 786440 | tf_op jit(solution)/shard_map/ppermute | solution.py:337
  777.0 15.4 %collective-permute-start.14 = (bf16[4,256,128]{2,1,0:T(8,128)(2,1)S(1)}, bf16[4,256,128]{2,1,0:T(8,128)(2,1)S(1)}, u32[]{:S(2)}, u32[]{:S(2)}) collective-permute-start(bf16[4,256,128]{2,1,0:T(8,128)(2,1)S(1)} %fusion.16), channel_id=1, source_target_pairs={{0,2},{1,3},{2,0},{3,1},{4,6},{5,7},{6,4},{7,5},{8,10},{9,11},{10,... | collective-permute-start | bytes 786440 | tf_op jit(solution)/shard_map/ppermute | solution.py:337
  777.2 16.1 %collective-permute-start.20 = (bf16[2,256,128]{2,1,0:T(8,128)(2,1)S(1)}, bf16[2,256,128]{2,1,0:T(8,128)(2,1)S(1)}, u32[]{:S(2)}, u32[]{:S(2)}) collective-permute-start(bf16[2,256,128]{2,1,0:T(8,128)(2,1)S(1)} %fusion.21), channel_id=1, source_target_pairs={{0,4},{1,5},{2,6},{3,7},{4,0},{5,1},{6,2},{7,3},{8,12},{9,13},{10,... | collective-permute-start | bytes 393224 | tf_op jit(solution)/shard_map/ppermute | solution.py:337
  793.4 21.6 %collective-permute-start.21 = (bf16[1,256,128]{2,1,0:T(8,128)(2,1)S(1)}, bf16[1,256,128]{2,1,0:T(8,128)(2,1)S(1)}, u32[]{:S(2)}, u32[]{:S(2)}) collective-permute-start(bf16[1,256,128]{2,1,0:T(8,128)(2,1)S(1)} %dynamic-slice_convert_fusion.11), channel_id=1, source_target_pairs={{0,8},{1,9},{2,10},{3,11},{4,12},{5,13},{6,14},{7,15},{8,0},{9,1},... | collective-permute-start | bytes 196616 | tf_op jit(solution)/shard_map/ppermute | solution.py:337
  801.8 14.5 %collective-permute-start.16 = (bf16[1,256,128]{2,1,0:T(8,128)(2,1)S(1)}, bf16[1,256,128]{2,1,0:T(8,128)(2,1)S(1)}, u32[]{:S(2)}, u32[]{:S(2)}) collective-permute-start(bf16[1,256,128]{2,1,0:T(8,128)(2,1)S(1)} %dynamic-slice_convert_fusion.12), channel_id=1, source_target_pairs={{0,8},{1,9},{2,10},{3,11},{4,12},{5,13},{6,14},{7,15},{8,0},{9,1},... | collective-permute-start | bytes 196616 | tf_op jit(solution)/shard_map/ppermute | solution.py:337
  (19 other events, 201.6 us)
Sparse Core Ops, SparseCore 0:
  127.5 64.3 all-gather.4
  225.1 14.7 all-gather.6
